TPU v7x, 32 devices: a whole 2x2x4 slice. The times are simulated.
32 devices in a mesh: dp: 8 (over z, y), tp: 4 (over x, core).
Axes of the slice: x: 2, y: 2, z: 4, core: 2. Of those that a mesh axis runs over, the one named last changes fastest.
Arguments:
- clean_latents: float32 [128, 256, 16], P(('dp', 'tp')), may hold values from -12 to 12
- noise_field: float32 [128, 256, 16], P(('dp', 'tp')), may hold values from -6 to 6
- timesteps: int32 [128], P(('dp', 'tp')), may hold values from 0 to 999
- labels: int32 [128], P(('dp', 'tp')), may hold values from 0 to 999
- drop_flags: int32 [128], P(('dp', 'tp')), may hold values 0 or 1
- entry_weight: float32 [656, 384], P(None, 'dp'), may hold values from -0.375 to 0.375
- class_table: float32 [1001, 384], P(None, 'dp'), may hold values from -0.2 to 0.2
- attn_weight: float32 [2, 384, 1536], P(None, None, ('dp', 'tp')), may hold values from -0.3125 to 0.3125
- ffn_in_weight: float32 [2, 384, 1536], P(None, None, ('dp', 'tp')), may hold values from -0.3125 to 0.3125
- ffn_out_weight: float32 [2, 1536, 384], P(None, ('dp', 'tp')), may hold values from -0.15625 to 0.15625
- ada_weight: float32 [2, 384, 2304], P(None, None, ('dp', 'tp')), may hold values from -0.21875 to 0.21875
- final_weight: float32 [384, 800], P('dp'), may hold values from -0.3125 to 0.3125
- entry_first: float32 [656, 384], P(None, 'dp'), may hold values from -2.2888184e-05 to 2.2888184e-05
- entry_second: float32 [656, 384], P(None, 'dp'), may hold values from 1.5995127e-11 to 6.398051e-11
- class_first: float32 [1001, 384], P(None, 'dp'), may hold values from -5.722046e-06 to 5.722046e-06
- class_second: float32 [1001, 384], P(None, 'dp'), may hold values from 9.996954e-13 to 3.9987818e-12
- attn_first: float32 [2, 384, 1536], P(None, None, ('dp', 'tp')), may hold values from -2.2888184e-05 to 2.2888184e-05
- attn_second: float32 [2, 384, 1536], P(None, None, ('dp', 'tp')), may hold values from 1.5995127e-11 to 6.398051e-11
- ffn_in_first: float32 [2, 384, 1536], P(None, None, ('dp', 'tp')), may hold values from -2.2888184e-05 to 2.2888184e-05
- ffn_in_second: float32 [2, 384, 1536], P(None, None, ('dp', 'tp')), may hold values from 1.5995127e-11 to 6.398051e-11
- ffn_out_first: float32 [2, 1536, 384], P(None, ('dp', 'tp')), may hold values from -2.2888184e-05 to 2.2888184e-05
- ffn_out_second: float32 [2, 1536, 384], P(None, ('dp', 'tp')), may hold values from 1.5995127e-11 to 6.398051e-11
- ada_first: float32 [2, 384, 2304], P(None, None, ('dp', 'tp')), may hold values from -2.2888184e-05 to 2.2888184e-05
- ada_second: float32 [2, 384, 2304], P(None, None, ('dp', 'tp')), may hold values from 1.5995127e-11 to 6.398051e-11
- final_first: float32 [384, 800], P('dp'), may hold values from -2.2888184e-05 to 2.2888184e-05
- final_second: float32 [384, 800], P('dp'), may hold values from 1.5995127e-11 to 6.398051e-11
Outputs:
- entry_new: float32 [656, 384], P(None, 'dp')
- entry_first_new: float32 [656, 384], P(None, 'dp')
- entry_second_new: float32 [656, 384], P(None, 'dp')
- class_new: float32 [1001, 384], P(None, 'dp')
- class_first_new: float32 [1001, 384], P(None, 'dp')
- class_second_new: float32 [1001, 384], P(None, 'dp')
- attn_new: float32 [2, 384, 1536], P(None, None, ('dp', 'tp'))
- attn_first_new: float32 [2, 384, 1536], P(None, None, ('dp', 'tp'))
- attn_second_new: float32 [2, 384, 1536], P(None, None, ('dp', 'tp'))
- ffn_in_new: float32 [2, 384, 1536], P(None, None, ('dp', 'tp'))
- ffn_in_first_new: float32 [2, 384, 1536], P(None, None, ('dp', 'tp'))
- ffn_in_second_new: float32 [2, 384, 1536], P(None, None, ('dp', 'tp'))
- ffn_out_new: float32 [2, 1536, 384], P(None, ('dp', 'tp'))
- ffn_out_first_new: float32 [2, 1536, 384], P(None, ('dp', 'tp'))
- ffn_out_second_new: float32 [2, 1536, 384], P(None, ('dp', 'tp'))
- ada_new: float32 [2, 384, 2304], P(None, None, ('dp', 'tp'))
- ada_first_new: float32 [2, 384, 2304], P(None, None, ('dp', 'tp'))
- ada_second_new: float32 [2, 384, 2304], P(None, None, ('dp', 'tp'))
- final_new: float32 [384, 800], P('dp')
- final_first_new: float32 [384, 800], P('dp')
- final_second_new: float32 [384, 800], P('dp')
- loss_sum: float32 [], replicated
- grad_norm: float32 [], replicated
- residual_rms: float32 [2], replicated
All inputs are finite; a program needn't handle non-finite values. No bound on the sum of `drop_flags` on one device may be relied on, other than what follows from the above.
Results may differ from a plain program's by a relative error of at most 0.0044.
The roundings to bfloat16 on the way count: a program that leaves them out, or rounds other values in their place, can miss the bound.
Values may be sent and summed in bfloat16 or wider, within the bound.
A program may use at most 192 MiB of HBM per device.

v0:
```python
import functools
import math

import jax
import jax.numpy as jnp
from jax import lax
from jax.experimental import pallas as pl
from jax.experimental.pallas import tpu as pltpu
from jax.sharding import PartitionSpec as P

D = 384
HEADS = 6
HEAD_DIM = 64
CLASSES = 1000
GRID = 16
PATCH_IN = 16
OUT = 32
FREQ = 256
NOISE_STEPS = 1000
STEP = 10
BF = jnp.bfloat16


highest = lax.Precision.HIGHEST


def dot_nn(a, b):
    return lax.dot_general(a, b, (((1,), (0,)), ((), ())), preferred_element_type=jnp.float32)


def dot_nt(a, b):
    return lax.dot_general(a, b, (((1,), (1,)), ((), ())), preferred_element_type=jnp.float32)


def dot_tn(a, b):
    return lax.dot_general(a, b, (((0,), (0,)), ((), ())), preferred_element_type=jnp.float32)


def norm_rows(rows):
    center = rows - jnp.mean(rows, axis=-1, keepdims=True)
    rstd = lax.rsqrt(jnp.mean(center * center, axis=-1, keepdims=True) + 1e-06)
    return center * rstd, rstd


def norm_back(d_out, hat, rstd, scale):
    d_shift = jnp.sum(d_out, axis=1, keepdims=True)
    d_scale = jnp.sum(d_out * hat, axis=1, keepdims=True)
    d_hat = d_out * (1.0 + scale)
    m_one = jnp.mean(d_hat, axis=-1, keepdims=True)
    m_two = jnp.mean(d_hat * hat, axis=-1, keepdims=True)
    return rstd * (d_hat - m_one - hat * m_two), d_shift, d_scale


def half_masks():
    lane = lax.broadcasted_iota(jnp.int32, (1, 2 * HEAD_DIM), 1)
    low = jnp.where(lane < HEAD_DIM, 1.0, 0.0)
    return low.astype(BF), (1.0 - low).astype(BF)


def stack_heads(pair, masks):
    return jnp.concatenate([pair * masks[0], pair * masks[1]], axis=0)


GELU_A = math.sqrt(2.0 / math.pi)
GELU_B = 0.044715


def forward_kernel(first, nb, tokens, *refs):
    if first:
        noisy_ref, patch_ref, pos_ref = refs[:3]
        refs = refs[3:]
    else:
        stream_ref = refs[0]
        refs = refs[1:]
    mod_ref, attn_ref, in_ref, out_ref = refs[:4]
    refs = refs[4:]
    if first:
        start_ref = refs[0]
        refs = refs[1:]
    (
        result_ref,
        qkv_ref,
        probs_ref,
        mixed_ref,
        branch_ref,
        middle_ref,
        mlp_ref,
        act_ref,
        slope_ref,
        square_ref,
    ) = refs
    rows = nb * tokens
    if first:
        parts = [
            lax.dot_general(
                noisy_ref[n], patch_ref[...], (((0,), (1,)), ((), ())), preferred_element_type=jnp.float32
            )
            + pos_ref[...]
            for n in range(nb)
        ]
        stream = parts[0] if nb == 1 else jnp.concatenate(parts, axis=0)
        start_ref[...] = stream
    else:
        stream = stream_ref[...]
    mod = mod_ref[...]
    stream = stream.reshape(nb, tokens, D)
    hat, _ = norm_rows(stream)
    attn_in = (hat * (1.0 + mod[:, 1:2]) + mod[:, 0:1]).astype(BF).reshape(rows, D)
    qkv_ref[...] = dot_nt(attn_in, attn_ref[: 3 * D, :]).astype(BF)
    masks = half_masks()
    for n in range(nb):
        here = slice(n * tokens, (n + 1) * tokens)
        for pair in range(HEADS // 2):
            col = pair * 2 * HEAD_DIM
            queries = qkv_ref[here, col : col + 2 * HEAD_DIM] * jnp.asarray(HEAD_DIM**-0.5, BF)
            keys = stack_heads(qkv_ref[here, D + col : D + col + 2 * HEAD_DIM], masks)
            values = stack_heads(qkv_ref[here, 2 * D + col : 2 * D + col + 2 * HEAD_DIM], masks)
            scores = dot_nt(queries, keys)
            halves = []
            for side in range(2):
                part = scores[:, side * tokens : (side + 1) * tokens]
                grown = jnp.exp(part - jnp.max(part, axis=-1, keepdims=True))
                halves.append((grown * (1.0 / jnp.sum(grown, axis=-1, keepdims=True))).astype(BF))
            probs = jnp.concatenate(halves, axis=1)
            probs_ref[here, pair * 2 * tokens : (pair + 1) * 2 * tokens] = probs
            mixed_ref[here, col : col + 2 * HEAD_DIM] = dot_nn(probs, values).astype(BF)
    branch = dot_nt(mixed_ref[...], attn_ref[3 * D :, :])
    branch_ref[...] = branch.astype(BF)
    middle = stream + mod[:, 2:3] * branch.reshape(nb, tokens, D)
    middle_ref[...] = middle.reshape(rows, D)
    hat, _ = norm_rows(middle)
    mlp_in = (hat * (1.0 + mod[:, 4:5]) + mod[:, 3:4]).astype(BF).reshape(rows, D)
    hidden = dot_nt(mlp_in, in_ref[...])
    squared = hidden * hidden
    bent = jnp.tanh(hidden * (GELU_A + (GELU_A * GELU_B) * squared))
    half = 0.5 * hidden
    act = (half + half * bent).astype(BF)
    act_ref[...] = act
    slope_ref[...] = (
        0.5
        + 0.5 * bent
        + half * (1.0 - bent * bent) * (GELU_A + (3.0 * GELU_A * GELU_B) * squared)
    ).astype(BF)
    mlp = dot_nn(act, out_ref[...])
    mlp_ref[...] = mlp.astype(BF)
    result = middle + mod[:, 5:6] * mlp.reshape(nb, tokens, D)
    result_ref[...] = result.reshape(rows, D)
    square_ref[0] = jnp.sum((result * result).reshape(rows // 8, 8, D), axis=0)


def backward_kernel(first, last, nb, tokens, steps, count_all, *refs):
    if last:
        final_ref, fmod_ref, head_ref, clean_ref, noise_ref = refs[:5]
        refs = refs[5:]
    else:
        d_stream_ref = refs[0]
        refs = refs[1:]
    if first:
        noisy_ref = refs[0]
        refs = refs[1:]
    (
        mod_ref,
        attn_ref,
        in_ref,
        out_ref,
        stream_ref,
        qkv_ref,
        probs_ref,
        mixed_ref,
        branch_ref,
        middle_ref,
        mlp_ref,
        act_ref,
        slope_ref,
    ) = refs[:13]
    refs = refs[13:]
    if last:
        loss_ref, dhead_ref, dfmod_ref = refs[:3]
        refs = refs[3:]
    if first:
        dpatch_ref = refs[0]
    else:
        d_prev_ref = refs[0]
    gattn_ref, gin_ref, gout_ref, dmod_ref, acc_attn, acc_in, acc_out, d_qkv_s = refs[1:]
    rows = nb * tokens
    step = pl.program_id(0)

    @pl.when(step == 0)
    def _():
        acc_attn[...] = jnp.zeros_like(acc_attn)
        acc_in[...] = jnp.zeros_like(acc_in)
        acc_out[...] = jnp.zeros_like(acc_out)
        if last:
            dhead_ref[...] = jnp.zeros_like(dhead_ref)
        if first:
            dpatch_ref[...] = jnp.zeros_like(dpatch_ref)

    mod = mod_ref[...]
    if last:
        fmod = fmod_ref[...]
        hat, rstd = norm_rows(final_ref[...].reshape(nb, tokens, D))
        final_in = (hat * (1.0 + fmod[:, 1:2]) + fmod[:, 0:1]).astype(BF)
        d_parts = []
        loss = jnp.zeros((8, tokens), jnp.float32)
        for n in range(nb):
            predicted = lax.dot_general(
                head_ref[...], final_in[n], (((0,), (1,)), ((), ())), preferred_element_type=jnp.float32
            )
            errors = predicted - jnp.concatenate([noise_ref[n], clean_ref[n]], axis=0)
            loss = loss + jnp.sum((errors * errors).reshape(OUT // 8, 8, tokens), axis=0)
            d_pred = (errors * (2.0 / count_all)).astype(BF)
            dhead_ref[...] += dot_nn(d_pred, final_in[n])
            d_parts.append(
                lax.dot_general(
                    d_pred, head_ref[...], (((0,), (1,)), ((), ())), preferred_element_type=jnp.float32
                )
            )
        loss_ref[0] = loss
        d_final = jnp.stack(d_parts, axis=0)
        d_stream, d_shift, d_scale = norm_back(d_final, hat, rstd, fmod[:, 1:2])
        dfmod_ref[:, 0:1] = d_shift
        dfmod_ref[:, 1:2] = d_scale
    else:
        d_stream = d_stream_ref[...].reshape(nb, tokens, D)
    dmod_ref[:, 5:6] = jnp.sum(d_stream * mlp_ref[...].astype(jnp.float32).reshape(nb, tokens, D), axis=1, keepdims=True)
    d_mlp = (d_stream * mod[:, 5:6]).astype(BF).reshape(rows, D)
    d_hidden = (dot_nt(d_mlp, out_ref[...]) * slope_ref[...].astype(jnp.float32)).astype(BF)
    acc_out[...] += dot_tn(act_ref[...], d_mlp)
    hat, rstd = norm_rows(middle_ref[...].reshape(nb, tokens, D))
    mlp_in = (hat * (1.0 + mod[:, 4:5]) + mod[:, 3:4]).astype(BF).reshape(rows, D)
    acc_in[...] += dot_tn(d_hidden, mlp_in)
    d_input = dot_nn(d_hidden, in_ref[...]).reshape(nb, tokens, D)
    d_middle, d_shift, d_scale = norm_back(d_input, hat, rstd, mod[:, 4:5])
    dmod_ref[:, 3:4] = d_shift
    dmod_ref[:, 4:5] = d_scale
    d_middle = d_middle + d_stream
    dmod_ref[:, 2:3] = jnp.sum(
        d_middle * branch_ref[...].astype(jnp.float32).reshape(nb, tokens, D), axis=1, keepdims=True
    )
    d_proj = (d_middle * mod[:, 2:3]).astype(BF).reshape(rows, D)
    acc_attn[3 * D :, :] += dot_tn(d_proj, mixed_ref[...])
    d_mix = dot_nn(d_proj, attn_ref[3 * D :, :]).astype(BF)
    masks = half_masks()
    lane = lax.broadcasted_iota(jnp.int32, (tokens, 2 * HEAD_DIM), 1)
    low_side = lane < HEAD_DIM
    root = HEAD_DIM**-0.5
    for n in range(nb):
        here = slice(n * tokens, (n + 1) * tokens)
        for pair in range(HEADS // 2):
            col = pair * 2 * HEAD_DIM
            queries = qkv_ref[here, col : col + 2 * HEAD_DIM]
            keys = stack_heads(qkv_ref[here, D + col : D + col + 2 * HEAD_DIM], masks)
            values = stack_heads(qkv_ref[here, 2 * D + col : 2 * D + col + 2 * HEAD_DIM], masks)
            d_out = d_mix[here, col : col + 2 * HEAD_DIM]
            probs_bf = probs_ref[here, pair * 2 * tokens : (pair + 1) * 2 * tokens]
            d_probs = dot_nt(d_out, values)
            halves = []
            for side in range(2):
                cut = slice(side * tokens, (side + 1) * tokens)
                probs = probs_bf[:, cut].astype(jnp.float32)
                part = d_probs[:, cut]
                halves.append((probs * (part - jnp.sum(probs * part, axis=-1, keepdims=True))).astype(BF))
            d_scores = jnp.concatenate(halves, axis=1)
            d_queries = dot_nn(d_scores, keys) * root
            d_keys = dot_tn(d_scores, queries)
            d_keys = jnp.where(low_side, d_keys[:tokens], d_keys[tokens:]) * root
            d_values = dot_tn(probs_bf, d_out)
            d_values = jnp.where(low_side, d_values[:tokens], d_values[tokens:])
            d_qkv_s[here, col : col + 2 * HEAD_DIM] = d_queries.astype(BF)
            d_qkv_s[here, D + col : D + col + 2 * HEAD_DIM] = d_keys.astype(BF)
            d_qkv_s[here, 2 * D + col : 2 * D + col + 2 * HEAD_DIM] = d_values.astype(BF)
    d_qkv = d_qkv_s[...]
    hat, rstd = norm_rows(stream_ref[...].reshape(nb, tokens, D))
    attn_in = (hat * (1.0 + mod[:, 1:2]) + mod[:, 0:1]).astype(BF).reshape(rows, D)
    acc_attn[: 3 * D, :] += dot_tn(d_qkv, attn_in)
    d_attn_in = dot_nn(d_qkv, attn_ref[: 3 * D, :]).reshape(nb, tokens, D)
    d_before, d_shift, d_scale = norm_back(d_attn_in, hat, rstd, mod[:, 1:2])
    dmod_ref[:, 0:1] = d_shift
    dmod_ref[:, 1:2] = d_scale
    d_prev = d_middle + d_before
    if first:
        for n in range(nb):
            dpatch_ref[...] += lax.dot_general(
                noisy_ref[n].astype(jnp.float32), d_prev[n], (((1,), (0,)), ((), ())), precision=highest
            )
    else:
        d_prev_ref[...] = d_prev.reshape(rows, D)

    @pl.when(step == steps - 1)
    def _():
        gattn_ref[...] = acc_attn[...].astype(BF)
        gin_ref[...] = acc_in[...].astype(BF)
        gout_ref[...] = acc_out[...].astype(BF)


def whole_spec(array):
    return pl.BlockSpec(array.shape, lambda i: (0,) * array.ndim)


def lead_spec(block, ndim):
    return pl.BlockSpec(block, lambda i: (i,) + (0,) * (ndim - 1))


LIMIT = 56 * 1024 * 1024


def forward_layer(first, entry_args, mod, weights, nb, tokens):
    lat_count = mod.shape[0]
    rows = nb * tokens
    steps = lat_count // nb
    total = lat_count * tokens
    kinds = [(D, jnp.float32)] if first else []
    kinds += [
        (D, jnp.float32),
        (3 * D, BF),
        (HEADS * tokens, BF),
        (D, BF),
        (D, BF),
        (D, jnp.float32),
        (D, BF),
        (4 * D, BF),
        (4 * D, BF),
    ]
    out_shape = [jax.ShapeDtypeStruct((total, cols), kind) for cols, kind in kinds]
    out_specs = [lead_spec((rows, cols), 2) for cols, _ in kinds]
    out_shape.append(jax.ShapeDtypeStruct((steps, 8, D), jnp.float32))
    out_specs.append(lead_spec((1, 8, D), 3))
    if first:
        noisy, patch, pos = entry_args
        in_specs = [lead_spec((nb, PATCH_IN, tokens), 3), whole_spec(patch), whole_spec(pos)]
    else:
        in_specs = [lead_spec((rows, D), 2)]
    in_specs += [lead_spec((nb, 8, D), 3)] + [whole_spec(w) for w in weights]
    return pl.pallas_call(
        functools.partial(forward_kernel, first, nb, tokens),
        grid=(steps,),
        out_shape=out_shape,
        in_specs=in_specs,
        out_specs=out_specs,
        compiler_params=pltpu.CompilerParams(vmem_limit_bytes=LIMIT),
        name="block_forward",
    )(*entry_args, mod, *weights)


def backward_layer(first, last, entry_args, mod, weights, saved, nb, tokens, count_all):
    lat_count = mod.shape[0]
    rows = nb * tokens
    steps = lat_count // nb
    total = lat_count * tokens
    in_specs = []
    args = list(entry_args)
    if last:
        in_specs += [
            lead_spec((rows, D), 2),
            lead_spec((nb, 8, D), 3),
            whole_spec(args[2]),
            lead_spec((nb, PATCH_IN, tokens), 3),
            lead_spec((nb, PATCH_IN, tokens), 3),
        ]
    else:
        in_specs += [lead_spec((rows, D), 2)]
    if first:
        in_specs += [lead_spec((nb, PATCH_IN, tokens), 3)]
    in_specs += [lead_spec((nb, 8, D), 3)] + [whole_spec(w) for w in weights]
    in_specs += [lead_spec((rows, s.shape[1]), 2) for s in saved]
    out_shape = []
    out_specs = []

    def add(shape, kind, spec):
        out_shape.append(jax.ShapeDtypeStruct(shape, kind))
        out_specs.append(spec)

    def whole(shape):
        return pl.BlockSpec(shape, lambda i: (0,) * len(shape))

    if last:
        add((steps, 8, tokens), jnp.float32, lead_spec((1, 8, tokens), 3))
        add((OUT, D), jnp.float32, whole((OUT, D)))
        add((lat_count, 8, D), jnp.float32, lead_spec((nb, 8, D), 3))
    if first:
        add((PATCH_IN, D), jnp.float32, whole((PATCH_IN, D)))
    else:
        add((total, D), jnp.float32, lead_spec((rows, D), 2))
    for _ in range(3):
        add((4 * D, D), BF, whole((4 * D, D)))
    add((lat_count, 8, D), jnp.float32, lead_spec((nb, 8, D), 3))
    return pl.pallas_call(
        functools.partial(backward_kernel, first, last, nb, tokens, steps, count_all),
        grid=(steps,),
        out_shape=out_shape,
        in_specs=in_specs,
        out_specs=out_specs,
        scratch_shapes=[pltpu.VMEM((4 * D, D), jnp.float32)] * 3 + [pltpu.VMEM((rows, 3 * D), BF)],
        compiler_params=pltpu.CompilerParams(vmem_limit_bytes=LIMIT),
        name="block_backward",
    )(*args, mod, *weights, *saved)


MESH = pl.DeviceIdType.MESH


class Places:
    def __init__(self, n_dp, n_tp):
        self.digits = []
        for axis, count, top in (("dp", n_dp, 4), ("tp", n_tp, 2)):
            sizes = []
            rest = count
            while rest > 1:
                size = next((s for s in (top, 2, 3, 5, 7) if rest % s == 0), rest)
                sizes.append(size)
                rest //= size
            stride = count
            for size in sizes:
                stride //= size
                self.digits.append((axis, stride, size))
        self.dims = tuple(size for _, _, size in self.digits)
        self.count = n_dp * n_tp

    def order(self, odd):
        names = list(range(len(self.digits)))
        if odd and len(names) >= 4:
            names[-3], names[-2] = names[-2], names[-3]
        return names

    def mine(self):
        return [lax.rem(lax.axis_index(axis) // stride, size) for axis, stride, size in self.digits]

    def other(self, mine, digit, shift):
        axis, stride, size = self.digits[digit]
        value = lax.rem(mine[digit] + shift, size)
        return {axis: lax.axis_index(axis) + (value - mine[digit]) * stride}, value

    def barrier(self, mine):
        barrier = pltpu.get_barrier_semaphore()
        count = 0
        for digit, size in enumerate(self.dims):
            for shift in range(1, size):
                target, _ = self.other(mine, digit, shift)
                pl.semaphore_signal(barrier, inc=1, device_id=target, device_id_type=MESH)
                count += 1
        pl.semaphore_wait(barrier, count)


SMALL = 8
SPLIT = 3


def small_blocks(entry_t, table_t, final):
    early = PATCH_IN + FREQ
    return [
        (0, 0, entry_t, 0, early),
        (1, 0, entry_t, early, early + D),
        (2, 0, table_t, 0, D),
        (3, 0, table_t, D, 2 * D),
        (4, 0, table_t, 2 * D, CLASSES + 1),
        (4, 256, final, 2 * D, 2 * D + OUT),
        (5, 0, final, 0, D),
        (6, 0, final, D, 2 * D),
    ]


def gather_kernel(places, slots, layers, *refs):
    entry_ref, table_ref, final_ref, ada_ref, attn_ref, in_ref, out_ref = refs[:7]
    chunks = slots + SPLIT + 3 * layers
    outs = refs[7 : 7 + chunks]
    small, packed, send_sems, recv_sems, own_sems = refs[7 + chunks :]
    mine = places.mine()
    depth = len(places.dims)
    small[...] = jnp.zeros_like(small)
    for k, at, source, low, high in small_blocks(entry_ref, table_ref, final_ref):
        small[k, : source.shape[0], at : at + high - low] = source[:, low:high].astype(BF)
    part = -(-ada_ref.shape[0] // SPLIT)
    for p in range(SPLIT):
        packed[p, :part, :] = ada_ref[p * part : (p + 1) * part, :].astype(BF)
    for l in range(layers):
        for k, source in enumerate((attn_ref, in_ref, out_ref)):
            packed[SPLIT + 3 * l + k, : source.shape[1], :] = source[l].astype(BF)
    first = lax.axis_index("tp") * slots
    ins = [small.at[first + s] for s in range(slots)]
    ins += [packed.at[m] for m in range(SPLIT + 3 * layers)]
    places.barrier(mine)
    started = {}
    own = []
    for m in range(chunks):
        copy = pltpu.make_async_copy(ins[m], outs[m].at[tuple(mine)], own_sems.at[m])
        copy.start()
        own.append(copy)

    def start(m, stage):
        order = places.order(m % 2 == 1)
        digit = order[stage]
        done = order[:stage]
        where = tuple(slice(None) if d in done else mine[d] for d in range(depth))
        source = ins[m] if stage == 0 else outs[m].at[where]
        copies = []
        for shift in range(1, places.dims[digit]):
            target, _ = places.other(mine, digit, shift)
            copy = pltpu.make_async_remote_copy(
                src_ref=source,
                dst_ref=outs[m].at[where],
                send_sem=send_sems.at[m, stage, shift - 1],
                recv_sem=recv_sems.at[m, stage, shift - 1],
                device_id=target,
                device_id_type=MESH,
            )
            copy.start()
            copies.append(copy)
        started[m, stage] = copies

    pairs = (chunks + 1) // 2
    for tick in range(pairs + depth):
        for stage in range(depth, -1, -1):
            if not 0 <= tick - stage < pairs:
                continue
            for m in range(2 * (tick - stage), min(2 * (tick - stage) + 2, chunks)):
                if stage == 1:
                    own[m].wait()
                if stage > 0:
                    for copy in started[m, stage - 1]:
                        copy.wait_recv()
                if stage < depth:
                    start(m, stage)
    for copies in started.values():
        for copy in copies:
            copy.wait_send()


def pad16(rows):
    return rows + -rows % 16


def gather_all(places, slots, entry_t, table_t, final, ada_t, attn_t, in_t, out_w):
    layers = attn_t.shape[0]
    depth, widest = len(places.dims), max(places.dims)
    small_rows, ada_rows = pad16(final.shape[0]), pad16(-(-ada_t.shape[0] // SPLIT))
    wide_rows = pad16(attn_t.shape[1])
    sizes = [small_rows] * slots + [ada_rows] * SPLIT + [wide_rows] * (3 * layers)
    chunks = len(sizes)
    vmem = pl.BlockSpec(memory_space=pltpu.VMEM)
    packed_rows = max(ada_rows, wide_rows)
    assert packed_rows == min(ada_rows, wide_rows)
    outs = pl.pallas_call(
        functools.partial(gather_kernel, places, slots, layers),
        out_shape=[jax.ShapeDtypeStruct((*places.dims, rows, D), BF) for rows in sizes],
        in_specs=[vmem] * 7,
        out_specs=[pl.BlockSpec(memory_space=pl.ANY)] * chunks,
        scratch_shapes=[
            pltpu.VMEM((slots * lax.axis_size("tp"), small_rows, D), BF),
            pltpu.VMEM((SPLIT + 3 * layers, packed_rows, D), BF),
            pltpu.SemaphoreType.DMA((chunks, depth, widest - 1)),
            pltpu.SemaphoreType.DMA((chunks, depth, widest - 1)),
            pltpu.SemaphoreType.DMA((chunks,)),
        ],
        compiler_params=pltpu.CompilerParams(collective_id=1, has_side_effects=True, vmem_limit_bytes=LIMIT),
        name="gather_weights",
    )(entry_t, table_t, final, ada_t, attn_t, in_t, out_w)
    return [o.reshape((places.count,) + o.shape[-2:]) for o in outs]


def reduce_kernel(places, chunks, slots, layers, *refs):
    ins = refs[:chunks]
    loss_ref = refs[chunks]
    square_refs = refs[chunks + 1 : chunks + 1 + layers]
    refs = refs[chunks + 1 + layers :]
    outs, both_ref, stats_ref = refs[:chunks], refs[chunks], refs[chunks + 1]
    refs = refs[chunks + 2 :]
    stats_land, stats_send, stats_recv, both_send, both_recv = refs[-5:]
    refs = refs[:-5]
    depth = len(places.dims)
    accs = refs[:chunks]
    lands = refs[chunks : chunks * (1 + depth)]
    send_sems, recv_sems, own_sems = refs[chunks * (1 + depth) :]
    mine = places.mine()
    places.barrier(mine)
    started = {}
    own = []

    def route(m):
        return places.order(m % 2 == 1)[::-1]

    for m in range(chunks):
        where = tuple(slice(None) if d < depth - 1 else mine[d] for d in range(depth))
        copy = pltpu.make_async_copy(ins[m].at[where], accs[m], own_sems.at[m])
        copy.start()
        own.append(copy)

    def start(m, stage):
        order = route(m)
        digit = order[stage]
        gone = order[:stage]
        copies = []
        for shift in range(1, places.dims[digit]):
            target, value = places.other(mine, digit, shift)
            where = tuple(
                mine[d] if d in gone else (value if d == digit else slice(None)) for d in range(depth)
            )
            source = ins[m].at[where] if stage == 0 else accs[m].at[where[: depth - 1]]
            copy = pltpu.make_async_remote_copy(
                src_ref=source,
                dst_ref=lands[m * depth + stage].at[shift - 1],
                send_sem=send_sems.at[m, stage, shift - 1],
                recv_sem=recv_sems.at[m, stage, shift - 1],
                device_id=target,
                device_id_type=MESH,
            )
            copy.start()
            copies.append(copy)
        started[m, stage] = copies

    def add(m, stage):
        order = route(m)
        gone = order[: stage + 1]
        left = [d for d in range(depth) if d not in gone]
        land = lands[m * depth + stage]
        count = math.prod(places.dims[d] for d in left)

        def one(flat, carry):
            values = {}
            rest = flat
            for d in reversed(left):
                values[d] = lax.rem(rest, places.dims[d])
                rest = rest // places.dims[d]
            here = tuple(values.get(d, mine[d]) for d in range(depth - 1))
            total = accs[m][here].astype(jnp.float32)
            for shift in range(1, places.dims[order[stage]]):
                total = total + land[(shift - 1, *(values[d] for d in left))].astype(jnp.float32)
            if left:
                accs[m][here] = total.astype(BF)
            else:
                outs[m][...] = total
            return carry

        lax.fori_loop(0, count, one, 0)

    pairs = (chunks + 1) // 2
    for tick in range(pairs + depth):
        for stage in range(depth, -1, -1):
            if not 0 <= tick - stage < pairs:
                continue
            for m in range(2 * (tick - stage), min(2 * (tick - stage) + 2, chunks)):
                if stage == 1:
                    own[m].wait()
                if stage > 0:
                    for copy in started[m, stage - 1]:
                        copy.wait_recv()
                    add(m, stage - 1)
                if stage < depth:
                    start(m, stage)
    for copies in started.values():
        for copy in copies:
            copy.wait_send()

    def lane_sums(rows):
        total = jnp.sum(rows, axis=0, keepdims=True)
        return sum(total[:, at : at + 128] for at in range(0, total.shape[1], 128))

    grad = sum(lane_sums(out[...] * out[...]) for out in outs)
    loss = lane_sums(jnp.sum(loss_ref[...], axis=0))
    squares = [lane_sums(jnp.sum(ref[...], axis=0)) for ref in square_refs]
    stats_ref[...] = jnp.concatenate([grad, loss, *squares, jnp.zeros((6 - layers, 128), jnp.float32)], axis=0)
    for s in range(slots):
        both_ref[(lax.axis_index("tp"), s)] = outs[s][...]
    inner = [d for d in range(depth) if places.digits[d][0] == "tp"]
    for stage, digit in enumerate(reversed(range(depth))):
        size = places.dims[digit]
        axis, stride, _ = places.digits[digit]
        stats_land[stage, mine[digit]] = stats_ref[...]
        copies = []
        for shift in range(1, size):
            target, _ = places.other(mine, digit, shift)
            copies.append(
                pltpu.make_async_remote_copy(
                    src_ref=stats_ref,
                    dst_ref=stats_land.at[stage, mine[digit]],
                    send_sem=stats_send.at[stage, shift - 1],
                    recv_sem=stats_recv.at[stage, shift - 1],
                    device_id=target,
                    device_id_type=MESH,
                )
            )
            if digit in inner:
                held = stride
                start = lax.axis_index("tp") // stride * stride
                where = both_ref.at[pl.ds(start, held)]
                copies.append(
                    pltpu.make_async_remote_copy(
                        src_ref=where,
                        dst_ref=where,
                        send_sem=both_send.at[stage, shift - 1],
                        recv_sem=both_recv.at[stage, shift - 1],
                        device_id=target,
                        device_id_type=MESH,
                    )
                )
        for copy in copies:
            copy.start()
        for copy in copies:
            copy.wait()
        total = stats_land[stage, 0]
        for value in range(1, size):
            total = total + stats_land[stage, value]
        stats_ref[...] = total


def reduce_all(places, slots, parts, loss, squares):
    layers = len(squares)
    vmem = pl.BlockSpec(memory_space=pltpu.VMEM)
    chunks = len(parts)
    dims = places.dims
    depth, widest = len(dims), max(dims)
    blocks = [p.shape[1:] for p in parts]
    lands = []
    for m in range(chunks):
        order = places.order(m % 2 == 1)[::-1]
        for stage in range(depth):
            gone = order[: stage + 1]
            left = tuple(dims[d] for d in range(depth) if d not in gone)
            lands.append(pltpu.VMEM((dims[order[stage]] - 1, *left, *blocks[m]), BF))
    return pl.pallas_call(
        functools.partial(reduce_kernel, places, chunks, slots, layers),
        out_shape=[jax.ShapeDtypeStruct(block, jnp.float32) for block in blocks]
        + [
            jax.ShapeDtypeStruct((lax.axis_size("tp"), slots, *blocks[0]), jnp.float32),
            jax.ShapeDtypeStruct((8, 128), jnp.float32),
        ],
        in_specs=[pl.BlockSpec(memory_space=pl.ANY)] * chunks + [vmem] * (1 + layers),
        out_specs=[vmem] * (chunks + 2),
        scratch_shapes=[pltpu.VMEM(dims[:-1] + block, BF) for block in blocks]
        + lands
        + [
            pltpu.SemaphoreType.DMA((chunks, depth, widest - 1)),
            pltpu.SemaphoreType.DMA((chunks, depth, widest - 1)),
            pltpu.SemaphoreType.DMA((chunks,)),
            pltpu.VMEM((depth, widest, 8, 128), jnp.float32),
            pltpu.SemaphoreType.DMA((depth, widest - 1)),
            pltpu.SemaphoreType.DMA((depth, widest - 1)),
            pltpu.SemaphoreType.DMA((depth, widest - 1)),
            pltpu.SemaphoreType.DMA((depth, widest - 1)),
        ],
        compiler_params=pltpu.CompilerParams(collective_id=2, has_side_effects=True, vmem_limit_bytes=LIMIT),
        name="reduce_gradients",
    )(*[p.reshape(dims + p.shape[1:]) for p in parts], loss, *squares)


def silu(values):
    return values * (1.0 / (1.0 + jnp.exp(-values)))


def silu_slope(values):
    gate = 1.0 / (1.0 + jnp.exp(-values))
    return gate * (1.0 + values * (1.0 - gate))


def split_low(values):
    high = values.astype(BF)
    return jnp.concatenate([high, (values - high.astype(jnp.float32)).astype(BF)], axis=0)


def block_of(refs, k):
    slots = len(refs)
    part = refs[k % slots][:, k // slots]
    return part.reshape(-1, D)


def condition_kernel(slots, lat_count, *refs):
    feat_ref, hot_ref = refs[:2]
    slot_refs = refs[2 : 2 + slots]
    ada_refs = refs[2 + slots : 2 + slots + SPLIT]
    mod_ref, fmod_ref, pre_ref, cond_ref, patch_ref, head_ref = refs[2 + slots + SPLIT :]
    entry = block_of(slot_refs, 0)
    patch_ref[...] = entry[:, :PATCH_IN]
    pre = dot_nt(feat_ref[...], entry)
    pre_ref[...] = pre
    cond = dot_nt(silu(pre).astype(BF), block_of(slot_refs, 1))
    for k in range(3):
        cond = cond + dot_nt(hot_ref[:, k * D : (k + 1) * D], block_of(slot_refs, 2 + k))
    cond_ref[...] = cond
    head_ref[...] = block_of(slot_refs, 4)[:, 256 : 256 + OUT]
    act = silu(cond).astype(BF)
    for p in range(SPLIT):
        wide = ada_refs[p].shape[0]
        mod_ref[:, p * wide : (p + 1) * wide] = dot_nt(act, ada_refs[p][...])
    for k in range(2):
        part = dot_nn(act, block_of(slot_refs, 5 + k))
        for b in range(lat_count):
            fmod_ref[b, k : k + 1, :] = part[b : b + 1, :]


def condition(feat, hot, slot_full, ada_full, lat_count):
    vmem = pl.BlockSpec(memory_space=pltpu.VMEM)
    wide = ada_full[0].shape[0]
    shapes = [
        ((8, SPLIT * wide), jnp.float32),
        ((lat_count, 8, D), jnp.float32),
        ((8, D), jnp.float32),
        ((8, D), jnp.float32),
        ((D, PATCH_IN), BF),
        ((D, OUT), BF),
    ]
    return pl.pallas_call(
        functools.partial(condition_kernel, len(slot_full), lat_count),
        out_shape=[jax.ShapeDtypeStruct(*s) for s in shapes],
        in_specs=[vmem] * (2 + len(slot_full) + SPLIT),
        out_specs=[vmem] * len(shapes),
        compiler_params=pltpu.CompilerParams(vmem_limit_bytes=LIMIT),
        name="condition",
    )(feat, hot, *slot_full, *ada_full)


def condition_back_kernel(slots, lat_count, *refs):
    feat_ref, hot_ref = refs[:2]
    slot_refs = refs[2 : 2 + slots]
    ada_refs = refs[2 + slots : 2 + slots + SPLIT]
    pre_ref, cond_ref, d_mod_ref, d_fmod_ref, d_patch_ref, d_head_ref = refs[2 + slots + SPLIT :][:6]
    outs = refs[2 + slots + SPLIT + 6 :]
    g_slots, g_ada = outs[:slots], outs[slots : slots + SPLIT]
    fmod_s = outs[slots + SPLIT]
    pre, cond = pre_ref[...], cond_ref[...]
    act = silu(cond).astype(BF)
    act_two = jnp.concatenate([act, act], axis=0)
    d_cond = jnp.zeros((16, D), jnp.float32)
    for p in range(SPLIT):
        wide = ada_refs[p].shape[0]
        d_mod = split_low(d_mod_ref[:, p * wide : (p + 1) * wide])
        d_cond = d_cond + dot_nn(d_mod, ada_refs[p][...])
        g_ada[p][...] = dot_tn(d_mod, act_two).astype(BF)

    def give(k, grad):
        ref = g_slots[k % slots]
        ref[:, k // slots] = grad.astype(BF).reshape(ref.shape[0], ref.shape[2], D)

    fmod_s[...] = jnp.zeros_like(fmod_s)
    for k in range(2):
        for b in range(lat_count):
            fmod_s[k, b : b + 1, :] = d_fmod_ref[b, k : k + 1, :]
        d_fmod = split_low(fmod_s[k])
        d_cond = d_cond + dot_nt(d_fmod, block_of(slot_refs, 5 + k))
        give(5 + k, dot_tn(act_two, d_fmod))
    d_pre = split_low((d_cond[:8] + d_cond[8:]) * silu_slope(cond))
    time_act = silu(pre).astype(BF)
    give(1, dot_tn(d_pre, jnp.concatenate([time_act, time_act], axis=0)))
    d_time = dot_nn(d_pre, block_of(slot_refs, 1))
    for k in range(3):
        hot = hot_ref[:, k * D : (k + 1) * D]
        grad = dot_tn(d_pre, jnp.concatenate([hot, hot], axis=0))
        if k == 2:
            here = jnp.pad(d_head_ref[...], ((0, 128 - OUT), (0, 0))).T
            grad = jnp.concatenate([grad[:, :256], grad[:, 256:] + here], axis=1)
        give(2 + k, grad)
    d_time = split_low((d_time[:8] + d_time[8:]) * silu_slope(pre))
    grad = dot_tn(d_time, jnp.concatenate([feat_ref[...], feat_ref[...]], axis=0))
    here = jnp.pad(d_patch_ref[...], ((0, 128 - PATCH_IN), (0, 0))).T
    give(0, jnp.concatenate([grad[:, :128] + here, grad[:, 128:]], axis=1))
    for k in range(7, SMALL):
        give(k, jnp.zeros((D, D), jnp.float32))


def condition_back(feat, hot, slot_full, ada_full, pre, cond, d_mod, d_fmod, d_patch, d_head):
    vmem = pl.BlockSpec(memory_space=pltpu.VMEM)
    lat_count = d_fmod.shape[0]
    args = (feat, hot, *slot_full, *ada_full, pre, cond, d_mod, d_fmod, d_patch, d_head)
    kept = (*slot_full, *ada_full)
    return pl.pallas_call(
        functools.partial(condition_back_kernel, len(slot_full), lat_count),
        out_shape=[jax.ShapeDtypeStruct(w.shape, BF) for w in kept],
        in_specs=[vmem] * len(args),
        out_specs=[vmem] * len(kept),
        scratch_shapes=[pltpu.VMEM((2, 8, D), jnp.float32)],
        compiler_params=pltpu.CompilerParams(vmem_limit_bytes=LIMIT),
        name="condition_back",
    )(*args)


def adam_kernel(slots, layers, count_rms, *refs):
    stats_ref, both_ref = refs[:2]
    grads = refs[2 : 2 + SPLIT + 3 * layers]
    states = refs[2 + SPLIT + 3 * layers :][:21]
    outs = refs[2 + SPLIT + 3 * layers + 21 :]
    news, (loss_ref, norm_ref, rms_ref) = outs[:21], outs[21:]
    totals = jnp.sum(stats_ref[...], axis=1, keepdims=True)
    norm = jnp.sqrt(totals[0:1])
    factor = jnp.minimum(1.0, 0.01 / (norm + 1e-06))
    loss_ref[...] = totals[1:2]
    norm_ref[...] = norm
    rms_ref[...] = jnp.sqrt(totals[2 : 2 + layers] / count_rms)
    correct = 1.0 - 0.5**STEP

    def update(name, where, grad):
        weight, first, second = (ref[where] for ref in states[3 * name : 3 * name + 3])
        clipped = grad * factor
        first_new = 0.5 * first + 0.5 * clipped
        second_new = 0.5 * second + 0.5 * clipped * clipped
        root = jnp.sqrt(second_new * (1.0 / correct)) + 1e-08
        new = weight - 0.02 * (first_new * (1.0 / correct) / root + 0.01 * weight)
        news[3 * name][where] = new
        news[3 * name + 1][where] = first_new
        news[3 * name + 2][where] = second_new

    def small(k):
        return both_ref[k // slots, k % slots]

    rows = states[0].shape[0]
    early = PATCH_IN + FREQ
    every = slice(0, rows)
    update(0, (every, slice(0, early)), small(0)[:rows, :early])
    update(0, (every, slice(early, early + D)), small(1)[:rows])
    update(1, (every, slice(0, D)), small(2)[:rows])
    update(1, (every, slice(D, 2 * D)), small(3)[:rows])
    update(1, (every, slice(2 * D, CLASSES + 1)), small(4)[:rows, : CLASSES + 1 - 2 * D])
    update(6, (every, slice(0, D)), small(5)[:rows])
    update(6, (every, slice(D, 2 * D)), small(6)[:rows])
    update(6, (every, slice(2 * D, 2 * D + OUT)), small(4)[:rows, 256 : 256 + OUT])
    part = -(-states[15].shape[0] // SPLIT)
    for p in range(SPLIT):
        update(5, (slice(p * part, (p + 1) * part), slice(0, D)), grads[p][:part])
    for l in range(layers):
        for k in range(3):
            update(2 + k, (l, slice(0, states[6].shape[1]), slice(0, D)), grads[SPLIT + 3 * l + k][: states[6].shape[1]])


def adam_all(slots, layers, count_rms, stats, both, grads, states):
    vmem = pl.BlockSpec(memory_space=pltpu.VMEM)
    args = (stats, both, *grads, *states)
    return pl.pallas_call(
        functools.partial(adam_kernel, slots, layers, count_rms),
        out_shape=[jax.ShapeDtypeStruct(s.shape, jnp.float32) for s in states]
        + [jax.ShapeDtypeStruct((n, 1), jnp.float32) for n in (1, 1, layers)],
        in_specs=[vmem] * len(args),
        out_specs=[vmem] * 24,
        compiler_params=pltpu.CompilerParams(vmem_limit_bytes=LIMIT),
        name="adam",
    )(*args)


def position_table(grid_side, columns):
    quarter = columns // 4
    omegas = jnp.exp(-math.log(10000.0) * jnp.arange(quarter, dtype=jnp.float32) / quarter)
    positions = jnp.arange(grid_side * grid_side, dtype=jnp.int32)
    row_pos = (positions // grid_side).astype(jnp.float32)[:, None] * omegas
    col_pos = (positions % grid_side).astype(jnp.float32)[:, None] * omegas
    return jnp.concatenate(
        [jnp.sin(row_pos), jnp.cos(row_pos), jnp.sin(col_pos), jnp.cos(col_pos)], axis=-1
    )


def time_table(step_ids, columns):
    half_cols = columns // 2
    frequency = jnp.exp(-math.log(10000.0) * jnp.arange(half_cols, dtype=jnp.float32) / half_cols)
    angles = step_ids.astype(jnp.float32)[:, None] * frequency
    return jnp.concatenate([jnp.cos(angles), jnp.sin(angles)], axis=-1)


def noise_scales(step_ids):
    phases = (step_ids.astype(jnp.float32) / NOISE_STEPS + 0.008) / 1.008 * (math.pi / 2)
    return (jnp.cos(phases), jnp.sin(phases))


def swap(array):
    return jnp.swapaxes(array, -1, -2)


def pad_rows(part):
    extra = -part.shape[-2] % 16
    if extra == 0:
        return part
    return jnp.pad(part, [(0, 0)] * (part.ndim - 2) + [(0, extra), (0, 0)])


def body(
    clean_latents,
    noise_field,
    timesteps,
    labels,
    drop_flags,
    entry_weight,
    class_table,
    attn_weight,
    ffn_in_weight,
    ffn_out_weight,
    ada_weight,
    final_weight,
    entry_first,
    entry_second,
    class_first,
    class_second,
    attn_first,
    attn_second,
    ffn_in_first,
    ffn_in_second,
    ffn_out_first,
    ffn_out_second,
    ada_first,
    ada_second,
    final_first,
    final_second,
):
    lat_count = clean_latents.shape[0]
    tokens = clean_latents.shape[1]
    layers = attn_weight.shape[0]
    both = ("dp", "tp")
    devices = lax.axis_size("dp") * lax.axis_size("tp")
    count_all = float(lat_count * devices * tokens * OUT)
    count_rms = float(lat_count * devices * tokens * D)
    nb = 1
    clean_t, noise_t = swap(clean_latents), swap(noise_field)
    cos_part, sin_part = noise_scales(timesteps)
    noisy = (cos_part[:, None, None] * clean_t + sin_part[:, None, None] * noise_t).astype(BF)
    n_dp, n_tp = lax.axis_size("dp"), lax.axis_size("tp")
    places = Places(n_dp, n_tp)
    slots = -(-SMALL // n_tp)
    dp_rows = final_weight.shape[0]
    wide_rows = attn_weight.shape[2]
    ada_rows = ada_weight.shape[2]
    part_rows = -(-layers * ada_rows // SPLIT)

    def flat_ada(array):
        return swap(array).reshape(layers * ada_rows, D)

    gathered = gather_all(
        places,
        slots,
        swap(entry_weight),
        swap(class_table),
        final_weight,
        flat_ada(ada_weight),
        swap(attn_weight),
        swap(ffn_in_weight),
        ffn_out_weight,
    )

    def whole_rows(block, rows):
        return block[:, :rows].reshape(-1, D)

    def to_slot(block):
        if dp_rows % 16 == 0:
            return block.reshape(n_dp, n_tp, dp_rows, D)
        block = block.reshape(n_dp, n_tp, -1, D)[:, :, :dp_rows]
        return block.swapaxes(0, 1).reshape(1, n_tp, n_dp * dp_rows, D)

    def from_slot(block):
        if dp_rows % 16 == 0:
            return block.reshape(places.count, dp_rows, D)
        block = block.reshape(n_tp, n_dp, dp_rows, D).swapaxes(0, 1)
        return pad_rows(block.reshape(places.count, dp_rows, D))

    slot_full = [to_slot(g) for g in gathered[:slots]]
    ada_full = [whole_rows(g, part_rows) for g in gathered[slots : slots + SPLIT]]
    block_full = [whole_rows(g, wide_rows) for g in gathered[slots + SPLIT :]]
    weights = [tuple(block_full[3 * l : 3 * l + 3]) for l in range(layers)]

    time_feat = time_table(timesteps, FREQ).astype(BF)
    feat = jnp.pad(time_feat, ((0, 8 - lat_count), (PATCH_IN, D - PATCH_IN - FREQ)))
    classes_used = jnp.where(drop_flags == 1, CLASSES, labels)
    classes_used = jnp.pad(classes_used, (0, 8 - lat_count), constant_values=3 * D)
    class_hot = (classes_used[:, None] == jnp.arange(3 * D, dtype=jnp.int32)[None, :]).astype(BF)
    raw, fmod, pre, cond, patch_t, head = condition(feat, class_hot, slot_full, ada_full, lat_count)
    mods = raw[:lat_count].reshape(lat_count, SPLIT, places.count, part_rows).swapaxes(1, 2)
    mods = mods.reshape(lat_count, places.count, layers, ada_rows).transpose(2, 0, 1, 3)
    mods = mods.reshape(layers, lat_count, 6, D)
    mods = jnp.pad(mods, ((0, 0), (0, 0), (0, 2), (0, 0)))
    mods = [mods[l] for l in range(layers)]
    pos = position_table(GRID, D)
    saved = []
    squares = []
    stream = None
    for l in range(layers):
        if l == 0:
            outs = forward_layer(True, (noisy, patch_t, pos), mods[l], weights[l], nb, tokens)
            stream, outs = outs[0], outs[1:]
        else:
            outs = forward_layer(False, (stream,), mods[l], weights[l], nb, tokens)
        saved.append((stream, *outs[1:9]))
        stream = outs[0]
        squares.append(outs[9])
    layer_grads = [None] * layers
    d_mods = [None] * layers
    d_stream = None
    for l in reversed(range(layers)):
        last, first = l == layers - 1, l == 0
        entry_args = (stream, fmod, head, clean_t, noise_t) if last else (d_stream,)
        if first:
            entry_args = (*entry_args, noisy)
        outs = list(backward_layer(first, last, entry_args, mods[l], weights[l], saved[l], nb, tokens, count_all))
        if last:
            loss_part, d_head_t, d_fmod = outs[:3]
            outs = outs[3:]
        if first:
            d_patch = outs[0]
        else:
            d_stream = outs[0]
        layer_grads[l] = outs[1:4]
        d_mods[l] = outs[4]
    d_raw = jnp.stack([d[:, :6] for d in d_mods]).reshape(layers, lat_count, places.count, ada_rows)
    d_raw = d_raw.transpose(1, 2, 0, 3).reshape(lat_count, places.count, SPLIT, part_rows)
    d_raw = d_raw.swapaxes(1, 2).reshape(lat_count, -1)
    d_raw = jnp.pad(d_raw, ((0, 8 - lat_count), (0, 0)))
    small_grads = condition_back(
        feat, class_hot, slot_full, ada_full, pre, cond, d_raw, d_fmod, d_patch, d_head_t
    )
    grads = [from_slot(g) for g in small_grads[:slots]]
    grads += [pad_rows(g.reshape(places.count, part_rows, D)) for g in small_grads[slots:]]
    for l in reversed(range(layers)):
        for k in range(3):
            grads.append(pad_rows(layer_grads[l][k].reshape(places.count, wide_rows, D)))
    *summed, both, stats = reduce_all(places, slots, grads, loss_part, squares)
    wide = summed[slots + SPLIT :]
    wide = [wide[3 * (layers - 1 - l) + k] for l in range(layers) for k in range(3)]
    states = []
    for shape_it, triple in (
        (swap, (entry_weight, entry_first, entry_second)),
        (swap, (class_table, class_first, class_second)),
        (swap, (attn_weight, attn_first, attn_second)),
        (swap, (ffn_in_weight, ffn_in_first, ffn_in_second)),
        (lambda a: a, (ffn_out_weight, ffn_out_first, ffn_out_second)),
        (flat_ada, (ada_weight, ada_first, ada_second)),
        (lambda a: a, (final_weight, final_first, final_second)),
    ):
        states.extend(shape_it(a) for a in triple)
    out = adam_all(slots, layers, count_rms, stats, both, [*summed[slots : slots + SPLIT], *wide], states)
    news = []
    for at in range(21):
        value = out[at]
        if at // 3 == 5:
            value = value.reshape(layers, ada_rows, D)
        news.append(value if at // 3 in (4, 6) else swap(value))
    return (*news, out[21].reshape(()), out[22].reshape(()), out[23].reshape(layers))


def solution(mesh):
    lead = P(("dp", "tp"), None, None)
    ids = P(("dp", "tp"))
    wide = P(None, "dp")
    cols = P(None, None, ("dp", "tp"))
    rows = P(None, ("dp", "tp"), None)
    top = P("dp", None)
    return jax.shard_map(
        body,
        mesh=mesh,
        in_specs=(
            lead,
            lead,
            ids,
            ids,
            ids,
            wide,
            wide,
            cols,
            cols,
            rows,
            cols,
            top,
            wide,
            wide,
            wide,
            wide,
            cols,
            cols,
            cols,
            cols,
            rows,
            rows,
            cols,
            cols,
            top,
            top,
        ),
        out_specs=(wide,) * 6 + (cols,) * 6 + (rows,) * 3 + (cols,) * 3 + (top,) * 3 + (P(), P(), P()),
        check_vma=False,
    )
```

profile of v0, /device:TPU:0, one launch (start us, length us, event | category | flops | bytes accessed | tf_op | source)
XLA Modules:
  0.0 303.8 jit_solution(7321394518913535535)
XLA Ops:
  0.7 0.7 compare_select_fusion
  1.3 0.7 convert_element_type.35
  2.0 0.1 fusion.10
  2.1 0.7 fusion.17
  2.8 0.7 fusion.8.refs_0_
  3.5 0.7 fusion.2.refs_1_
  4.2 1.6 add_convert_fusion.refs_0_.refs_1_
  5.8 1.0 multiply_sine_fusion.1
  6.8 1.0 pad_maximum_fusion.refs_2_
  7.7 79.8 %gather_weights.1 = (bf16[4,2,2,2,48,384]{5,4,3,2,1,0:T(8,128)(2,1)}, bf16[4,2,2,2,48,384]{5,4,3,2,1,0:T(8,128)(2,1)}, bf16[4,2,2,2,48,384]{5,4,3,2,1,0:T(8,128)...) custom-call(f32[48,656]{1,0:T(8,128)} %bitcast.126, ...), custom_call_target="tpu_custom_call" | custom-call | tf_op jit(solution)/shard_map/gather_weights/pallas_call | solution.py:542
  87.6 5.1 %condition.1 = (f32[8,4608]{1,0:T(8,128)}, f32[4,8,384]{2,1,0:T(8,128)}, f32[8,384]{1,0:T(8,128)}, f32[8,384]{1,0:T(8,128)}, bf16[384,16]{1,0:T(8,128)(2,1)}, /*index=5*/bf16[384,32]{1,0:T(8,128)(2,1)}) custom-call(bf16[8,384]{1,0:T(8,128)(2,1)} %fusion.8.refs_0_, bf16[8,1152]{1,0:T(8,128)(2,1)} %fusion.2.refs_1_, bf16[8,4,48,384]{3,2,1,0:T(8,128)(2,1)} %bitcast.99, ...), custom_call_target="tpu_custom_call" | custom-call | tf_op jit(solution)/shard_map/condition/pallas_call | solution.py:800
  92.7 0.9 slice.15
  93.6 0.1 reshape.135
  93.7 0.1 copy.55
  93.9 0.2 reshape.136
  94.1 0.1 reshape.137
  94.2 0.6 fusion.1
  94.9 20.0 %block_forward.2 = (f32[1024,384]{1,0:T(8,128)}, f32[1024,384]{1,0:T(8,128)}, bf16[1024,1152]{1,0:T(8,128)(2,1)}, bf16[1024,1536]{1,0:T(8,128)(2,1)}, bf16[1024,...) custom-call(bf16[4,16,256]{2,1,0:T(8,128)(2,1)} %add_convert_fusion., ...), custom_call_target="tpu_custom_call" | custom-call | tf_op jit(solution)/shard_map/block_forward/pallas_call | solution.py:334
  114.9 19.4 %block_forward.3 = (f32[1024,384]{1,0:T(8,128)}, bf16[1024,1152]{1,0:T(8,128)(2,1)}, bf16[1024,1536]{1,0:T(8,128)(2,1)}, bf16[1024,384]{1,0:T(8,128)(2,1)}, bf16...) custom-call(f32[1024,384]{1,0:T(8,128)} %get-tuple-element.127.refs_, ...), custom_call_target="tpu_custom_call" | custom-call | tf_op jit(solution)/shard_map/block_forward/pallas_call | solution.py:334
  134.3 29.9 %block_backward.2 = (f32[4,8,256]{2,1,0:T(8,128)}, f32[32,384]{1,0:T(8,128)}, f32[4,8,384]{2,1,0:T(8,128)}, f32[1024,384]{1,0:T(8,128)}, bf16[1536,384]{1,0:T(8,...) custom-call(f32[1024,384]{1,0:T(8,128)} %get-tuple-element.131.refs_0_, ...), custom_call_target="tpu_custom_call" | custom-call | tf_op jit(solution)/shard_map/block_backward/pallas_call | solution.py:387
  164.2 0.0 copy-start
  164.2 27.9 %block_backward.3 = (f32[16,384]{1,0:T(8,128)}, bf16[1536,384]{1,0:T(8,128)(2,1)}, bf16[1536,384]{1,0:T(8,128)(2,1)}, bf16[1536,384]{1,0:T(8,128)(2,1)}, f32[4,8,384]{2,1,0:T(8,128)}) custom-call(f32[1024,384]{1,0:T(8,128)} %get-tuple-element.142.refs_0_, bf16[4,16,256]{2,1,0:T(8,128)(2,1)} %add_convert_fusion.refs_0_.refs_1_, ...), custom_call_target="tpu_custom_call" | custom-call | tf_op jit(solution)/shard_map/block_backward/pallas_call | solution.py:387
  192.1 0.1 stack.10
  192.2 0.9 stack.9
  193.1 0.1 copy.52
  193.2 0.2 reshape.138
  193.4 0.2 reshape.139
  193.6 0.7 pad.19.refs_9_
  194.3 6.8 %condition_back.1 = (bf16[8,4,48,384]{3,2,1,0:T(8,128)(2,1)}, bf16[8,4,48,384]{3,2,1,0:T(8,128)(2,1)}, bf16[1536,384]{1,0:T(8,128)(2,1)}, bf16[1536,384]{1,0:T(8,128)(2,1)}, bf16[1536,384]{1,0:T(8,128)(2,1)}) custom-call(bf16[8,384]{1,0:T(8,128)(2,1)} %fusion.8.refs_0_, bf16[8,1152]{1,0:T(8,128)(2,1)} %fusion.2.refs_1_, bf16[8,4,48,384]{3,2,1,0:T(8,128)(2,1)} %bitcast.100, ...), custom_call_target="tpu_custom_call" | custom-call | tf_op jit(solution)/shard_map/condition_back/pallas_call | solution.py:863
  201.1 96.9 %reduce_gradients.1 = (f32[48,384]{1,0:T(8,128)}, f32[48,384]{1,0:T(8,128)}, f32[48,384]{1,0:T(8,128)}, f32[48,384]{1,0:T(8,128)}, f32[48,384]{1,0:T(8,128)}, /*...) custom-call(bf16[4,2,2,2,48,384]{5,4,3,2,1,0:T(8,128)(2,1)} %bitcast, ...), custom_call_target="tpu_custom_call" | custom-call | tf_op jit(solution)/shard_map/reduce_gradients/pallas_call | solution.py:719
  298.0 4.6 %adam.1 = (f32[48,656]{1,0:T(8,128)}, f32[48,656]{1,0:T(8,128)}, f32[48,656]{1,0:T(8,128)}, f32[48,1001]{1,0:T(8,128)}, f32[48,1001]{1,0:T(8,128)}, /*index=5*/f...) custom-call(f32[8,128]{1,0:T(8,128)} %get-tuple-element.171.refs_0_,, ...), custom_call_target="tpu_custom_call" | custom-call | tf_op jit(solution)/shard_map/adam/pallas_call | solution.py:924
  302.5 1.2 reduce
  (8 shorter events, 0.1 us)
Async XLA Ops:
  164.2 27.9 %copy-start = (f32[4,8,384]{2,1,0:T(8,128)S(1)}, f32[4,8,384]{2,1,0:T(8,128)}, u32[]{:S(2)}) copy-start(f32[4,8,384]{2,1,0:T(8,128)} %get-tuple-element.153) | copy-start | bytes 147460
where the time goes:
time: 304 us
  Pallas kernels  290 us (95%)
  other arithmetic  8.3 us (3%)
  local copies, waits for them, and re-layouts  4.33 us (1%)
    pallas_call x1, Pallas kernels, reduce_all(): pl.pallas_call(functools.partial(reduce_kernel, places, chunks, slots, la...  96.9 us
    pallas_call x1, Pallas kernels, gather_all(): pl.pallas_call(functools.partial(gather_kernel, places, slots, layers), o...  79.8 us
    pallas_call x2, Pallas kernels, backward_layer(): pl.pallas_call(functools.partial(backward_kernel, first, last, nb, tokens...  57.8 us
    pallas_call x2, Pallas kernels, forward_layer(): pl.pallas_call(functools.partial(forward_kernel, first, nb, tokens), grid...  39.4 us
    pallas_call x1, Pallas kernels, condition_back(): pl.pallas_call(functools.partial(condition_back_kernel, len(slot_full), l...  6.82 us

commit v1 on v0

--- a/solution.py
+++ b/solution.py
@@ -350,8 +350,13 @@
     in_specs = []
     args = list(entry_args)
     if last:
+        if isinstance(args[0], tuple):
+            layer = args[0][1]
+            in_specs.append(pl.BlockSpec((None, rows, D), lambda i: (layer, i, 0)))
+            args[0] = args[0][0]
+        else:
+            in_specs.append(lead_spec((rows, D), 2))
         in_specs += [
-            lead_spec((rows, D), 2),
             lead_spec((nb, 8, D), 3),
             whole_spec(args[2]),
             lead_spec((nb, PATCH_IN, tokens), 3),
@@ -362,7 +367,15 @@
     if first:
         in_specs += [lead_spec((nb, PATCH_IN, tokens), 3)]
     in_specs += [lead_spec((nb, 8, D), 3)] + [whole_spec(w) for w in weights]
-    in_specs += [lead_spec((rows, s.shape[1]), 2) for s in saved]
+    for kept in saved:
+        if isinstance(kept, tuple):
+            array, layer = kept
+            in_specs.append(
+                pl.BlockSpec((None, rows, array.shape[2]), lambda i, layer=layer: (layer, i, 0))
+            )
+        else:
+            in_specs.append(lead_spec((rows, kept.shape[1]), 2))
+    saved = [kept[0] if isinstance(kept, tuple) else kept for kept in saved]
     out_shape = []
     out_specs = []
 
@@ -459,13 +472,195 @@
     ]
 
 
+class Traffic:
+    def __init__(self, places, mine, sends, recvs, locals_):
+        self.places, self.mine = places, mine
+        self.sends, self.recvs, self.locals = sends, recvs, locals_
+        self.used = self.used_local = 0
+        self.copies = []
+
+    def remote(self, source, target_ref, digit, shift):
+        target, _ = self.places.other(self.mine, digit, shift)
+        at = self.used
+        self.used += 1
+        copy = pltpu.make_async_remote_copy(
+            src_ref=source,
+            dst_ref=target_ref,
+            send_sem=self.sends.at[at],
+            recv_sem=self.recvs.at[at],
+            device_id=target,
+            device_id_type=MESH,
+        )
+        self.copies.append(copy)
+        return copy
+
+    def local(self, source, target_ref):
+        at = self.used_local
+        self.used_local += 1
+        return pltpu.make_async_copy(source, target_ref, self.locals.at[at])
+
+    def ahead(self, digit, shift):
+        return lax.rem(self.mine[digit] + shift, self.places.dims[digit])
+
+    def finish(self):
+        for copy in self.copies:
+            copy.wait_send()
+
+
+def copies_per_part(places):
+    dims = places.dims
+    return sum(dims) - len(dims) + max(dims) * max(dims)
+
+
+def gather_job(traffic, odd, source, out):
+    places, mine = traffic.places, traffic.mine
+    order = places.order(odd)
+    depth = len(order)
+    split = depth - 2 if depth >= 4 else -1
+    own = traffic.local(source, out.at[tuple(mine)])
+    waits = [[] for _ in range(depth + 1)]
+    starts = [[] for _ in range(depth + 1)]
+
+    def region(done, fixed):
+        return tuple(fixed.get(d, slice(None) if d in done else mine[d]) for d in range(depth))
+
+    for stage, digit in enumerate(order):
+        done = order[:stage]
+        for shift in range(1, places.dims[digit]):
+            pieces = [(stage, {})]
+            if stage == split:
+                before = order[stage - 1]
+                pieces = [(stage - 1, {before: mine[before]})]
+                pieces += [(stage, {before: traffic.ahead(before, k)}) for k in range(1, places.dims[before])]
+            for when, fixed in pieces:
+                where = region(done, fixed)
+                copy = traffic.remote(source if stage == 0 else out.at[where], out.at[where], digit, shift)
+                starts[when].append(copy)
+                waits[stage + 1].append(copy)
+
+    def action(k):
+        if k == 0:
+            own.start()
+        if k == 1:
+            own.wait()
+        for copy in waits[k]:
+            copy.wait_recv()
+        for copy in starts[k]:
+            copy.start()
+
+    return [functools.partial(action, k) for k in range(depth + 1)]
+
+
+def land_shapes(places, odd, block):
+    route = places.order(odd)[::-1]
+    depth = len(route)
+    shapes = []
+    for stage, digit in enumerate(route):
+        left = [d for d in range(depth) if d not in route[: stage + 1]]
+        shapes.append((places.dims[digit] - 1, *(places.dims[d] for d in left), *block))
+    return shapes
+
+
+def reduce_job(traffic, odd, source, acc, lands, out):
+    places, mine = traffic.places, traffic.mine
+    route = places.order(odd)[::-1]
+    depth = len(route)
+    split = 1 if depth >= 4 else -1
+    waits = [[] for _ in range(depth + 1)]
+    starts = [[] for _ in range(depth + 1)]
+    adds = [[] for _ in range(depth + 1)]
+    own = traffic.local(
+        source.at[tuple(mine[d] if d == route[0] else slice(None) for d in range(depth))], acc
+    )
+
+    def left_of(stage):
+        return [d for d in range(depth) if d not in route[: stage + 1]]
+
+    def in_acc(values):
+        return tuple(values.get(d, mine[d]) for d in range(depth) if d != route[0])
+
+    for stage, digit in enumerate(route):
+        gone = route[:stage]
+        left = left_of(stage)
+        pieces = [(stage + 1, {})]
+        if stage == split:
+            after = route[stage + 1]
+            pieces = [(stage + 1, {after: traffic.ahead(after, k)}) for k in range(1, places.dims[after])]
+            pieces += [(stage + 2, {after: mine[after]})]
+        for when, fixed in pieces:
+            for shift in range(1, places.dims[digit]):
+                values = {d: slice(None) for d in left} | fixed | {digit: traffic.ahead(digit, shift)}
+                if stage == 0:
+                    sent = source.at[tuple(values[d] for d in range(depth))]
+                else:
+                    sent = acc.at[in_acc(values)]
+                target = lands[stage].at[(shift - 1, *(values[d] for d in left))]
+                copy = traffic.remote(sent, target, digit, shift)
+                starts[stage].append(copy)
+                waits[when].append(copy)
+            adds[when].append((stage, fixed))
+
+    def add(group):
+        stage, fixed = group[-1]
+        free = [d for d in left_of(stage) if d not in fixed]
+        count = math.prod(places.dims[d] for d in free)
+        last = stage == depth - 1
+
+        def one(flat, carry):
+            values = dict(fixed)
+            rest = flat
+            for d in reversed(free):
+                values[d] = lax.rem(rest, places.dims[d])
+                rest = rest // places.dims[d]
+            total = acc[in_acc(values)].astype(jnp.float32)
+            for near, _ in group:
+                for shift in range(places.dims[route[near]] - 1):
+                    index = (shift, *(values.get(d, mine[d]) for d in left_of(near)))
+                    total = total + lands[near][index].astype(jnp.float32)
+            if last:
+                out[...] = total
+            else:
+                acc[in_acc(values)] = total.astype(BF)
+            return carry
+
+        lax.fori_loop(0, count, one, 0)
+
+    def action(k):
+        if k == 0:
+            own.start()
+        if k == 1:
+            own.wait()
+        for copy in waits[k]:
+            copy.wait_recv()
+        if k == split + 2:
+            add(adds[k])
+        else:
+            for entry in adds[k]:
+                add([entry])
+        if k < depth:
+            for copy in starts[k]:
+                copy.start()
+
+    return [functools.partial(action, k) for k in range(depth + 1)]
+
+
+def in_waves(jobs):
+    pairs = [jobs[at : at + 2] for at in range(0, len(jobs), 2)]
+    depth = len(jobs[0])
+    sequence = []
+    for tick in range(len(pairs) + depth - 1):
+        for k in range(depth):
+            if 0 <= tick - k < len(pairs):
+                sequence.extend(job[k] for job in pairs[tick - k])
+    return sequence
+
+
 def gather_kernel(places, slots, layers, *refs):
     entry_ref, table_ref, final_ref, ada_ref, attn_ref, in_ref, out_ref = refs[:7]
     chunks = slots + SPLIT + 3 * layers
     outs = refs[7 : 7 + chunks]
     small, packed, send_sems, recv_sems, own_sems = refs[7 + chunks :]
     mine = places.mine()
-    depth = len(places.dims)
     small[...] = jnp.zeros_like(small)
     for k, at, source, low, high in small_blocks(entry_ref, table_ref, final_ref):
         small[k, : source.shape[0], at : at + high - low] = source[:, low:high].astype(BF)
@@ -479,50 +674,11 @@
     ins = [small.at[first + s] for s in range(slots)]
     ins += [packed.at[m] for m in range(SPLIT + 3 * layers)]
     places.barrier(mine)
-    started = {}
-    own = []
-    for m in range(chunks):
-        copy = pltpu.make_async_copy(ins[m], outs[m].at[tuple(mine)], own_sems.at[m])
-        copy.start()
-        own.append(copy)
-
-    def start(m, stage):
-        order = places.order(m % 2 == 1)
-        digit = order[stage]
-        done = order[:stage]
-        where = tuple(slice(None) if d in done else mine[d] for d in range(depth))
-        source = ins[m] if stage == 0 else outs[m].at[where]
-        copies = []
-        for shift in range(1, places.dims[digit]):
-            target, _ = places.other(mine, digit, shift)
-            copy = pltpu.make_async_remote_copy(
-                src_ref=source,
-                dst_ref=outs[m].at[where],
-                send_sem=send_sems.at[m, stage, shift - 1],
-                recv_sem=recv_sems.at[m, stage, shift - 1],
-                device_id=target,
-                device_id_type=MESH,
-            )
-            copy.start()
-            copies.append(copy)
-        started[m, stage] = copies
-
-    pairs = (chunks + 1) // 2
-    for tick in range(pairs + depth):
-        for stage in range(depth, -1, -1):
-            if not 0 <= tick - stage < pairs:
-                continue
-            for m in range(2 * (tick - stage), min(2 * (tick - stage) + 2, chunks)):
-                if stage == 1:
-                    own[m].wait()
-                if stage > 0:
-                    for copy in started[m, stage - 1]:
-                        copy.wait_recv()
-                if stage < depth:
-                    start(m, stage)
-    for copies in started.values():
-        for copy in copies:
-            copy.wait_send()
+    traffic = Traffic(places, mine, send_sems, recv_sems, own_sems)
+    jobs = [gather_job(traffic, m % 2 == 1, ins[m], outs[m]) for m in range(chunks)]
+    for action in in_waves(jobs):
+        action()
+    traffic.finish()
 
 
 def pad16(rows):
@@ -531,7 +687,6 @@
 
 def gather_all(places, slots, entry_t, table_t, final, ada_t, attn_t, in_t, out_w):
     layers = attn_t.shape[0]
-    depth, widest = len(places.dims), max(places.dims)
     small_rows, ada_rows = pad16(final.shape[0]), pad16(-(-ada_t.shape[0] // SPLIT))
     wide_rows = pad16(attn_t.shape[1])
     sizes = [small_rows] * slots + [ada_rows] * SPLIT + [wide_rows] * (3 * layers)
@@ -547,8 +702,8 @@
         scratch_shapes=[
             pltpu.VMEM((slots * lax.axis_size("tp"), small_rows, D), BF),
             pltpu.VMEM((SPLIT + 3 * layers, packed_rows, D), BF),
-            pltpu.SemaphoreType.DMA((chunks, depth, widest - 1)),
-            pltpu.SemaphoreType.DMA((chunks, depth, widest - 1)),
+            pltpu.SemaphoreType.DMA((chunks * copies_per_part(places),)),
+            pltpu.SemaphoreType.DMA((chunks * copies_per_part(places),)),
             pltpu.SemaphoreType.DMA((chunks,)),
         ],
         compiler_params=pltpu.CompilerParams(collective_id=1, has_side_effects=True, vmem_limit_bytes=LIMIT),
@@ -572,83 +727,14 @@
     send_sems, recv_sems, own_sems = refs[chunks * (1 + depth) :]
     mine = places.mine()
     places.barrier(mine)
-    started = {}
-    own = []
-
-    def route(m):
-        return places.order(m % 2 == 1)[::-1]
-
-    for m in range(chunks):
-        where = tuple(slice(None) if d < depth - 1 else mine[d] for d in range(depth))
-        copy = pltpu.make_async_copy(ins[m].at[where], accs[m], own_sems.at[m])
-        copy.start()
-        own.append(copy)
-
-    def start(m, stage):
-        order = route(m)
-        digit = order[stage]
-        gone = order[:stage]
-        copies = []
-        for shift in range(1, places.dims[digit]):
-            target, value = places.other(mine, digit, shift)
-            where = tuple(
-                mine[d] if d in gone else (value if d == digit else slice(None)) for d in range(depth)
-            )
-            source = ins[m].at[where] if stage == 0 else accs[m].at[where[: depth - 1]]
-            copy = pltpu.make_async_remote_copy(
-                src_ref=source,
-                dst_ref=lands[m * depth + stage].at[shift - 1],
-                send_sem=send_sems.at[m, stage, shift - 1],
-                recv_sem=recv_sems.at[m, stage, shift - 1],
-                device_id=target,
-                device_id_type=MESH,
-            )
-            copy.start()
-            copies.append(copy)
-        started[m, stage] = copies
-
-    def add(m, stage):
-        order = route(m)
-        gone = order[: stage + 1]
-        left = [d for d in range(depth) if d not in gone]
-        land = lands[m * depth + stage]
-        count = math.prod(places.dims[d] for d in left)
-
-        def one(flat, carry):
-            values = {}
-            rest = flat
-            for d in reversed(left):
-                values[d] = lax.rem(rest, places.dims[d])
-                rest = rest // places.dims[d]
-            here = tuple(values.get(d, mine[d]) for d in range(depth - 1))
-            total = accs[m][here].astype(jnp.float32)
-            for shift in range(1, places.dims[order[stage]]):
-                total = total + land[(shift - 1, *(values[d] for d in left))].astype(jnp.float32)
-            if left:
-                accs[m][here] = total.astype(BF)
-            else:
-                outs[m][...] = total
-            return carry
-
-        lax.fori_loop(0, count, one, 0)
-
-    pairs = (chunks + 1) // 2
-    for tick in range(pairs + depth):
-        for stage in range(depth, -1, -1):
-            if not 0 <= tick - stage < pairs:
-                continue
-            for m in range(2 * (tick - stage), min(2 * (tick - stage) + 2, chunks)):
-                if stage == 1:
-                    own[m].wait()
-                if stage > 0:
-                    for copy in started[m, stage - 1]:
-                        copy.wait_recv()
-                    add(m, stage - 1)
-                if stage < depth:
-                    start(m, stage)
-    for copies in started.values():
-        for copy in copies:
-            copy.wait_send()
+    traffic = Traffic(places, mine, send_sems, recv_sems, own_sems)
+    jobs = [
+        reduce_job(traffic, m % 2 == 1, ins[m], accs[m], lands[m * depth : (m + 1) * depth], outs[m])
+        for m in range(chunks)
+    ]
+    for action in in_waves(jobs):
+        action()
+    traffic.finish()
 
     def lane_sums(rows):
         total = jnp.sum(rows, axis=0, keepdims=True)
@@ -711,11 +797,7 @@
     blocks = [p.shape[1:] for p in parts]
     lands = []
     for m in range(chunks):
-        order = places.order(m % 2 == 1)[::-1]
-        for stage in range(depth):
-            gone = order[: stage + 1]
-            left = tuple(dims[d] for d in range(depth) if d not in gone)
-            lands.append(pltpu.VMEM((dims[order[stage]] - 1, *left, *blocks[m]), BF))
+        lands += [pltpu.VMEM(shape, BF) for shape in land_shapes(places, m % 2 == 1, blocks[m])]
     return pl.pallas_call(
         functools.partial(reduce_kernel, places, chunks, slots, layers),
         out_shape=[jax.ShapeDtypeStruct(block, jnp.float32) for block in blocks]
@@ -728,8 +810,8 @@
         scratch_shapes=[pltpu.VMEM(dims[:-1] + block, BF) for block in blocks]
         + lands
         + [
-            pltpu.SemaphoreType.DMA((chunks, depth, widest - 1)),
-            pltpu.SemaphoreType.DMA((chunks, depth, widest - 1)),
+            pltpu.SemaphoreType.DMA((chunks * copies_per_part(places),)),
+            pltpu.SemaphoreType.DMA((chunks * copies_per_part(places),)),
             pltpu.SemaphoreType.DMA((chunks,)),
             pltpu.VMEM((depth, widest, 8, 128), jnp.float32),
             pltpu.SemaphoreType.DMA((depth, widest - 1)),
@@ -929,6 +1011,350 @@
         out_specs=[vmem] * 24,
         compiler_params=pltpu.CompilerParams(vmem_limit_bytes=LIMIT),
         name="adam",
+    )(*args)
+
+
+def modulation_pieces(layers, ada_rows, part_rows, count):
+    pieces = []
+    for j in range(count):
+        for l in range(layers):
+            low = l * ada_rows
+            while low < (l + 1) * ada_rows:
+                p, r = divmod(low, part_rows)
+                length = min((l + 1) * ada_rows - low, part_rows - r)
+                pieces.append((l, j * ada_rows + low - l * ada_rows, p, j * part_rows + r, length))
+                low += length
+    return pieces
+
+
+def embed_condition(slots, lat_count, feat_ref, hot_ref, slot_refs, pre_ref, cond_ref, fmod_ref):
+    pre = dot_nt(feat_ref[...], block_of(slot_refs, 0))
+    pre_ref[...] = pre
+    cond = dot_nt(silu(pre).astype(BF), block_of(slot_refs, 1))
+    for k in range(3):
+        cond = cond + dot_nt(hot_ref[:, k * D : (k + 1) * D], block_of(slot_refs, 2 + k))
+    cond_ref[...] = cond
+    act = silu(cond).astype(BF)
+    for k in range(2):
+        fmod_ref[:, k * D : (k + 1) * D] = dot_nn(act, block_of(slot_refs, 5 + k))
+
+
+def mod_rows(mod_ref, index, n, nb, part):
+    rows = [mod_ref[(*index, pl.ds(n * nb + b, 1), slice(part * D, (part + 1) * D))] for b in range(nb)]
+    return jnp.stack(rows, axis=0)
+
+
+def attend_forward(nb, tokens, stream, mod, attn_w, out_w, qkv_ref, probs_ref, mixed_ref, branch_ref):
+    rows = nb * tokens
+    hat, _ = norm_rows(stream)
+    attn_in = (hat * (1.0 + mod(1)) + mod(0)).astype(BF).reshape(rows, D)
+    qkv_ref[...] = dot_nt(attn_in, attn_w[...]).astype(BF)
+    masks = half_masks()
+    for b in range(nb):
+        here = slice(b * tokens, (b + 1) * tokens)
+        for pair in range(HEADS // 2):
+            col = pair * 2 * HEAD_DIM
+            queries = qkv_ref[here, col : col + 2 * HEAD_DIM] * jnp.asarray(HEAD_DIM**-0.5, BF)
+            keys = stack_heads(qkv_ref[here, D + col : D + col + 2 * HEAD_DIM], masks)
+            values = stack_heads(qkv_ref[here, 2 * D + col : 2 * D + col + 2 * HEAD_DIM], masks)
+            scores = dot_nt(queries, keys)
+            halves = []
+            for side in range(2):
+                part = scores[:, side * tokens : (side + 1) * tokens]
+                grown = jnp.exp(part - jnp.max(part, axis=-1, keepdims=True))
+                halves.append((grown * (1.0 / jnp.sum(grown, axis=-1, keepdims=True))).astype(BF))
+            probs = jnp.concatenate(halves, axis=1)
+            probs_ref[here, pair * 2 * tokens : (pair + 1) * 2 * tokens] = probs
+            mixed_ref[here, col : col + 2 * HEAD_DIM] = dot_nn(probs, values).astype(BF)
+    branch = dot_nt(mixed_ref[...], out_w[...])
+    branch_ref[...] = branch.astype(BF)
+    return stream + mod(2) * branch.reshape(nb, tokens, D)
+
+
+def feed_forward(nb, tokens, middle, mod, in_w, out_w, mlp_ref, act_ref, slope_ref):
+    rows = nb * tokens
+    hat, _ = norm_rows(middle)
+    mlp_in = (hat * (1.0 + mod(4)) + mod(3)).astype(BF).reshape(rows, D)
+    hidden = dot_nt(mlp_in, in_w[...])
+    squared = hidden * hidden
+    bent = jnp.tanh(hidden * (GELU_A + (GELU_A * GELU_B) * squared))
+    half = 0.5 * hidden
+    act = (half + half * bent).astype(BF)
+    act_ref[...] = act
+    slope_ref[...] = (
+        0.5
+        + 0.5 * bent
+        + half * (1.0 - bent * bent) * (GELU_A + (3.0 * GELU_A * GELU_B) * squared)
+    ).astype(BF)
+    mlp = dot_nn(act, out_w[...])
+    mlp_ref[...] = mlp.astype(BF)
+    return middle + mod(5) * mlp.reshape(nb, tokens, D)
+
+
+def waves(jobs):
+    pairs = [jobs[at : at + 2] for at in range(0, len(jobs), 2)]
+    depth = len(jobs[0])
+    ticks = []
+    for tick in range(len(pairs) + depth - 1):
+        ticks.append(
+            [job[k] for k in range(depth) if 0 <= tick - k < len(pairs) for job in pairs[tick - k]]
+        )
+    return ticks
+
+
+def fused_forward_kernel(places, slots, layers, nb, tokens, lat_count, sizes, *refs):
+    small_rows, ada_rows, part_rows, wide_rows = sizes
+    chunks = slots + SPLIT + 3 * layers
+    entry_ref, table_ref, final_ref, ada_ref, attn_ref, in_ref, out_ref = refs[:7]
+    feat_ref, hot_ref, noisy_ref, pos_ref = refs[7:11]
+    given = refs[11 : 11 + chunks]
+    (
+        mods_ref,
+        fmod_ref,
+        pre_ref,
+        cond_ref,
+        start_ref,
+        result_ref,
+        qkv_ref,
+        probs_ref,
+        mixed_ref,
+        branch_ref,
+        middle_ref,
+        mlp_ref,
+        act_ref,
+        slope_ref,
+        square_ref,
+    ) = refs[11 + chunks : 26 + chunks]
+    refs = refs[26 + chunks :]
+    fulls = refs[:chunks]
+    small, packed, stream_s, middle_s, send_sems, recv_sems, own_sems, give_sems = refs[chunks:]
+    l, h, n = (pl.program_id(axis) for axis in range(3))
+    mine = places.mine()
+    first = lax.axis_index("tp") * slots
+    order = [*range(slots), slots, slots + 1, slots + SPLIT, slots + SPLIT + 1, slots + SPLIT + 2, slots + 2]
+    order += range(slots + SPLIT + 3, chunks)
+    sources = [small.at[first + s] for s in range(slots)] + [packed.at[m] for m in range(SPLIT + 3 * layers)]
+    traffic = Traffic(places, mine, send_sems, recv_sems, own_sems)
+    jobs = [gather_job(traffic, at % 2 == 1, sources[m], fulls[m]) for at, m in enumerate(order)]
+    ticks = waves(jobs)
+    handed = [
+        pltpu.make_async_copy(fulls[m], given[m], give_sems.at[m]) for m in range(chunks)
+    ]
+
+    def flat(m, rows):
+        return fulls[m].reshape(places.count * rows, D)
+
+    def run(numbers):
+        for tick in numbers:
+            for action in ticks[tick]:
+                action()
+
+    def at_step(layer, half, step):
+        return pl.when((l == layer) & (h == half) & (n == step))
+
+    def set_mods(layer):
+        act = silu(cond_ref[...]).astype(BF)
+        low, high = layer * ada_rows, (layer + 1) * ada_rows
+        parts = range(low // part_rows, -(-high // part_rows))
+        raw = {p: dot_nt(act, flat(slots + p, part_rows)[...]) for p in parts}
+        for ll, col, p, at, length in modulation_pieces(layers, ada_rows, part_rows, places.count):
+            if ll == layer:
+                mods_ref[layer, :, col : col + length] = raw[p][:, at : at + length]
+
+    slot_refs = [f.reshape(-1, lax.axis_size("tp"), small_rows, D) for f in fulls[:slots]]
+    last = len(ticks) - 1
+
+    @at_step(0, 0, 0)
+    def _():
+        small[...] = jnp.zeros_like(small)
+        for k, at, source, low, high in small_blocks(entry_ref, table_ref, final_ref):
+            small[k, : source.shape[0], at : at + high - low] = source[:, low:high].astype(BF)
+        for p in range(SPLIT):
+            packed[p] = ada_ref[p * part_rows : (p + 1) * part_rows, :].astype(BF)
+        for ll in range(layers):
+            for k, source in enumerate((attn_ref, in_ref, out_ref)):
+                packed[SPLIT + 3 * ll + k] = source[ll].astype(BF)
+        places.barrier(mine)
+        run(range(6))
+        embed_condition(slots, lat_count, feat_ref, hot_ref, slot_refs, pre_ref, cond_ref, fmod_ref)
+        set_mods(0)
+        run([6])
+
+    @at_step(0, 1, 0)
+    def _():
+        run([7])
+
+    @at_step(1, 0, 0)
+    def _():
+        run([8])
+        for layer in range(1, layers):
+            set_mods(layer)
+
+    @at_step(1, 1, 0)
+    def _():
+        run(range(9, last + 1))
+        for copy in handed:
+            copy.start()
+
+    rows = nb * tokens
+    here = pl.ds(pl.multiple_of(n * rows, rows), rows)
+
+    def weight(layer, k):
+        return flat(slots + SPLIT + 3 * layer + k, wide_rows)
+
+    for layer in range(layers):
+        mod = lambda part, layer=layer: mod_rows(mods_ref, (layer,), n, nb, part)
+
+        @pl.when((l == layer) & (h == 0))
+        def _(layer=layer, mod=mod):
+            if layer == 0:
+                patch = block_of(slot_refs, 0)[:, :PATCH_IN]
+                parts = [
+                    lax.dot_general(
+                        noisy_ref[b], patch, (((0,), (1,)), ((), ())), preferred_element_type=jnp.float32
+                    )
+                    + pos_ref[...]
+                    for b in range(nb)
+                ]
+                stream = parts[0] if nb == 1 else jnp.concatenate(parts, axis=0)
+                start_ref[...] = stream
+            else:
+                stream = stream_s[here, :]
+            stream = stream.reshape(nb, tokens, D)
+            middle = attend_forward(
+                nb,
+                tokens,
+                stream,
+                mod,
+                weight(layer, 0).at[: 3 * D],
+                weight(layer, 0).at[3 * D :],
+                qkv_ref.at[0],
+                probs_ref.at[0],
+                mixed_ref.at[0],
+                branch_ref.at[0],
+            )
+            middle_ref[0] = middle.reshape(rows, D)
+            middle_s[here, :] = middle.reshape(rows, D)
+
+        @pl.when((l == layer) & (h == 1))
+        def _(layer=layer, mod=mod):
+            middle = middle_s[here, :].reshape(nb, tokens, D)
+            result = feed_forward(
+                nb,
+                tokens,
+                middle,
+                mod,
+                weight(layer, 1),
+                weight(layer, 2),
+                mlp_ref.at[0],
+                act_ref.at[0],
+                slope_ref.at[0],
+            )
+            result_ref[0] = result.reshape(rows, D)
+            if layer < layers - 1:
+                stream_s[here, :] = result.reshape(rows, D)
+            square_ref[0, 0] = jnp.sum((result * result).reshape(rows // 8, 8, D), axis=0)
+
+    @at_step(layers - 1, 1, lat_count // nb - 1)
+    def _():
+        for copy in handed:
+            copy.wait()
+        traffic.finish()
+
+
+def fused_forward(places, slots, nb, weights_in, feat, hot, noisy, pos):
+    entry_t, table_t, final, ada_t, attn_t, in_t, out_w = weights_in
+    layers, wide_rows = attn_t.shape[:2]
+    lat_count, _, tokens = noisy.shape
+    small_rows, part_rows, ada_rows = final.shape[0], ada_t.shape[0] // SPLIT, ada_t.shape[0] // layers
+    sizes = [small_rows] * slots + [part_rows] * SPLIT + [wide_rows] * (3 * layers)
+    chunks = len(sizes)
+    steps = lat_count // nb
+    rows, total = nb * tokens, lat_count * tokens
+    full_shapes = [(*places.dims, r, D) for r in sizes]
+
+    def const(array):
+        return pl.BlockSpec(array.shape, lambda l, h, n: (0,) * array.ndim)
+
+    def const_shape(shape):
+        return pl.BlockSpec(shape, lambda l, h, n: (0,) * len(shape))
+
+    def early(l, h, n):
+        return jnp.where(h == 0, n, steps - 1)
+
+    def half_one(cols):
+        return pl.BlockSpec((1, rows, cols), lambda l, h, n: (l, early(l, h, n), 0))
+
+    def half_two(cols):
+        def index(l, h, n):
+            before = jnp.where(l == 0, 0, steps - 1)
+            return (jnp.where(h == 0, jnp.maximum(l - 1, 0), l), jnp.where(h == 0, before, n), 0)
+
+        return pl.BlockSpec((1, rows, cols), index)
+
+    def square_index(l, h, n):
+        before = jnp.where(l == 0, 0, steps - 1)
+        return (jnp.where(h == 0, jnp.maximum(l - 1, 0), l), jnp.where(h == 0, before, n), 0, 0)
+
+    out_shape = [jax.ShapeDtypeStruct(s, BF) for s in full_shapes]
+    out_specs = [pl.BlockSpec(memory_space=pl.ANY)] * chunks
+
+    def add(shape, kind, spec):
+        out_shape.append(jax.ShapeDtypeStruct(shape, kind))
+        out_specs.append(spec)
+
+    for shape in ((layers, 8, 6 * D), (8, 2 * D), (8, D), (8, D)):
+        add(shape, jnp.float32, const_shape(shape))
+    add(
+        (total, D),
+        jnp.float32,
+        pl.BlockSpec((rows, D), lambda l, h, n: (jnp.where((l == 0) & (h == 0), n, steps - 1), 0)),
+    )
+    add((layers, total, D), jnp.float32, half_two(D))
+    for cols, kind in ((3 * D, BF), (HEADS * tokens, BF), (D, BF), (D, BF), (D, jnp.float32)):
+        add((layers, total, cols), kind, half_one(cols))
+    for cols in (D, 4 * D, 4 * D):
+        add((layers, total, cols), BF, half_two(cols))
+    add((layers, steps, 8, D), jnp.float32, pl.BlockSpec((1, 1, 8, D), square_index))
+    args = (*weights_in, feat, hot, noisy, pos)
+    in_specs = [const(a) for a in args[:-2]]
+    in_specs.append(
+        pl.BlockSpec(
+            (nb, PATCH_IN, tokens), lambda l, h, n: (jnp.where((l == 0) & (h == 0), n, steps - 1), 0, 0)
+        )
+    )
+    in_specs.append(const(pos))
+    count = chunks * copies_per_part(places)
+    return pl.pallas_call(
+        functools.partial(
+            fused_forward_kernel,
+            places,
+            slots,
+            layers,
+            nb,
+            tokens,
+            lat_count,
+            (small_rows, ada_rows, part_rows, wide_rows),
+        ),
+        grid=(layers, 2, steps),
+        out_shape=out_shape,
+        in_specs=in_specs,
+        out_specs=out_specs,
+        scratch_shapes=[pltpu.VMEM(s, BF) for s in full_shapes]
+        + [
+            pltpu.VMEM((slots * lax.axis_size("tp"), small_rows, D), BF),
+            pltpu.VMEM((SPLIT + 3 * layers, wide_rows, D), BF),
+            pltpu.VMEM((total, D), jnp.float32),
+            pltpu.VMEM((total, D), jnp.float32),
+            pltpu.SemaphoreType.DMA((count,)),
+            pltpu.SemaphoreType.DMA((count,)),
+            pltpu.SemaphoreType.DMA((chunks,)),
+            pltpu.SemaphoreType.DMA((chunks,)),
+        ],
+        compiler_params=pltpu.CompilerParams(
+            collective_id=3, has_side_effects=True, vmem_limit_bytes=LIMIT
+        ),
+        name="gather_and_forward",
     )(*args)
 
 
@@ -1016,9 +1442,7 @@
     def flat_ada(array):
         return swap(array).reshape(layers * ada_rows, D)
 
-    gathered = gather_all(
-        places,
-        slots,
+    weights_in = (
         swap(entry_weight),
         swap(class_table),
         final_weight,
@@ -1027,7 +1451,6 @@
         swap(ffn_in_weight),
         ffn_out_weight,
     )
-
     def whole_rows(block, rows):
         return block[:, :rows].reshape(-1, D)
 
@@ -1043,35 +1466,50 @@
         block = block.reshape(n_tp, n_dp, dp_rows, D).swapaxes(0, 1)
         return pad_rows(block.reshape(places.count, dp_rows, D))
 
-    slot_full = [to_slot(g) for g in gathered[:slots]]
-    ada_full = [whole_rows(g, part_rows) for g in gathered[slots : slots + SPLIT]]
-    block_full = [whole_rows(g, wide_rows) for g in gathered[slots + SPLIT :]]
-    weights = [tuple(block_full[3 * l : 3 * l + 3]) for l in range(layers)]
-
     time_feat = time_table(timesteps, FREQ).astype(BF)
     feat = jnp.pad(time_feat, ((0, 8 - lat_count), (PATCH_IN, D - PATCH_IN - FREQ)))
     classes_used = jnp.where(drop_flags == 1, CLASSES, labels)
     classes_used = jnp.pad(classes_used, (0, 8 - lat_count), constant_values=3 * D)
     class_hot = (classes_used[:, None] == jnp.arange(3 * D, dtype=jnp.int32)[None, :]).astype(BF)
-    raw, fmod, pre, cond, patch_t, head = condition(feat, class_hot, slot_full, ada_full, lat_count)
-    mods = raw[:lat_count].reshape(lat_count, SPLIT, places.count, part_rows).swapaxes(1, 2)
-    mods = mods.reshape(lat_count, places.count, layers, ada_rows).transpose(2, 0, 1, 3)
-    mods = mods.reshape(layers, lat_count, 6, D)
-    mods = jnp.pad(mods, ((0, 0), (0, 0), (0, 2), (0, 0)))
-    mods = [mods[l] for l in range(layers)]
     pos = position_table(GRID, D)
-    saved = []
-    squares = []
-    stream = None
-    for l in range(layers):
-        if l == 0:
-            outs = forward_layer(True, (noisy, patch_t, pos), mods[l], weights[l], nb, tokens)
-            stream, outs = outs[0], outs[1:]
-        else:
-            outs = forward_layer(False, (stream,), mods[l], weights[l], nb, tokens)
-        saved.append((stream, *outs[1:9]))
-        stream = outs[0]
-        squares.append(outs[9])
+    fused = dp_rows == wide_rows == part_rows and dp_rows % 16 == 0 and len(places.dims) >= 4 and layers == 2
+    if fused:
+        outs = fused_forward(places, slots, nb, weights_in, feat, class_hot, noisy, pos)
+        gathered = [o.reshape((places.count,) + o.shape[-2:]) for o in outs[: slots + SPLIT + 3 * layers]]
+        mods_all, fmod_all, pre, cond, start, result, *kept, square = outs[slots + SPLIT + 3 * layers :]
+    else:
+        gathered = gather_all(places, slots, *weights_in)
+    slot_full = [to_slot(g) for g in gathered[:slots]]
+    ada_full = [whole_rows(g, part_rows) for g in gathered[slots : slots + SPLIT]]
+    block_full = [whole_rows(g, wide_rows) for g in gathered[slots + SPLIT :]]
+    weights = [tuple(block_full[3 * l : 3 * l + 3]) for l in range(layers)]
+
+    if fused:
+        mods = jnp.pad(mods_all[:, :lat_count].reshape(layers, lat_count, 6, D), ((0, 0), (0, 0), (0, 2), (0, 0)))
+        fmod = jnp.pad(fmod_all[:lat_count].reshape(lat_count, 2, D), ((0, 0), (0, 6), (0, 0)))
+        head = slot_full[4 % slots][:, 4 // slots].reshape(D, D)[:, 256 : 256 + OUT]
+        saved = [(start if l == 0 else (result, l - 1), *((k, l) for k in kept)) for l in range(layers)]
+        stream = (result, layers - 1)
+        squares = [square[l] for l in range(layers)]
+    else:
+        raw, fmod, pre, cond, patch_t, head = condition(feat, class_hot, slot_full, ada_full, lat_count)
+        mods = raw[:lat_count].reshape(lat_count, SPLIT, places.count, part_rows).swapaxes(1, 2)
+        mods = mods.reshape(lat_count, places.count, layers, ada_rows).transpose(2, 0, 1, 3)
+        mods = mods.reshape(layers, lat_count, 6, D)
+        mods = jnp.pad(mods, ((0, 0), (0, 0), (0, 2), (0, 0)))
+        mods = [mods[l] for l in range(layers)]
+        saved = []
+        squares = []
+        stream = None
+        for l in range(layers):
+            if l == 0:
+                outs = forward_layer(True, (noisy, patch_t, pos), mods[l], weights[l], nb, tokens)
+                stream, outs = outs[0], outs[1:]
+            else:
+                outs = forward_layer(False, (stream,), mods[l], weights[l], nb, tokens)
+            saved.append((stream, *outs[1:9]))
+            stream = outs[0]
+            squares.append(outs[9])
     layer_grads = [None] * layers
     d_mods = [None] * layers
     d_stream = None

time: 304 us -> 289 us (0.951)
  Pallas kernels: 290 us -> 271 us
  local copies, waits for them, and re-layouts: 4.33 us -> 8.25 us
    pallas_call x4 -> x1, Pallas kernels: 124 us -> 108 us  [fused_forward(): pl.pallas_call(functools.partial(fused_forward_kernel, places, slots, lay...]
where the time goes in v1:
time: 289 us; the launch traced here: 288 us
  Pallas kernels  271 us (94%)
  other arithmetic  8.37 us (3%)
  local copies, waits for them, and re-layouts  8.25 us (3%)
    pallas_call x1, Pallas kernels, fused_forward(): pl.pallas_call(functools.partial(fused_forward_kernel, places, slots, lay...  108 us
    pallas_call x1, Pallas kernels, reduce_all(): pl.pallas_call(functools.partial(reduce_kernel, places, chunks, slots, la...  94 us
    pallas_call x2, Pallas kernels, backward_layer(): pl.pallas_call(functools.partial(backward_kernel, first, last, nb, tokens...  57.7 us
    pallas_call x1, Pallas kernels, condition_back(): pl.pallas_call(functools.partial(condition_back_kernel, len(slot_full), l...  6.84 us

profile of v1, /device:TPU:0, one launch (start us, length us, event | category | flops | bytes accessed | tf_op | source)
XLA Modules:
  0.0 288.4 jit_solution(4314221167882511718)
XLA Ops:
  0.7 0.7 compare_select_fusion
  1.3 0.7 convert_element_type.37
  2.0 0.1 fusion.10
  2.1 0.7 fusion.17
  2.8 0.7 fusion.8.refs_7_.refs_0_
  3.5 0.7 fusion.2.refs_8_.refs_1_
  4.2 1.6 add_convert_fusion.refs_9_.refs_1_
  5.8 1.0 multiply_sine_fusion.1
  6.8 1.0 pad_maximum_fusion.refs_10_
  7.7 107.8 %gather_and_forward.1 = (bf16[4,2,2,2,48,384]{5,4,3,2,1,0:T(8,128)(2,1)}, bf16[4,2,2,2,48,384]{5,4,3,2,1,0:T(8,128)(2,1)}, bf16[4,2,2,2,48,384]{5,4,3,2,1,0:T(8,...) custom-call(f32[48,656]{1,0:T(8,128)} %bitcast.114, ...), custom_call_target="tpu_custom_call" | custom-call | tf_op jit(solution)/shard_map/gather_and_forward/pallas_call | solution.py:1328
  115.6 0.7 slice.30
  116.3 0.6 pad.22.refs_1_
  117.0 0.9 slice.33
  117.9 0.6 fusion.1
  118.6 1.5 slice_bitcast_fusion
  120.0 1.0 slice.40
  121.0 0.6 slice.41.refs_2_
  121.7 29.8 %block_backward.2 = (f32[4,8,256]{2,1,0:T(8,128)}, f32[32,384]{1,0:T(8,128)}, f32[4,8,384]{2,1,0:T(8,128)}, f32[1024,384]{1,0:T(8,128)}, bf16[1536,384]{1,0:T(8,...) custom-call(f32[2,1024,384]{2,1,0:T(8,128)} %get-tuple-element.110.refs_0_.refs_9_, ...), custom_call_target="tpu_custom_call" | custom-call | tf_op jit(solution)/shard_map/block_backward/pallas_call | solution.py:400
  151.5 0.0 copy-start
  151.5 27.9 %block_backward.3 = (f32[16,384]{1,0:T(8,128)}, bf16[1536,384]{1,0:T(8,128)(2,1)}, bf16[1536,384]{1,0:T(8,128)(2,1)}, bf16[1536,384]{1,0:T(8,128)(2,1)}, f32[4,8,384]{2,1,0:T(8,128)}) custom-call(f32[1024,384]{1,0:T(8,128)} %get-tuple-element.124.refs_0_, bf16[4,16,256]{2,1,0:T(8,128)(2,1)} %add_convert_fusion.refs_9_.refs_1_, ...), custom_call_target="tpu_custom_call" | custom-call | tf_op jit(solution)/shard_map/block_backward/pallas_call | solution.py:400
  179.4 0.0 copy-done
  179.4 0.1 stack.10
  179.5 0.9 stack.9
  180.4 0.1 copy.50
  180.5 0.2 reshape.134
  180.8 0.2 reshape.135
  180.9 0.7 pad.24.refs_9_
  181.6 6.8 %condition_back.1 = (bf16[8,4,48,384]{3,2,1,0:T(8,128)(2,1)}, bf16[8,4,48,384]{3,2,1,0:T(8,128)(2,1)}, bf16[1536,384]{1,0:T(8,128)(2,1)}, bf16[1536,384]{1,0:T(8,128)(2,1)}, bf16[1536,384]{1,0:T(8,128)(2,1)}) custom-call(bf16[8,384]{1,0:T(8,128)(2,1)} %fusion.8.refs_7_.refs_0_, bf16[8,1152]{1,0:T(8,128)(2,1)} %fusion.2.refs_8_.refs_1_, ...), custom_call_target="tpu_custom_call" | custom-call | tf_op jit(solution)/shard_map/condition_back/pallas_call | solution.py:945
  188.5 94.0 %reduce_gradients.1 = (f32[48,384]{1,0:T(8,128)}, f32[48,384]{1,0:T(8,128)}, f32[48,384]{1,0:T(8,128)}, f32[48,384]{1,0:T(8,128)}, f32[48,384]{1,0:T(8,128)}, /*...) custom-call(bf16[4,2,2,2,48,384]{5,4,3,2,1,0:T(8,128)(2,1)} %bitcast, ...), custom_call_target="tpu_custom_call" | custom-call | tf_op jit(solution)/shard_map/reduce_gradients/pallas_call | solution.py:801
  282.5 4.6 %adam.1 = (f32[48,656]{1,0:T(8,128)}, f32[48,656]{1,0:T(8,128)}, f32[48,656]{1,0:T(8,128)}, f32[48,1001]{1,0:T(8,128)}, f32[48,1001]{1,0:T(8,128)}, /*index=5*/f...) custom-call(f32[8,128]{1,0:T(8,128)} %get-tuple-element.147.refs_0_,, ...), custom_call_target="tpu_custom_call" | custom-call | tf_op jit(solution)/shard_map/adam/pallas_call | solution.py:1006
  287.1 1.3 reduce
  (8 shorter events, 0.1 us)
Async XLA Ops:
  151.5 27.9 %copy-start = (f32[4,8,384]{2,1,0:T(8,128)S(1)}, f32[4,8,384]{2,1,0:T(8,128)}, u32[]{:S(2)}) copy-start(f32[4,8,384]{2,1,0:T(8,128)} %get-tuple-element.130) | copy-start | bytes 147460

commit v2 on v1

--- a/solution.py
+++ b/solution.py
@@ -350,13 +350,8 @@
     in_specs = []
     args = list(entry_args)
     if last:
-        if isinstance(args[0], tuple):
-            layer = args[0][1]
-            in_specs.append(pl.BlockSpec((None, rows, D), lambda i: (layer, i, 0)))
-            args[0] = args[0][0]
-        else:
-            in_specs.append(lead_spec((rows, D), 2))
         in_specs += [
+            lead_spec((rows, D), 2),
             lead_spec((nb, 8, D), 3),
             whole_spec(args[2]),
             lead_spec((nb, PATCH_IN, tokens), 3),
@@ -367,15 +362,7 @@
     if first:
         in_specs += [lead_spec((nb, PATCH_IN, tokens), 3)]
     in_specs += [lead_spec((nb, 8, D), 3)] + [whole_spec(w) for w in weights]
-    for kept in saved:
-        if isinstance(kept, tuple):
-            array, layer = kept
-            in_specs.append(
-                pl.BlockSpec((None, rows, array.shape[2]), lambda i, layer=layer: (layer, i, 0))
-            )
-        else:
-            in_specs.append(lead_spec((rows, kept.shape[1]), 2))
-    saved = [kept[0] if isinstance(kept, tuple) else kept for kept in saved]
+    in_specs += [lead_spec((rows, s.shape[1]), 2) for s in saved]
     out_shape = []
     out_specs = []
 
@@ -1358,6 +1345,531 @@
     )(*args)
 
 
+LIMIT_B = 62 * 1024 * 1024
+
+
+def attend_backward(nb, tokens, qkv_ref, probs_ref, d_mix, d_qkv_s):
+    masks = half_masks()
+    lane = lax.broadcasted_iota(jnp.int32, (tokens, 2 * HEAD_DIM), 1)
+    low_side = lane < HEAD_DIM
+    root = HEAD_DIM**-0.5
+    for b in range(nb):
+        here = slice(b * tokens, (b + 1) * tokens)
+        for pair in range(HEADS // 2):
+            col = pair * 2 * HEAD_DIM
+            queries = qkv_ref[here, col : col + 2 * HEAD_DIM]
+            keys = stack_heads(qkv_ref[here, D + col : D + col + 2 * HEAD_DIM], masks)
+            values = stack_heads(qkv_ref[here, 2 * D + col : 2 * D + col + 2 * HEAD_DIM], masks)
+            d_out = d_mix[here, col : col + 2 * HEAD_DIM]
+            probs_bf = probs_ref[here, pair * 2 * tokens : (pair + 1) * 2 * tokens]
+            d_probs = dot_nt(d_out, values)
+            halves = []
+            for side in range(2):
+                cut = slice(side * tokens, (side + 1) * tokens)
+                probs = probs_bf[:, cut].astype(jnp.float32)
+                part = d_probs[:, cut]
+                halves.append((probs * (part - jnp.sum(probs * part, axis=-1, keepdims=True))).astype(BF))
+            d_scores = jnp.concatenate(halves, axis=1)
+            d_queries = dot_nn(d_scores, keys) * root
+            d_keys = dot_tn(d_scores, queries)
+            d_keys = jnp.where(low_side, d_keys[:tokens], d_keys[tokens:]) * root
+            d_values = dot_tn(probs_bf, d_out)
+            d_values = jnp.where(low_side, d_values[:tokens], d_values[tokens:])
+            d_qkv_s[here, col : col + 2 * HEAD_DIM] = d_queries.astype(BF)
+            d_qkv_s[here, D + col : D + col + 2 * HEAD_DIM] = d_keys.astype(BF)
+            d_qkv_s[here, 2 * D + col : 2 * D + col + 2 * HEAD_DIM] = d_values.astype(BF)
+
+
+def lane_sums(rows):
+    total = jnp.sum(rows, axis=0, keepdims=True)
+    return sum(total[:, at : at + 128] for at in range(0, total.shape[1], 128))
+
+
+def fused_backward_kernel(places, slots, layers, nb, tokens, lat_count, count_all, sizes, *refs):
+    small_rows, ada_rows, part_rows, wide_rows = sizes
+    chunks = slots + SPLIT + 3 * layers
+    steps = lat_count // nb
+    depth = len(places.dims)
+    rows = nb * tokens
+    given = refs[:chunks]
+    feat_ref, hot_ref, mods_ref, fmod_ref, pre_ref, cond_ref, square_ref = refs[chunks : chunks + 7]
+    (
+        clean_ref,
+        noise_ref,
+        noisy_ref,
+        start_ref,
+        result_ref,
+        qkv_ref,
+        probs_ref,
+        mixed_ref,
+        branch_ref,
+        middle_ref,
+        mlp_ref,
+        act_ref,
+        slope_ref,
+    ) = refs[chunks + 7 : chunks + 20]
+    refs = refs[chunks + 20 :]
+    outs, both_ref, stats_ref = refs[:chunks], refs[chunks], refs[chunks + 1]
+    refs = refs[chunks + 2 :]
+    fulls, accs = refs[:chunks], refs[chunks : 2 * chunks]
+    lands = refs[2 * chunks : (2 + depth) * chunks]
+    (
+        stage_attn,
+        stage_in,
+        stage_out,
+        acc_one,
+        acc_two,
+        d_stream_s,
+        d_qkv_s,
+        d_mods_s,
+        d_raw_s,
+        d_fmod_s,
+        d_patch_s,
+        d_head_s,
+        loss_s,
+        sum_s,
+        stats_s,
+        both_s,
+        stats_land,
+        send_sems,
+        recv_sems,
+        own_sems,
+        take_sems,
+        stats_send,
+        stats_recv,
+        both_send,
+        both_recv,
+    ) = refs[(2 + depth) * chunks :]
+    turn, h, n = (pl.program_id(axis) for axis in range(3))
+    mine = places.mine()
+    lead = slots + SPLIT
+
+    def flat(ref, count):
+        return ref.reshape(places.count * count, D)
+
+    takes = [pltpu.make_async_copy(given[m], fulls[m], take_sems.at[m]) for m in range(chunks)]
+    slot_refs = [f.reshape(-1, lax.axis_size("tp"), small_rows, D) for f in fulls[:slots]]
+    ada_refs = [flat(f, part_rows) for f in fulls[slots:lead]]
+    staged = {0: stage_attn, 1: stage_in, 2: stage_out}
+    order = [lead + 4, lead + 5, lead + 3, slots + 2, lead + 1, lead + 2, lead, 0, 1, slots, slots + 1]
+    traffic = Traffic(places, mine, send_sems, recv_sems, own_sems)
+    jobs = []
+    first_copies = []
+    for at, m in enumerate(order):
+        source = fulls[m] if m < lead else staged[(m - lead) % 3]
+        used = traffic.used
+        jobs.append(
+            reduce_job(
+                traffic, at % 2 == 1, source, accs[at], lands[at * depth : (at + 1) * depth], outs[m]
+            )
+        )
+        digit = places.order(at % 2 == 1)[-1]
+        first_copies.append(traffic.copies[used : used + places.dims[digit] - 1])
+
+    def run(*names):
+        for job, k in names:
+            jobs[job][k]()
+
+    def at_step(number):
+        layer_turn, rest = divmod(number, 2 * steps)
+        half, step = divmod(rest, steps)
+        return pl.when((turn == layer_turn) & (h == half) & (n == step))
+
+    def both(pair, k):
+        return [(job, k) for job in (2 * pair, 2 * pair + 1) if job < len(jobs)]
+
+    here = pl.ds(pl.multiple_of(n * rows, rows), rows)
+
+    def mod_of(layer):
+        return lambda part: mod_rows(mods_ref, (layer,), n, nb, part)
+
+    def put_mod(layer, part, value):
+        for b in range(nb):
+            d_mods_s[layer, pl.ds(n * nb + b, 1), part * D : (part + 1) * D] = value[b]
+
+    @at_step(0)
+    def _():
+        for m in [*range(slots), lead + 5, lead + 4, lead + 3, lead + 2, lead + 1, lead, *range(slots, lead)]:
+            takes[m].start()
+        d_mods_s[...] = jnp.zeros_like(d_mods_s)
+        d_fmod_s[...] = jnp.zeros_like(d_fmod_s)
+        d_patch_s[...] = jnp.zeros_like(d_patch_s)
+        d_head_s[...] = jnp.zeros_like(d_head_s)
+        loss_s[...] = jnp.zeros_like(loss_s)
+        sum_s[...] = jnp.zeros_like(sum_s)
+        places.barrier(mine)
+        for m in (*range(slots), lead + 5, lead + 4):
+            takes[m].wait()
+
+    hooks = {
+        steps: [],
+        steps + 1: both(0, 1),
+        2 * steps - 1: both(0, 2),
+        2 * steps + 1: both(0, 3) + both(1, 1),
+        3 * steps - 1: both(1, 2) + both(0, 4),
+        3 * steps + 1: both(1, 3) + both(2, 1),
+        4 * steps - 1: both(2, 2) + both(1, 4),
+    }
+    early_ada = [slots + p for p in range(SPLIT) if p * part_rows < (layers - 1) * ada_rows]
+    loads = {steps: [lead + 3], 2 * steps: [lead + 2, lead + 1], 3 * steps: [lead, *early_ada]}
+    for number in sorted(set(hooks) | set(loads)):
+
+        @at_step(number)
+        def _(number=number):
+            for m in loads.get(number, []):
+                takes[m].wait()
+            run(*hooks.get(number, []))
+
+    def spread(layer):
+        wide = places.count * part_rows
+        for l, col, p, at, length in modulation_pieces(layers, ada_rows, part_rows, places.count):
+            if l == layer:
+                d_raw_s[:, p * wide + at : p * wide + at + length] = d_mods_s[layer, :, col : col + length]
+
+    def finish_all():
+        run((6, 0))
+        cond = cond_ref[...]
+        pre = pre_ref[...]
+        cond_act = silu(cond).astype(BF)
+        cond_two = jnp.concatenate([cond_act, cond_act], axis=0)
+        spread(0)
+        wide = places.count * part_rows
+        d_cond = sum_s[...]
+        d_mods = {}
+        for p in range(SPLIT):
+            if p * part_rows < (layers - 1) * ada_rows:
+                d_mods[p] = split_low(d_raw_s[:, p * wide : (p + 1) * wide])
+                d_cond = d_cond + dot_nn(d_mods[p], ada_refs[p][...])
+        d_fmods = [split_low(d_fmod_s[:, k * D : (k + 1) * D]) for k in range(2)]
+        for k in range(2):
+            d_cond = d_cond + dot_nt(d_fmods[k], block_of(slot_refs, 5 + k))
+        run(*both(2, 3))
+        d_pre = split_low((d_cond[:8] + d_cond[8:]) * silu_slope(cond))
+        d_time = dot_nn(d_pre, block_of(slot_refs, 1))
+        d_time = split_low((d_time[:8] + d_time[8:]) * silu_slope(pre))
+        time_act = silu(pre).astype(BF)
+
+        def give(k, grad):
+            ref = slot_refs[k % slots]
+            ref[:, k // slots] = grad.astype(BF).reshape(ref.shape[0], ref.shape[2], D)
+
+        def twice(values):
+            return jnp.concatenate([values, values], axis=0)
+
+        def k_time():
+            grad = dot_tn(d_time, twice(feat_ref[...]))
+            corner = jnp.pad(d_patch_s[...], ((0, 128 - PATCH_IN), (0, 0))).T
+            return jnp.concatenate([grad[:, :128] + corner, grad[:, 128:]], axis=1)
+
+        def k_class(k):
+            grad = dot_tn(d_pre, twice(hot_ref[:, k * D : (k + 1) * D]))
+            if k == 2:
+                corner = jnp.pad(d_head_s[...], ((0, 128 - OUT), (0, 0))).T
+                grad = jnp.concatenate([grad[:, :256], grad[:, 256:] + corner], axis=1)
+            return grad
+
+        makers = {
+            0: k_time,
+            1: lambda: dot_tn(d_pre, twice(time_act)),
+            2: lambda: k_class(0),
+            3: lambda: k_class(1),
+            4: lambda: k_class(2),
+            5: lambda: dot_tn(cond_two, d_fmods[0]),
+            6: lambda: dot_tn(cond_two, d_fmods[1]),
+        }
+        for slot in range(slots):
+            for k in range(slot, SMALL, slots):
+                give(k, makers[k]() if k in makers else jnp.zeros((D, D), jnp.float32))
+            if slot == 0:
+                run((7, 0), (6, 1))
+        run((8, 0))
+        for p, d_mod in d_mods.items():
+            ada_refs[p][...] = dot_tn(d_mod, cond_two).astype(BF)
+        run((9, 0), (10, 0), (7, 1), (8, 1), (9, 1))
+        run(*both(2, 4), *both(3, 2), (10, 1), (8, 2), *both(3, 3), (9, 2), (10, 2), (8, 3))
+        run((9, 3), *both(3, 4), (8, 4))
+        inner = [d for d in reversed(range(depth)) if places.digits[d][0] == "tp"]
+        for s in range(slots):
+            both_s[(lax.axis_index("tp"), s)] = outs[s][...]
+
+        def both_stage(stage):
+            digit = inner[stage]
+            _, stride, size = places.digits[digit]
+            start = lax.axis_index("tp") // stride * stride
+            copies = []
+            for shift in range(1, size):
+                target, _ = places.other(mine, digit, shift)
+                where = both_s.at[pl.ds(start, stride)]
+                copies.append(
+                    pltpu.make_async_remote_copy(
+                        src_ref=where,
+                        dst_ref=where,
+                        send_sem=both_send.at[stage, shift - 1],
+                        recv_sem=both_recv.at[stage, shift - 1],
+                        device_id=target,
+                        device_id_type=MESH,
+                    )
+                )
+                copies[-1].start()
+            return copies
+
+        pending = both_stage(0)
+        run((10, 3), (9, 4))
+        for stage in range(1, len(inner)):
+            for copy in pending:
+                copy.wait()
+            pending = both_stage(stage)
+        run((10, 4))
+        grad = sum(lane_sums(out[...] * out[...]) for out in outs)
+        squares = [lane_sums(jnp.sum(square_ref[l], axis=0)) for l in range(layers)]
+        stats_s[...] = jnp.concatenate(
+            [grad, lane_sums(loss_s[...]), *squares, jnp.zeros((6 - layers, 128), jnp.float32)], axis=0
+        )
+        for stage, digit in enumerate(reversed(range(depth))):
+            size = places.dims[digit]
+            stats_land[stage, mine[digit]] = stats_s[...]
+            copies = []
+            for shift in range(1, size):
+                target, _ = places.other(mine, digit, shift)
+                copies.append(
+                    pltpu.make_async_remote_copy(
+                        src_ref=stats_s,
+                        dst_ref=stats_land.at[stage, mine[digit]],
+                        send_sem=stats_send.at[stage, shift - 1],
+                        recv_sem=stats_recv.at[stage, shift - 1],
+                        device_id=target,
+                        device_id_type=MESH,
+                    )
+                )
+                copies[-1].start()
+            for copy in copies:
+                copy.wait()
+            total = stats_land[stage, 0]
+            for value in range(1, size):
+                total = total + stats_land[stage, value]
+            stats_s[...] = total
+        stats_ref[...] = stats_s[...]
+        for copy in pending:
+            copy.wait()
+        both_ref[...] = both_s[...]
+        waited = {id(copy) for group in first_copies[:3] for copy in group}
+        for copy in traffic.copies:
+            if id(copy) not in waited:
+                copy.wait_send()
+
+    for layer in range(layers):
+        mod = mod_of(layer)
+        is_turn = turn == layers - 1 - layer
+        attn_w, in_w, out_w = (flat(fulls[lead + 3 * layer + k], wide_rows) for k in range(3))
+
+        @pl.when(is_turn & (h == 0))
+        def _(layer=layer, mod=mod, in_w=in_w, out_w=out_w):
+            @pl.when(n == 0)
+            def _():
+                acc_one[...] = jnp.zeros_like(acc_one)
+                acc_two[...] = jnp.zeros_like(acc_two)
+
+            if layer == layers - 1:
+                head = block_of(slot_refs, 4)[:, 256 : 256 + OUT]
+                fmod = lambda part: mod_rows(fmod_ref, (), n, nb, part)
+                hat, rstd = norm_rows(result_ref[0].reshape(nb, tokens, D))
+                final_in = (hat * (1.0 + fmod(1)) + fmod(0)).astype(BF)
+                d_parts = []
+                for b in range(nb):
+                    predicted = lax.dot_general(
+                        head, final_in[b], (((0,), (1,)), ((), ())), preferred_element_type=jnp.float32
+                    )
+                    errors = predicted - jnp.concatenate([noise_ref[b], clean_ref[b]], axis=0)
+                    loss_s[...] += jnp.sum((errors * errors).reshape(OUT // 8, 8, tokens), axis=0)
+                    d_pred = (errors * (2.0 / count_all)).astype(BF)
+                    d_head_s[...] += dot_nn(d_pred, final_in[b])
+                    d_parts.append(
+                        lax.dot_general(
+                            d_pred, head, (((0,), (1,)), ((), ())), preferred_element_type=jnp.float32
+                        )
+                    )
+                d_stream, d_shift, d_scale = norm_back(jnp.stack(d_parts, axis=0), hat, rstd, fmod(1))
+                for b in range(nb):
+                    d_fmod_s[pl.ds(n * nb + b, 1), :D] = d_shift[b]
+                    d_fmod_s[pl.ds(n * nb + b, 1), D:] = d_scale[b]
+            else:
+                d_stream = d_stream_s[here, :].reshape(nb, tokens, D)
+            mlp = mlp_ref[0].astype(jnp.float32).reshape(nb, tokens, D)
+            put_mod(layer, 5, jnp.sum(d_stream * mlp, axis=1, keepdims=True))
+            d_mlp = (d_stream * mod(5)).astype(BF).reshape(rows, D)
+            d_hidden = (dot_nt(d_mlp, out_w[...]) * slope_ref[0].astype(jnp.float32)).astype(BF)
+            acc_two[...] += dot_tn(act_ref[0], d_mlp)
+            hat, rstd = norm_rows(middle_ref[0].reshape(nb, tokens, D))
+            mlp_in = (hat * (1.0 + mod(4)) + mod(3)).astype(BF).reshape(rows, D)
+            acc_one[...] += dot_tn(d_hidden, mlp_in)
+            d_input = dot_nn(d_hidden, in_w[...]).reshape(nb, tokens, D)
+            d_middle, d_shift, d_scale = norm_back(d_input, hat, rstd, mod(4))
+            put_mod(layer, 3, d_shift)
+            put_mod(layer, 4, d_scale)
+            d_stream_s[here, :] = (d_middle + d_stream).reshape(rows, D)
+
+            @pl.when(n == steps - 1)
+            def _():
+                pair = 0 if layer == layers - 1 else 2
+                if pair:
+                    for copy in first_copies[0] + first_copies[1]:
+                        copy.wait_send()
+                flat(stage_in, wide_rows)[...] = acc_one[...].astype(BF)
+                flat(stage_out, wide_rows)[...] = acc_two[...].astype(BF)
+                run(*both(pair, 0))
+
+        @pl.when(is_turn & (h == 1))
+        def _(layer=layer, mod=mod, attn_w=attn_w):
+            @pl.when(n == 0)
+            def _():
+                acc_one[...] = jnp.zeros_like(acc_one)
+
+            d_middle = d_stream_s[here, :].reshape(nb, tokens, D)
+            branch = branch_ref[0].astype(jnp.float32).reshape(nb, tokens, D)
+            put_mod(layer, 2, jnp.sum(d_middle * branch, axis=1, keepdims=True))
+            d_proj = (d_middle * mod(2)).astype(BF).reshape(rows, D)
+            acc_one[3 * D :, :] += dot_tn(d_proj, mixed_ref[0])
+            d_mix = dot_nn(d_proj, attn_w[3 * D :, :]).astype(BF)
+            attend_backward(nb, tokens, qkv_ref.at[0], probs_ref.at[0], d_mix, d_qkv_s)
+            d_qkv = d_qkv_s[...]
+            stream = start_ref[...] if layer == 0 else result_ref[0]
+            hat, rstd = norm_rows(stream.reshape(nb, tokens, D))
+            attn_in = (hat * (1.0 + mod(1)) + mod(0)).astype(BF).reshape(rows, D)
+            acc_one[: 3 * D, :] += dot_tn(d_qkv, attn_in)
+            d_attn_in = dot_nn(d_qkv, attn_w[: 3 * D, :]).reshape(nb, tokens, D)
+            d_before, d_shift, d_scale = norm_back(d_attn_in, hat, rstd, mod(1))
+            put_mod(layer, 0, d_shift)
+            put_mod(layer, 1, d_scale)
+            d_prev = d_middle + d_before
+            if layer == 0:
+                for b in range(nb):
+                    d_patch_s[...] += lax.dot_general(
+                        noisy_ref[b].astype(jnp.float32),
+                        d_prev[b],
+                        (((1,), (0,)), ((), ())),
+                        precision=highest,
+                    )
+            else:
+                d_stream_s[here, :] = d_prev.reshape(rows, D)
+
+            @pl.when(n == steps - 1)
+            def _():
+                if layer == 0:
+                    for copy in first_copies[2]:
+                        copy.wait_send()
+                flat(stage_attn, wide_rows)[...] = acc_one[...].astype(BF)
+                if layer > 0:
+                    cond_act = silu(cond_ref[...]).astype(BF)
+                    cond_two = jnp.concatenate([cond_act, cond_act], axis=0)
+                    spread(layer)
+                    wide = places.count * part_rows
+                    for p in range(SPLIT):
+                        if p * part_rows >= layer * ada_rows:
+                            d_mod = split_low(d_raw_s[:, p * wide : (p + 1) * wide])
+                            takes[slots + p].wait()
+                            sum_s[...] += dot_nn(d_mod, ada_refs[p][...])
+                            ada_refs[p][...] = dot_tn(d_mod, cond_two).astype(BF)
+                    run(*both(1, 0))
+                else:
+                    finish_all()
+
+
+def fused_backward(places, slots, nb, count_all, given, feat, hot, mods, fmod, pre, cond, square, streams):
+    clean_t, noise_t, noisy, start, result, *kept = streams
+    layers = mods.shape[0]
+    lat_count, _, tokens = noisy.shape
+    total, rows, steps = lat_count * tokens, nb * tokens, lat_count // nb
+    chunks = len(given)
+    dims = places.dims
+    depth, widest = len(dims), max(dims)
+    block = given[0].shape[-2:]
+    last = steps - 1
+
+    def const_shape(shape):
+        return pl.BlockSpec(shape, lambda t, h, n: (0,) * len(shape))
+
+    def only(turn, half, before, after):
+        def pick(t, h, n):
+            at, phase = 2 * t + h, 2 * turn + half
+            return jnp.where(at == phase, n, jnp.where(at < phase, before, after))
+
+        return pick
+
+    def spec(block_shape, pick):
+        return pl.BlockSpec(block_shape, lambda t, h, n: (pick(t, h, n),) + (0,) * (len(block_shape) - 1))
+
+    def result_index(t, h, n):
+        head = (t == 0) & (h == 0)
+        body_step = (t == 0) & (h == 1)
+        return (jnp.where(head, 1, 0), jnp.where(head | body_step, n, last), 0)
+
+    def mlp_spec(cols):
+        return pl.BlockSpec(
+            (1, rows, cols), lambda t, h, n: (layers - 1 - t, jnp.where(h == 0, n, last), 0)
+        )
+
+    def attn_spec(cols):
+        return pl.BlockSpec((1, rows, cols), lambda t, h, n: (layers - 1 - t, jnp.where(h == 1, n, 0), 0))
+
+    consts = (feat, hot, mods, fmod, pre, cond, square)
+    in_specs = [pl.BlockSpec(memory_space=pl.ANY)] * chunks + [const_shape(a.shape) for a in consts]
+    in_specs += [spec((nb, PATCH_IN, tokens), only(0, 0, 0, last))] * 2
+    in_specs += [
+        spec((nb, PATCH_IN, tokens), only(1, 1, 0, last)),
+        spec((rows, D), only(1, 1, 0, last)),
+        pl.BlockSpec((1, rows, D), result_index),
+    ]
+    in_specs += [attn_spec(a.shape[2]) for a in kept[:4]] + [mlp_spec(a.shape[2]) for a in kept[4:]]
+    shared = (lax.axis_size("tp"), slots, *block)
+    out_shape = [jax.ShapeDtypeStruct(block, jnp.float32)] * chunks
+    out_shape += [jax.ShapeDtypeStruct(s, jnp.float32) for s in (shared, (8, 128))]
+    full = (*dims, *block)
+    lands = []
+    for at in range(chunks):
+        lands += [pltpu.VMEM(shape, BF) for shape in land_shapes(places, at % 2 == 1, block)]
+    f32 = jnp.float32
+    scratch = [pltpu.VMEM(full, BF)] * chunks + [pltpu.VMEM(dims[:-1] + block, BF)] * chunks + lands
+    scratch += [pltpu.VMEM(full, BF)] * 3
+    scratch += [
+        pltpu.VMEM(shape, kind)
+        for shape, kind in (
+            ((4 * D, D), f32),
+            ((4 * D, D), f32),
+            ((total, D), f32),
+            ((rows, 3 * D), BF),
+            (mods.shape, f32),
+            ((8, SPLIT * places.count * block[0]), f32),
+            ((8, 2 * D), f32),
+            ((PATCH_IN, D), f32),
+            ((OUT, D), f32),
+            ((8, tokens), f32),
+            ((16, D), f32),
+            ((8, 128), f32),
+            (shared, f32),
+            ((depth, widest, 8, 128), f32),
+        )
+    ]
+    dma = pltpu.SemaphoreType.DMA
+    count = chunks * copies_per_part(places)
+    scratch += [dma((count,)), dma((count,)), dma((chunks,)), dma((chunks,))]
+    scratch += [dma((depth, widest - 1))] * 4
+    sizes = (block[0], 6 * D // places.count, block[0], block[0])
+    return pl.pallas_call(
+        functools.partial(
+            fused_backward_kernel, places, slots, layers, nb, tokens, lat_count, count_all, sizes
+        ),
+        grid=(layers, 2, steps),
+        out_shape=out_shape,
+        in_specs=in_specs,
+        out_specs=[const_shape(s.shape) for s in out_shape],
+        scratch_shapes=scratch,
+        compiler_params=pltpu.CompilerParams(
+            collective_id=4, has_side_effects=True, vmem_limit_bytes=LIMIT_B
+        ),
+        name="backward_and_reduce",
+    )(*given, *consts, *streams)
+
+
 def position_table(grid_side, columns):
     quarter = columns // 4
     omegas = jnp.exp(-math.log(10000.0) * jnp.arange(quarter, dtype=jnp.float32) / quarter)
@@ -1475,23 +1987,20 @@
     fused = dp_rows == wide_rows == part_rows and dp_rows % 16 == 0 and len(places.dims) >= 4 and layers == 2
     if fused:
         outs = fused_forward(places, slots, nb, weights_in, feat, class_hot, noisy, pos)
-        gathered = [o.reshape((places.count,) + o.shape[-2:]) for o in outs[: slots + SPLIT + 3 * layers]]
-        mods_all, fmod_all, pre, cond, start, result, *kept, square = outs[slots + SPLIT + 3 * layers :]
+        chunks = slots + SPLIT + 3 * layers
+        mods, fmod, pre, cond, start, result, *kept, square = outs[chunks:]
+        streams = (clean_t, noise_t, noisy, start, result, *kept)
+        *summed, both, stats = fused_backward(
+            places, slots, nb, count_all, outs[:chunks], feat, class_hot, mods, fmod, pre, cond, square, streams
+        )
+        wide = summed[slots + SPLIT :]
     else:
         gathered = gather_all(places, slots, *weights_in)
-    slot_full = [to_slot(g) for g in gathered[:slots]]
-    ada_full = [whole_rows(g, part_rows) for g in gathered[slots : slots + SPLIT]]
-    block_full = [whole_rows(g, wide_rows) for g in gathered[slots + SPLIT :]]
-    weights = [tuple(block_full[3 * l : 3 * l + 3]) for l in range(layers)]
-
-    if fused:
-        mods = jnp.pad(mods_all[:, :lat_count].reshape(layers, lat_count, 6, D), ((0, 0), (0, 0), (0, 2), (0, 0)))
-        fmod = jnp.pad(fmod_all[:lat_count].reshape(lat_count, 2, D), ((0, 0), (0, 6), (0, 0)))
-        head = slot_full[4 % slots][:, 4 // slots].reshape(D, D)[:, 256 : 256 + OUT]
-        saved = [(start if l == 0 else (result, l - 1), *((k, l) for k in kept)) for l in range(layers)]
-        stream = (result, layers - 1)
-        squares = [square[l] for l in range(layers)]
-    else:
+        slot_full = [to_slot(g) for g in gathered[:slots]]
+        ada_full = [whole_rows(g, part_rows) for g in gathered[slots : slots + SPLIT]]
+        block_full = [whole_rows(g, wide_rows) for g in gathered[slots + SPLIT :]]
+        weights = [tuple(block_full[3 * l : 3 * l + 3]) for l in range(layers)]
+
         raw, fmod, pre, cond, patch_t, head = condition(feat, class_hot, slot_full, ada_full, lat_count)
         mods = raw[:lat_count].reshape(lat_count, SPLIT, places.count, part_rows).swapaxes(1, 2)
         mods = mods.reshape(lat_count, places.count, layers, ada_rows).transpose(2, 0, 1, 3)
@@ -1510,39 +2019,39 @@
             saved.append((stream, *outs[1:9]))
             stream = outs[0]
             squares.append(outs[9])
-    layer_grads = [None] * layers
-    d_mods = [None] * layers
-    d_stream = None
-    for l in reversed(range(layers)):
-        last, first = l == layers - 1, l == 0
-        entry_args = (stream, fmod, head, clean_t, noise_t) if last else (d_stream,)
-        if first:
-            entry_args = (*entry_args, noisy)
-        outs = list(backward_layer(first, last, entry_args, mods[l], weights[l], saved[l], nb, tokens, count_all))
-        if last:
-            loss_part, d_head_t, d_fmod = outs[:3]
-            outs = outs[3:]
-        if first:
-            d_patch = outs[0]
-        else:
-            d_stream = outs[0]
-        layer_grads[l] = outs[1:4]
-        d_mods[l] = outs[4]
-    d_raw = jnp.stack([d[:, :6] for d in d_mods]).reshape(layers, lat_count, places.count, ada_rows)
-    d_raw = d_raw.transpose(1, 2, 0, 3).reshape(lat_count, places.count, SPLIT, part_rows)
-    d_raw = d_raw.swapaxes(1, 2).reshape(lat_count, -1)
-    d_raw = jnp.pad(d_raw, ((0, 8 - lat_count), (0, 0)))
-    small_grads = condition_back(
-        feat, class_hot, slot_full, ada_full, pre, cond, d_raw, d_fmod, d_patch, d_head_t
-    )
-    grads = [from_slot(g) for g in small_grads[:slots]]
-    grads += [pad_rows(g.reshape(places.count, part_rows, D)) for g in small_grads[slots:]]
-    for l in reversed(range(layers)):
-        for k in range(3):
-            grads.append(pad_rows(layer_grads[l][k].reshape(places.count, wide_rows, D)))
-    *summed, both, stats = reduce_all(places, slots, grads, loss_part, squares)
-    wide = summed[slots + SPLIT :]
-    wide = [wide[3 * (layers - 1 - l) + k] for l in range(layers) for k in range(3)]
+        layer_grads = [None] * layers
+        d_mods = [None] * layers
+        d_stream = None
+        for l in reversed(range(layers)):
+            last, first = l == layers - 1, l == 0
+            entry_args = (stream, fmod, head, clean_t, noise_t) if last else (d_stream,)
+            if first:
+                entry_args = (*entry_args, noisy)
+            outs = list(backward_layer(first, last, entry_args, mods[l], weights[l], saved[l], nb, tokens, count_all))
+            if last:
+                loss_part, d_head_t, d_fmod = outs[:3]
+                outs = outs[3:]
+            if first:
+                d_patch = outs[0]
+            else:
+                d_stream = outs[0]
+            layer_grads[l] = outs[1:4]
+            d_mods[l] = outs[4]
+        d_raw = jnp.stack([d[:, :6] for d in d_mods]).reshape(layers, lat_count, places.count, ada_rows)
+        d_raw = d_raw.transpose(1, 2, 0, 3).reshape(lat_count, places.count, SPLIT, part_rows)
+        d_raw = d_raw.swapaxes(1, 2).reshape(lat_count, -1)
+        d_raw = jnp.pad(d_raw, ((0, 8 - lat_count), (0, 0)))
+        small_grads = condition_back(
+            feat, class_hot, slot_full, ada_full, pre, cond, d_raw, d_fmod, d_patch, d_head_t
+        )
+        grads = [from_slot(g) for g in small_grads[:slots]]
+        grads += [pad_rows(g.reshape(places.count, part_rows, D)) for g in small_grads[slots:]]
+        for l in reversed(range(layers)):
+            for k in range(3):
+                grads.append(pad_rows(layer_grads[l][k].reshape(places.count, wide_rows, D)))
+        *summed, both, stats = reduce_all(places, slots, grads, loss_part, squares)
+        wide = summed[slots + SPLIT :]
+        wide = [wide[3 * (layers - 1 - l) + k] for l in range(layers) for k in range(3)]
     states = []
     for shape_it, triple in (
         (swap, (entry_weight, entry_first, entry_second)),

time: 289 us -> 244 us (0.84)
  Pallas kernels: 271 us -> 235 us
  local copies, waits for them, and re-layouts: 8.25 us -> 0.01 us
    pallas_call x4 -> x1, Pallas kernels: 159 us -> 123 us  [fused_backward(): pl.pallas_call(functools.partial(fused_backward_kernel, places, slots, la...]
    slice x4 -> x0, local copies, waits for them, and re-layouts: 3.3 us -> none  [the longest x2 1.64 us: body(): head = slot_full[4 % slots][:, 4 // slots].reshape(D, D)[:, 256:256 + OUT]]
where the time goes in v2:
time: 244 us
  Pallas kernels  235 us (96%)
  other arithmetic  8.37 us (3%)
    pallas_call x1, Pallas kernels, fused_backward(): pl.pallas_call(functools.partial(fused_backward_kernel, places, slots, la...  123 us
    pallas_call x1, Pallas kernels, fused_forward(): pl.pallas_call(functools.partial(fused_forward_kernel, places, slots, lay...  108 us

profile of v2, /device:TPU:0, one launch (start us, length us, event | category | flops | bytes accessed | tf_op | source)
XLA Modules:
  0.0 244.2 jit_solution(14134663958575409308)
XLA Ops:
  0.7 0.7 compare_select_fusion
  1.3 0.7 convert_element_type.31
  2.0 0.1 fusion.8
  2.1 0.7 fusion.15
  2.8 0.7 fusion.6.refs_7_.refs_11_
  3.5 0.7 fusion.refs_8_.refs_12_
  4.2 1.6 add_convert_fusion.refs_9_.refs_20_
  5.8 1.0 multiply_sine_fusion.1
  6.8 1.0 pad_maximum_fusion.refs_10_
  7.8 107.8 %gather_and_forward.1 = (bf16[4,2,2,2,48,384]{5,4,3,2,1,0:T(8,128)(2,1)}, bf16[4,2,2,2,48,384]{5,4,3,2,1,0:T(8,128)(2,1)}, bf16[4,2,2,2,48,384]{5,4,3,2,1,0:T(8,...) custom-call(f32[48,656]{1,0:T(8,128)} %bitcast.52, ...), custom_call_target="tpu_custom_call" | custom-call | tf_op jit(solution)/shard_map/gather_and_forward/pallas_call | solution.py:1315
  115.5 122.7 %backward_and_reduce.1 = (f32[48,384]{1,0:T(8,128)}, f32[48,384]{1,0:T(8,128)}, f32[48,384]{1,0:T(8,128)}, f32[48,384]{1,0:T(8,128)}, f32[48,384]{1,0:T(8,128)},...) custom-call(bf16[4,2,2,2,48,384]{5,4,3,2,1,0:T(8,128)(2,1)} %get-tup, ...), custom_call_target="tpu_custom_call" | custom-call | tf_op jit(solution)/shard_map/backward_and_reduce/pallas_call | solution.py:1857
  238.3 4.6 %adam.1 = (f32[48,656]{1,0:T(8,128)}, f32[48,656]{1,0:T(8,128)}, f32[48,656]{1,0:T(8,128)}, f32[48,1001]{1,0:T(8,128)}, f32[48,1001]{1,0:T(8,128)}, /*index=5*/f...) custom-call(f32[8,128]{1,0:T(8,128)} %get-tuple-element.111.refs_0_,, ...), custom_call_target="tpu_custom_call" | custom-call | tf_op jit(solution)/shard_map/adam/pallas_call | solution.py:993
  242.9 1.3 reduce
  (4 shorter events, 0.0 us)

commit v3 on v2

--- a/solution.py
+++ b/solution.py
@@ -3,6 +3,7 @@
 
 import jax
 import jax.numpy as jnp
+import numpy as np
 from jax import lax
 from jax.experimental import pallas as pl
 from jax.experimental.pallas import tpu as pltpu
@@ -1001,6 +1002,63 @@
     )(*args)
 
 
+def fused_adam_kernel(layers, count_rms, *refs):
+    stats_ref, both_ref, early_ref, late_ref, class_ref, ada_ref, patch_ref = refs[:7]
+    grads = refs[7 : 7 + 3 * layers]
+    states = refs[7 + 3 * layers :][:21]
+    outs = refs[7 + 3 * layers + 21 :]
+    news, (loss_ref, norm_ref, rms_ref) = outs[:21], outs[21:]
+    totals = jnp.sum(stats_ref[...], axis=1, keepdims=True)
+    norm = jnp.sqrt(totals[0:1])
+    factor = jnp.minimum(1.0, 0.01 / (norm + 1e-06))
+    loss_ref[...] = totals[1:2]
+    norm_ref[...] = norm
+    rms = jnp.sqrt(totals / count_rms)
+    rms_ref[...] = jnp.concatenate([rms[2 + l : 3 + l] for l in range(layers)], axis=1)
+    correct = 1.0 - 0.5**STEP
+
+    def update(name, where, grad):
+        weight, first, second = (ref[where] for ref in states[3 * name : 3 * name + 3])
+        clipped = grad * factor
+        first_new = 0.5 * first + 0.5 * clipped
+        second_new = 0.5 * second + 0.5 * clipped * clipped
+        root = jnp.sqrt(second_new * (1.0 / correct)) + 1e-08
+        new = weight - 0.02 * (first_new * (1.0 / correct) / root + 0.01 * weight)
+        news[3 * name][where] = new
+        news[3 * name + 1][where] = first_new
+        news[3 * name + 2][where] = second_new
+
+    rows = states[0].shape[0]
+    early = PATCH_IN + FREQ
+    every = slice(0, rows)
+    patch = patch_ref[...].T[:rows, :PATCH_IN]
+    update(0, (every, slice(0, PATCH_IN)), patch)
+    update(0, (every, slice(PATCH_IN, early)), early_ref[:, PATCH_IN:early])
+    update(0, (every, slice(early, early + D)), late_ref[...])
+    update(1, (every, slice(0, CLASSES + 1)), class_ref[:, : CLASSES + 1])
+    update(6, (every, slice(0, D)), both_ref[1])
+    update(6, (every, slice(D, 2 * D)), both_ref[2])
+    update(6, (every, slice(2 * D, 2 * D + OUT)), both_ref[0][:, :OUT])
+    update(5, (slice(0, states[15].shape[0]), slice(0, D)), ada_ref[...])
+    for l in range(layers):
+        for k in range(3):
+            update(2 + k, (l, slice(0, states[6].shape[1]), slice(0, D)), grads[3 * l + k][: states[6].shape[1]])
+
+
+def fused_adam(layers, count_rms, small, grads, states):
+    vmem = pl.BlockSpec(memory_space=pltpu.VMEM)
+    args = (*small, *grads, *states)
+    return pl.pallas_call(
+        functools.partial(fused_adam_kernel, layers, count_rms),
+        out_shape=[jax.ShapeDtypeStruct(s.shape, jnp.float32) for s in states]
+        + [jax.ShapeDtypeStruct((1, n), jnp.float32) for n in (1, 1, layers)],
+        in_specs=[vmem] * len(args),
+        out_specs=[vmem] * 24,
+        compiler_params=pltpu.CompilerParams(vmem_limit_bytes=LIMIT),
+        name="adam_update",
+    )(*args)
+
+
 def modulation_pieces(layers, ada_rows, part_rows, count):
     pieces = []
     for j in range(count):
@@ -1014,14 +1072,40 @@
     return pieces
 
 
-def embed_condition(slots, lat_count, feat_ref, hot_ref, slot_refs, pre_ref, cond_ref, fmod_ref):
-    pre = dot_nt(feat_ref[...], block_of(slot_refs, 0))
+def class_of(labels_ref, drops_ref, b):
+    return jnp.where(drops_ref[b] == 1, CLASSES, labels_ref[b])
+
+
+def embed_inputs(lat_count, times_ref, labels_ref, drops_ref, freq_ref, feat_s, hot_s, fact_s):
+    feat_s[...] = jnp.zeros_like(feat_s)
+    hot_s[...] = jnp.zeros_like(hot_s)
+    fact_s[...] = jnp.zeros_like(fact_s)
+    column = lax.broadcasted_iota(jnp.int32, (1, 3 * D), 1)
+    half = FREQ // 2
+    for b in range(lat_count):
+        angles = times_ref[b].astype(jnp.float32) * freq_ref[...]
+        feat_s[b : b + 1, PATCH_IN : PATCH_IN + half] = jnp.cos(angles)
+        feat_s[b : b + 1, PATCH_IN + half : PATCH_IN + FREQ] = jnp.sin(angles)
+        label = class_of(labels_ref, drops_ref, b)
+        hot_s[b : b + 1, :] = jnp.where(column == label, 1.0, 0.0)
+        low = lax.rem(label, 32)
+        high = (label - low) // 32
+        fact_s[12 + b : 13 + b, :128] = jnp.full((1, 128), low, jnp.int32).astype(jnp.float32)
+        fact_s[12 + b : 13 + b, 128:256] = jnp.full((1, 128), high, jnp.int32).astype(jnp.float32)
+    fact_s[8 : 8 + lat_count, :] = feat_s[:lat_count, :]
+
+
+def embed_condition(lat_count, feat_s, hot_s, fact_s, slot_refs, pre_ref, cond_ref, fmod_ref):
+    pre = dot_nt(feat_s[...].astype(BF), block_of(slot_refs, 0))
     pre_ref[...] = pre
-    cond = dot_nt(silu(pre).astype(BF), block_of(slot_refs, 1))
+    time_act = silu(pre).astype(BF)
+    cond = dot_nt(time_act, block_of(slot_refs, 1))
     for k in range(3):
-        cond = cond + dot_nt(hot_ref[:, k * D : (k + 1) * D], block_of(slot_refs, 2 + k))
+        cond = cond + dot_nt(hot_s[:, k * D : (k + 1) * D].astype(BF), block_of(slot_refs, 2 + k))
     cond_ref[...] = cond
     act = silu(cond).astype(BF)
+    fact_s[:lat_count, :] = act.astype(jnp.float32)[:lat_count]
+    fact_s[4 : 4 + lat_count, :] = time_act.astype(jnp.float32)[:lat_count]
     for k in range(2):
         fmod_ref[:, k * D : (k + 1) * D] = dot_nn(act, block_of(slot_refs, 5 + k))
 
@@ -1078,28 +1162,66 @@
     return middle + mod(5) * mlp.reshape(nb, tokens, D)
 
 
-def waves(jobs):
-    pairs = [jobs[at : at + 2] for at in range(0, len(jobs), 2)]
-    depth = len(jobs[0])
-    ticks = []
-    for tick in range(len(pairs) + depth - 1):
-        ticks.append(
-            [job[k] for k in range(depth) if 0 <= tick - k < len(pairs) for job in pairs[tick - k]]
-        )
-    return ticks
+def fixed_tables(tokens):
+    half, quarter = FREQ // 2, D // 4
+    freq = np.exp(np.float32(-math.log(10000.0)) * np.arange(half, dtype=np.float32) / np.float32(half))
+    omegas = np.exp(np.float32(-math.log(10000.0)) * np.arange(quarter, dtype=np.float32) / np.float32(quarter))
+    token = np.arange(tokens)
+    row = (token // GRID).astype(np.float32)[:, None] * omegas
+    col = (token % GRID).astype(np.float32)[:, None] * omegas
+    table = np.concatenate([np.sin(row), np.cos(row), np.sin(col), np.cos(col)], axis=-1)
+    return jnp.asarray(freq[None], jnp.float32), jnp.asarray(table, jnp.float32)
+
+
+PROLOGUE = [
+    (0, 1),
+    (2, 0),
+    (1, 1),
+    (0, 2),
+    (3, 0),
+    (2, 1),
+    (1, 2),
+    (0, 3),
+    (4, 0),
+    (3, 1),
+    (2, 2),
+    (1, 3),
+    (0, 4),
+    "cond",
+    (5, 0),
+    (4, 1),
+    (3, 2),
+    (2, 3),
+    (1, 4),
+    "mods",
+    (5, 1),
+    (4, 2),
+    (3, 3),
+    (2, 4),
+]
+LATER = {
+    1: [(6, 0)],
+    3: [(6, 1)],
+    4: [(5, 2), (4, 3), (3, 4)],
+    6: [(6, 2)],
+    8: [(5, 3), (4, 4), "mods", (6, 3)],
+    12: [(5, 4), (6, 4), "hand"],
+}
 
 
 def fused_forward_kernel(places, slots, layers, nb, tokens, lat_count, sizes, *refs):
     small_rows, ada_rows, part_rows, wide_rows = sizes
     chunks = slots + SPLIT + 3 * layers
     entry_ref, table_ref, final_ref, ada_ref, attn_ref, in_ref, out_ref = refs[:7]
-    feat_ref, hot_ref, noisy_ref, pos_ref = refs[7:11]
-    given = refs[11 : 11 + chunks]
+    times_ref, labels_ref, drops_ref, freq_ref, clean_ref, noise_ref, pos_ref = refs[7:14]
+    refs = refs[14:]
+    given = refs[: chunks + 1]
     (
         mods_ref,
         fmod_ref,
         pre_ref,
         cond_ref,
+        noisy_ref,
         start_ref,
         result_ref,
         qkv_ref,
@@ -1111,10 +1233,23 @@
         act_ref,
         slope_ref,
         square_ref,
-    ) = refs[11 + chunks : 26 + chunks]
-    refs = refs[26 + chunks :]
-    fulls = refs[:chunks]
-    small, packed, stream_s, middle_s, send_sems, recv_sems, own_sems, give_sems = refs[chunks:]
+    ) = refs[chunks + 1 : chunks + 17]
+    refs = refs[chunks + 17 :]
+    fulls = refs[: chunks + 1]
+    (
+        small,
+        packed,
+        stream_s,
+        middle_s,
+        feat_s,
+        hot_s,
+        fact_s,
+        fact_bf,
+        send_sems,
+        recv_sems,
+        own_sems,
+        give_sems,
+    ) = refs[chunks + 1 :]
     l, h, n = (pl.program_id(axis) for axis in range(3))
     mine = places.mine()
     first = lax.axis_index("tp") * slots
@@ -1123,18 +1258,17 @@
     sources = [small.at[first + s] for s in range(slots)] + [packed.at[m] for m in range(SPLIT + 3 * layers)]
     traffic = Traffic(places, mine, send_sems, recv_sems, own_sems)
     jobs = [gather_job(traffic, at % 2 == 1, sources[m], fulls[m]) for at, m in enumerate(order)]
-    ticks = waves(jobs)
-    handed = [
-        pltpu.make_async_copy(fulls[m], given[m], give_sems.at[m]) for m in range(chunks)
-    ]
+    pairs = [jobs[at : at + 2] for at in range(0, chunks, 2)]
+    pairs.append([gather_job(traffic, False, fact_bf, fulls[chunks])])
+    handed = [pltpu.make_async_copy(fulls[m], given[m], give_sems.at[m]) for m in range(chunks + 1)]
 
     def flat(m, rows):
         return fulls[m].reshape(places.count * rows, D)
 
-    def run(numbers):
-        for tick in numbers:
-            for action in ticks[tick]:
-                action()
+    def run(*names):
+        for pair, k in names:
+            for job in pairs[pair]:
+                job[k]()
 
     def at_step(layer, half, step):
         return pl.when((l == layer) & (h == half) & (n == step))
@@ -1149,39 +1283,49 @@
                 mods_ref[layer, :, col : col + length] = raw[p][:, at : at + length]
 
     slot_refs = [f.reshape(-1, lax.axis_size("tp"), small_rows, D) for f in fulls[:slots]]
-    last = len(ticks) - 1
+
+    def pack_blocks():
+        for ll in range(layers):
+            for k, source in enumerate((attn_ref, in_ref, out_ref)):
+                packed[SPLIT + 3 * ll + k] = source[ll].astype(BF)
 
     @at_step(0, 0, 0)
     def _():
         small[...] = jnp.zeros_like(small)
         for k, at, source, low, high in small_blocks(entry_ref, table_ref, final_ref):
             small[k, : source.shape[0], at : at + high - low] = source[:, low:high].astype(BF)
+        places.barrier(mine)
+        run((0, 0))
         for p in range(SPLIT):
             packed[p] = ada_ref[p * part_rows : (p + 1) * part_rows, :].astype(BF)
-        for ll in range(layers):
-            for k, source in enumerate((attn_ref, in_ref, out_ref)):
-                packed[SPLIT + 3 * ll + k] = source[ll].astype(BF)
-        places.barrier(mine)
-        run(range(6))
-        embed_condition(slots, lat_count, feat_ref, hot_ref, slot_refs, pre_ref, cond_ref, fmod_ref)
-        set_mods(0)
-        run([6])
-
-    @at_step(0, 1, 0)
-    def _():
-        run([7])
-
-    @at_step(1, 0, 0)
-    def _():
-        run([8])
-        for layer in range(1, layers):
-            set_mods(layer)
-
-    @at_step(1, 1, 0)
-    def _():
-        run(range(9, last + 1))
-        for copy in handed:
-            copy.start()
+        run((1, 0))
+        pack_blocks()
+        embed_inputs(lat_count, times_ref, labels_ref, drops_ref, freq_ref, feat_s, hot_s, fact_s)
+        for entry in PROLOGUE:
+            if entry == "cond":
+                embed_condition(lat_count, feat_s, hot_s, fact_s, slot_refs, pre_ref, cond_ref, fmod_ref)
+                fact_bf[...] = fact_s[...].astype(BF)
+            elif entry == "mods":
+                set_mods(0)
+            else:
+                run(entry)
+
+    steps = lat_count // nb
+    for number, names in sorted(LATER.items()):
+        number = number * steps // 4
+        layer_at, rest = divmod(number, 2 * steps)
+
+        @at_step(layer_at, rest // steps, rest % steps)
+        def _(names=names):
+            for entry in names:
+                if entry == "mods":
+                    for layer in range(1, layers):
+                        set_mods(layer)
+                elif entry == "hand":
+                    for copy in handed:
+                        copy.start()
+                else:
+                    run(entry)
 
     rows = nb * tokens
     here = pl.ds(pl.multiple_of(n * rows, rows), rows)
@@ -1196,6 +1340,10 @@
         def _(layer=layer, mod=mod):
             if layer == 0:
                 patch = block_of(slot_refs, 0)[:, :PATCH_IN]
+                for b in range(nb):
+                    when = jnp.full((1, tokens), times_ref[n * nb + b], jnp.int32).astype(jnp.float32)
+                    phase = (when / NOISE_STEPS + 0.008) / 1.008 * (math.pi / 2)
+                    noisy_ref[b] = (jnp.cos(phase) * clean_ref[b] + jnp.sin(phase) * noise_ref[b]).astype(BF)
                 parts = [
                     lax.dot_general(
                         noisy_ref[b], patch, (((0,), (1,)), ((), ())), preferred_element_type=jnp.float32
@@ -1249,16 +1397,16 @@
         traffic.finish()
 
 
-def fused_forward(places, slots, nb, weights_in, feat, hot, noisy, pos):
+def fused_forward(places, slots, nb, weights_in, ids, clean_t, noise_t):
     entry_t, table_t, final, ada_t, attn_t, in_t, out_w = weights_in
     layers, wide_rows = attn_t.shape[:2]
-    lat_count, _, tokens = noisy.shape
+    lat_count, _, tokens = clean_t.shape
     small_rows, part_rows, ada_rows = final.shape[0], ada_t.shape[0] // SPLIT, ada_t.shape[0] // layers
     sizes = [small_rows] * slots + [part_rows] * SPLIT + [wide_rows] * (3 * layers)
     chunks = len(sizes)
     steps = lat_count // nb
     rows, total = nb * tokens, lat_count * tokens
-    full_shapes = [(*places.dims, r, D) for r in sizes]
+    full_shapes = [(*places.dims, r, D) for r in (*sizes, 16)]
 
     def const(array):
         return pl.BlockSpec(array.shape, lambda l, h, n: (0,) * array.ndim)
@@ -1284,7 +1432,7 @@
         return (jnp.where(h == 0, jnp.maximum(l - 1, 0), l), jnp.where(h == 0, before, n), 0, 0)
 
     out_shape = [jax.ShapeDtypeStruct(s, BF) for s in full_shapes]
-    out_specs = [pl.BlockSpec(memory_space=pl.ANY)] * chunks
+    out_specs = [pl.BlockSpec(memory_space=pl.ANY)] * (chunks + 1)
 
     def add(shape, kind, spec):
         out_shape.append(jax.ShapeDtypeStruct(shape, kind))
@@ -1292,26 +1440,23 @@
 
     for shape in ((layers, 8, 6 * D), (8, 2 * D), (8, D), (8, D)):
         add(shape, jnp.float32, const_shape(shape))
-    add(
-        (total, D),
-        jnp.float32,
-        pl.BlockSpec((rows, D), lambda l, h, n: (jnp.where((l == 0) & (h == 0), n, steps - 1), 0)),
-    )
+    def opening(l, h, n):
+        return jnp.where((l == 0) & (h == 0), n, steps - 1)
+
+    latents = pl.BlockSpec((nb, PATCH_IN, tokens), lambda l, h, n: (opening(l, h, n), 0, 0))
+    add((lat_count, PATCH_IN, tokens), BF, latents)
+    add((total, D), jnp.float32, pl.BlockSpec((rows, D), lambda l, h, n: (opening(l, h, n), 0)))
     add((layers, total, D), jnp.float32, half_two(D))
     for cols, kind in ((3 * D, BF), (HEADS * tokens, BF), (D, BF), (D, BF), (D, jnp.float32)):
         add((layers, total, cols), kind, half_one(cols))
     for cols in (D, 4 * D, 4 * D):
         add((layers, total, cols), BF, half_two(cols))
     add((layers, steps, 8, D), jnp.float32, pl.BlockSpec((1, 1, 8, D), square_index))
-    args = (*weights_in, feat, hot, noisy, pos)
-    in_specs = [const(a) for a in args[:-2]]
-    in_specs.append(
-        pl.BlockSpec(
-            (nb, PATCH_IN, tokens), lambda l, h, n: (jnp.where((l == 0) & (h == 0), n, steps - 1), 0, 0)
-        )
-    )
-    in_specs.append(const(pos))
-    count = chunks * copies_per_part(places)
+    freq, pos = fixed_tables(tokens)
+    args = (*weights_in, *ids, freq, clean_t, noise_t, pos)
+    in_specs = [const(a) for a in weights_in]
+    in_specs += [pl.BlockSpec(memory_space=pltpu.SMEM)] * 3 + [const(freq), latents, latents, const(pos)]
+    count = (chunks + 1) * copies_per_part(places)
     return pl.pallas_call(
         functools.partial(
             fused_forward_kernel,
@@ -1333,10 +1478,14 @@
             pltpu.VMEM((SPLIT + 3 * layers, wide_rows, D), BF),
             pltpu.VMEM((total, D), jnp.float32),
             pltpu.VMEM((total, D), jnp.float32),
+            pltpu.VMEM((8, D), jnp.float32),
+            pltpu.VMEM((8, 3 * D), jnp.float32),
+            pltpu.VMEM((16, D), jnp.float32),
+            pltpu.VMEM((16, D), BF),
             pltpu.SemaphoreType.DMA((count,)),
             pltpu.SemaphoreType.DMA((count,)),
-            pltpu.SemaphoreType.DMA((chunks,)),
-            pltpu.SemaphoreType.DMA((chunks,)),
+            pltpu.SemaphoreType.DMA((chunks + 1,)),
+            pltpu.SemaphoreType.DMA((chunks + 1,)),
         ],
         compiler_params=pltpu.CompilerParams(
             collective_id=3, has_side_effects=True, vmem_limit_bytes=LIMIT
@@ -1346,6 +1495,64 @@
 
 
 LIMIT_B = 62 * 1024 * 1024
+
+LATER_BACK = {
+    5: [(0, 1)],
+    7: [(0, 2)],
+    9: [(0, 3), (1, 1), (7, 1)],
+    11: [(1, 2), (0, 4), (7, 2)],
+    13: [(1, 3), (2, 1), (7, 3)],
+    14: [(1, 4), (7, 4)],
+    15: [(2, 2)],
+}
+SHARES = {14: 0, 15: 1}
+TAIL_ONE = [(3, 1), (6, 1), (4, 1)]
+TAIL_TWO = [
+    (5, 0),
+    (2, 3),
+    (3, 2),
+    (6, 2),
+    (5, 1),
+    (4, 2),
+    (3, 3),
+    (6, 3),
+    (5, 2),
+    (4, 3),
+    (2, 4),
+    (5, 3),
+    (6, 4),
+    "ada",
+    (5, 4),
+    "small",
+    "share",
+    (4, 4),
+    (3, 4),
+]
+
+
+def exchange_job(traffic, bufs):
+    places, mine = traffic.places, traffic.mine
+    depth = len(places.dims)
+    stages = []
+    for k, digit in enumerate(reversed(range(depth))):
+        copies = []
+        for shift in range(1, places.dims[digit]):
+            there = tuple(traffic.ahead(digit, shift) if d == digit else slice(None) for d in range(depth))
+            here = tuple(mine[d] if d == digit else slice(None) for d in range(depth))
+            copies.append(traffic.remote(bufs[k].at[there], bufs[k + 1].at[here], digit, shift))
+        stages.append((copies, here))
+
+    def action(k):
+        if k > 0:
+            for copy in stages[k - 1][0]:
+                copy.wait_recv()
+        if k < depth:
+            copies, here = stages[k]
+            for copy in copies:
+                copy.start()
+            bufs[k + 1][here] = bufs[k][here]
+
+    return [functools.partial(action, k) for k in range(depth + 1)]
 
 
 def attend_backward(nb, tokens, qkv_ref, probs_ref, d_mix, d_qkv_s):
@@ -1391,8 +1598,9 @@
     steps = lat_count // nb
     depth = len(places.dims)
     rows = nb * tokens
-    given = refs[:chunks]
-    feat_ref, hot_ref, mods_ref, fmod_ref, pre_ref, cond_ref, square_ref = refs[chunks : chunks + 7]
+    given = refs[: chunks + 1]
+    refs = refs[1:]
+    mods_ref, fmod_ref, pre_ref, cond_ref, square_ref = refs[chunks : chunks + 5]
     (
         clean_ref,
         noise_ref,
@@ -1407,13 +1615,24 @@
         mlp_ref,
         act_ref,
         slope_ref,
-    ) = refs[chunks + 7 : chunks + 20]
-    refs = refs[chunks + 20 :]
-    outs, both_ref, stats_ref = refs[:chunks], refs[chunks], refs[chunks + 1]
-    refs = refs[chunks + 2 :]
-    fulls, accs = refs[:chunks], refs[chunks : 2 * chunks]
-    lands = refs[2 * chunks : (2 + depth) * chunks]
+    ) = refs[chunks + 5 : chunks + 18]
+    refs = refs[chunks + 18 :]
+    count = 3 * layers + 2
+    outs = refs[: count - 1]
+    both_ref, early_ref, late_ref, class_ref, ada_grad_ref, stats_ref = refs[count - 1 : count + 5]
+    refs = refs[count + 5 :]
+    fulls = refs[: chunks + 1]
+    refs = refs[chunks + 1 :]
+    accs = refs[:count]
+    lands = refs[count : (1 + depth) * count]
     (
+        *swaps,
+        wide_s,
+        small_s,
+        patch_s,
+        small_out,
+        mine_s,
+        all_s,
         stage_attn,
         stage_in,
         stage_out,
@@ -1439,7 +1658,7 @@
         stats_recv,
         both_send,
         both_recv,
-    ) = refs[(2 + depth) * chunks :]
+    ) = refs[(1 + depth) * count :]
     turn, h, n = (pl.program_id(axis) for axis in range(3))
     mine = places.mine()
     lead = slots + SPLIT
@@ -1447,24 +1666,60 @@
     def flat(ref, count):
         return ref.reshape(places.count * count, D)
 
-    takes = [pltpu.make_async_copy(given[m], fulls[m], take_sems.at[m]) for m in range(chunks)]
+    takes = [pltpu.make_async_copy(given[m], fulls[m], take_sems.at[m]) for m in range(chunks + 1)]
     slot_refs = [f.reshape(-1, lax.axis_size("tp"), small_rows, D) for f in fulls[:slots]]
     ada_refs = [flat(f, part_rows) for f in fulls[slots:lead]]
     staged = {0: stage_attn, 1: stage_in, 2: stage_out}
-    order = [lead + 4, lead + 5, lead + 3, slots + 2, lead + 1, lead + 2, lead, 0, 1, slots, slots + 1]
+    order = [lead + 4, lead + 5, lead + 3, lead + 1, lead + 2, lead]
+    sources = [staged[(m - lead) % 3] for m in order] + [patch_s]
+    targets = [outs[m - lead] for m in order] + [outs[count - 2]]
+    sources.insert(3, small_s)
+    targets.insert(3, small_out)
     traffic = Traffic(places, mine, send_sems, recv_sems, own_sems)
     jobs = []
     first_copies = []
-    for at, m in enumerate(order):
-        source = fulls[m] if m < lead else staged[(m - lead) % 3]
+    for at in range(count):
         used = traffic.used
         jobs.append(
             reduce_job(
-                traffic, at % 2 == 1, source, accs[at], lands[at * depth : (at + 1) * depth], outs[m]
+                traffic, at % 2 == 1, sources[at], accs[at], lands[at * depth : (at + 1) * depth], targets[at]
             )
         )
         digit = places.order(at % 2 == 1)[-1]
         first_copies.append(traffic.copies[used : used + places.dims[digit] - 1])
+    factors = len(jobs)
+    jobs.append(gather_job(traffic, False, mine_s, all_s))
+    for l in range(layers):
+        jobs.append(exchange_job(traffic, swaps[l * (depth + 1) : (l + 1) * (depth + 1)]))
+    inner = [d for d in reversed(range(depth)) if places.digits[d][0] == "tp"]
+
+    def both_copies(stage):
+        digit = inner[stage]
+        _, stride, size = places.digits[digit]
+        where = both_s.at[pl.ds(lax.axis_index("tp") // stride * stride, stride)]
+        return [
+            pltpu.make_async_remote_copy(
+                src_ref=where,
+                dst_ref=where,
+                send_sem=both_send.at[stage, shift - 1],
+                recv_sem=both_recv.at[stage, shift - 1],
+                device_id=places.other(mine, digit, shift)[0],
+                device_id_type=MESH,
+            )
+            for shift in range(1, size)
+        ]
+
+    exchange = [both_copies(stage) for stage in range(len(inner))]
+
+    def share(stage):
+        if stage == 0:
+            both_s[lax.axis_index("tp")] = small_out[...]
+        else:
+            for copy in exchange[stage - 1]:
+                copy.wait()
+        if stage < len(exchange):
+            for copy in exchange[stage]:
+                copy.start()
 
     def run(*names):
         for job, k in names:
@@ -1476,7 +1731,13 @@
         return pl.when((turn == layer_turn) & (h == half) & (n == step))
 
     def both(pair, k):
-        return [(job, k) for job in (2 * pair, 2 * pair + 1) if job < len(jobs)]
+        return [(job, k) for job in (2 * pair, 2 * pair + 1)]
+
+    def extra(name, k):
+        return [({3: 6, 4: 7}.get(name, name + 3), k)]
+
+    def swap_job(layer):
+        return factors + 1 + layer
 
     here = pl.ds(pl.multiple_of(n * rows, rows), rows)
 
@@ -1489,7 +1750,7 @@
 
     @at_step(0)
     def _():
-        for m in [*range(slots), lead + 5, lead + 4, lead + 3, lead + 2, lead + 1, lead, *range(slots, lead)]:
+        for m in [*range(slots), *range(chunks - 1, slots - 1, -1), chunks]:
             takes[m].start()
         d_mods_s[...] = jnp.zeros_like(d_mods_s)
         d_fmod_s[...] = jnp.zeros_like(d_fmod_s)
@@ -1497,21 +1758,21 @@
         d_head_s[...] = jnp.zeros_like(d_head_s)
         loss_s[...] = jnp.zeros_like(loss_s)
         sum_s[...] = jnp.zeros_like(sum_s)
+        mine_s[...] = jnp.zeros_like(mine_s)
+        wide_s[...] = jnp.zeros_like(wide_s)
+        small_s[...] = jnp.zeros_like(small_s)
+        patch_s[...] = jnp.zeros_like(patch_s)
         places.barrier(mine)
         for m in (*range(slots), lead + 5, lead + 4):
             takes[m].wait()
 
     hooks = {
-        steps: [],
-        steps + 1: both(0, 1),
-        2 * steps - 1: both(0, 2),
-        2 * steps + 1: both(0, 3) + both(1, 1),
-        3 * steps - 1: both(1, 2) + both(0, 4),
-        3 * steps + 1: both(1, 3) + both(2, 1),
-        4 * steps - 1: both(2, 2) + both(1, 4),
+        at * steps // 4: [job for name, k in names for job in (both(name, k) if name < 3 else extra(name, k))]
+        for at, names in LATER_BACK.items()
     }
+    shares = {at * steps // 4: stage for at, stage in SHARES.items()}
     early_ada = [slots + p for p in range(SPLIT) if p * part_rows < (layers - 1) * ada_rows]
-    loads = {steps: [lead + 3], 2 * steps: [lead + 2, lead + 1], 3 * steps: [lead, *early_ada]}
+    loads = {steps: [lead + 3], 2 * steps: [lead + 2, lead + 1], 3 * steps: [lead, chunks, *early_ada]}
     for number in sorted(set(hooks) | set(loads)):
 
         @at_step(number)
@@ -1519,6 +1780,28 @@
             for m in loads.get(number, []):
                 takes[m].wait()
             run(*hooks.get(number, []))
+            if number in shares:
+                share(shares[number])
+
+    def raw_part(p):
+        wide = places.count * part_rows
+        return split_low(d_raw_s[:, p * wide : (p + 1) * wide])
+
+    def send_mods(layer):
+        first = swaps[layer * (depth + 1)].reshape(places.count, 8, 128)
+        for j in range(places.count):
+            first[j] = d_mods_s[layer, :, j * ada_rows : j * ada_rows + 128]
+        run((swap_job(layer), 0))
+
+    def ada_grads(layer):
+        arrived = swaps[layer * (depth + 1) + depth].reshape(places.count, 8, 128)
+        wide_s[:, :8, :] = arrived[...]
+        signal = wide_s.reshape(places.count * 16, 128)[...]
+        high = signal.astype(BF)
+        low = (signal - high.astype(jnp.float32)).astype(BF)
+        fact = fulls[chunks].reshape(places.count * 16, D)[...]
+        grad = dot_tn(high, fact) + dot_tn(low, fact)
+        ada_grad_ref[layer * ada_rows : (layer + 1) * ada_rows, :] = grad[:ada_rows]
 
     def spread(layer):
         wide = places.count * part_rows
@@ -1526,101 +1809,67 @@
             if l == layer:
                 d_raw_s[:, p * wide + at : p * wide + at + length] = d_mods_s[layer, :, col : col + length]
 
+    def send_small():
+        cond_act = silu(cond_ref[...]).astype(BF)
+        cond_two = jnp.concatenate([cond_act, cond_act], axis=0)
+        view = small_s.reshape(-1, lax.axis_size("tp"), small_rows, D)
+
+        def give(k, grad):
+            view[:, k] = grad.astype(BF).reshape(view.shape[0], small_rows, D)
+
+        head = jnp.pad(d_head_s[...], ((0, 128 - OUT), (0, 0))).T
+        give(0, jnp.pad(head, ((0, 0), (0, D - 128))))
+        for k in range(2):
+            give(1 + k, dot_tn(cond_two, split_low(d_fmod_s[:, k * D : (k + 1) * D])))
+
+    def expand(entry):
+        name, k = entry
+        return both(name, k) if name < 3 else extra(name, k)
+
     def finish_all():
         run((6, 0))
+        send_mods(0)
+        patch = jnp.pad(d_patch_s[...], ((0, 0), (0, 128)))
+        view = patch_s.reshape(-1, lax.axis_size("tp"), PATCH_IN, 128)
+        for i in range(view.shape[0]):
+            here_cols = patch[:, i * small_rows : i * small_rows + 128].astype(BF)
+            for t in range(view.shape[1]):
+                view[i, t] = here_cols
+        run((7, 0))
+        for entry in TAIL_ONE:
+            run(*expand(entry))
         cond = cond_ref[...]
         pre = pre_ref[...]
-        cond_act = silu(cond).astype(BF)
-        cond_two = jnp.concatenate([cond_act, cond_act], axis=0)
         spread(0)
-        wide = places.count * part_rows
         d_cond = sum_s[...]
-        d_mods = {}
         for p in range(SPLIT):
             if p * part_rows < (layers - 1) * ada_rows:
-                d_mods[p] = split_low(d_raw_s[:, p * wide : (p + 1) * wide])
-                d_cond = d_cond + dot_nn(d_mods[p], ada_refs[p][...])
-        d_fmods = [split_low(d_fmod_s[:, k * D : (k + 1) * D]) for k in range(2)]
+                d_cond = d_cond + dot_nn(raw_part(p), ada_refs[p][...])
         for k in range(2):
-            d_cond = d_cond + dot_nt(d_fmods[k], block_of(slot_refs, 5 + k))
-        run(*both(2, 3))
-        d_pre = split_low((d_cond[:8] + d_cond[8:]) * silu_slope(cond))
-        d_time = dot_nn(d_pre, block_of(slot_refs, 1))
-        d_time = split_low((d_time[:8] + d_time[8:]) * silu_slope(pre))
-        time_act = silu(pre).astype(BF)
-
-        def give(k, grad):
-            ref = slot_refs[k % slots]
-            ref[:, k // slots] = grad.astype(BF).reshape(ref.shape[0], ref.shape[2], D)
-
-        def twice(values):
-            return jnp.concatenate([values, values], axis=0)
-
-        def k_time():
-            grad = dot_tn(d_time, twice(feat_ref[...]))
-            corner = jnp.pad(d_patch_s[...], ((0, 128 - PATCH_IN), (0, 0))).T
-            return jnp.concatenate([grad[:, :128] + corner, grad[:, 128:]], axis=1)
-
-        def k_class(k):
-            grad = dot_tn(d_pre, twice(hot_ref[:, k * D : (k + 1) * D]))
-            if k == 2:
-                corner = jnp.pad(d_head_s[...], ((0, 128 - OUT), (0, 0))).T
-                grad = jnp.concatenate([grad[:, :256], grad[:, 256:] + corner], axis=1)
-            return grad
-
-        makers = {
-            0: k_time,
-            1: lambda: dot_tn(d_pre, twice(time_act)),
-            2: lambda: k_class(0),
-            3: lambda: k_class(1),
-            4: lambda: k_class(2),
-            5: lambda: dot_tn(cond_two, d_fmods[0]),
-            6: lambda: dot_tn(cond_two, d_fmods[1]),
-        }
-        for slot in range(slots):
-            for k in range(slot, SMALL, slots):
-                give(k, makers[k]() if k in makers else jnp.zeros((D, D), jnp.float32))
-            if slot == 0:
-                run((7, 0), (6, 1))
-        run((8, 0))
-        for p, d_mod in d_mods.items():
-            ada_refs[p][...] = dot_tn(d_mod, cond_two).astype(BF)
-        run((9, 0), (10, 0), (7, 1), (8, 1), (9, 1))
-        run(*both(2, 4), *both(3, 2), (10, 1), (8, 2), *both(3, 3), (9, 2), (10, 2), (8, 3))
-        run((9, 3), *both(3, 4), (8, 4))
-        inner = [d for d in reversed(range(depth)) if places.digits[d][0] == "tp"]
-        for s in range(slots):
-            both_s[(lax.axis_index("tp"), s)] = outs[s][...]
-
-        def both_stage(stage):
-            digit = inner[stage]
-            _, stride, size = places.digits[digit]
-            start = lax.axis_index("tp") // stride * stride
-            copies = []
-            for shift in range(1, size):
-                target, _ = places.other(mine, digit, shift)
-                where = both_s.at[pl.ds(start, stride)]
-                copies.append(
-                    pltpu.make_async_remote_copy(
-                        src_ref=where,
-                        dst_ref=where,
-                        send_sem=both_send.at[stage, shift - 1],
-                        recv_sem=both_recv.at[stage, shift - 1],
-                        device_id=target,
-                        device_id_type=MESH,
-                    )
-                )
-                copies[-1].start()
-            return copies
-
-        pending = both_stage(0)
-        run((10, 3), (9, 4))
-        for stage in range(1, len(inner)):
-            for copy in pending:
-                copy.wait()
-            pending = both_stage(stage)
-        run((10, 4))
-        grad = sum(lane_sums(out[...] * out[...]) for out in outs)
+            d_fmod = split_low(d_fmod_s[:, k * D : (k + 1) * D])
+            d_cond = d_cond + dot_nt(d_fmod, block_of(slot_refs, 5 + k))
+        d_pre = (d_cond[:8] + d_cond[8:]) * silu_slope(cond)
+        d_time = dot_nn(split_low(d_pre), block_of(slot_refs, 1))
+        d_time = (d_time[:8] + d_time[8:]) * silu_slope(pre)
+        mine_s[4 : 4 + lat_count, :] = d_pre[:lat_count]
+        mine_s[8 : 8 + lat_count, :] = d_time[:lat_count]
+        mine_s[12 : 12 + lat_count, :] = d_pre[:lat_count]
+        for entry in TAIL_TWO:
+            if entry == "small":
+                small_grads()
+            elif entry == "ada":
+                for layer in range(layers):
+                    ada_grads(layer)
+            elif entry == "share":
+                share(len(exchange))
+            else:
+                run(*expand(entry))
+        copies_of_tp = 1.0 / lax.axis_size("tp")
+        grad = sum(lane_sums(out[...] * out[...]) for out in (*outs[:-1], small_out, ada_grad_ref))
+        lane = lax.broadcasted_iota(jnp.int32, (PATCH_IN, 128), 1)
+        patch = jnp.where(lane < small_rows, outs[-1][...], 0.0)
+        alike = sum(lane_sums(g * g) for g in (patch, early_ref[...], late_ref[...], class_ref[...]))
+        grad = grad + alike * copies_of_tp
         squares = [lane_sums(jnp.sum(square_ref[l], axis=0)) for l in range(layers)]
         stats_s[...] = jnp.concatenate(
             [grad, lane_sums(loss_s[...]), *squares, jnp.zeros((6 - layers, 128), jnp.float32)], axis=0
@@ -1649,13 +1898,34 @@
                 total = total + stats_land[stage, value]
             stats_s[...] = total
         stats_ref[...] = stats_s[...]
-        for copy in pending:
-            copy.wait()
         both_ref[...] = both_s[...]
         waited = {id(copy) for group in first_copies[:3] for copy in group}
         for copy in traffic.copies:
             if id(copy) not in waited:
                 copy.wait_send()
+
+    def small_grads():
+        total = places.count * 16
+        fact = fulls[chunks].reshape(total, D)[...]
+        signal = all_s.reshape(total, D)[...]
+        row = lax.broadcasted_iota(jnp.int32, (D, small_rows), 0)
+        column = lax.broadcasted_iota(jnp.int32, (D, small_rows), 1)
+        pick = jnp.where(row == column + lax.axis_index("dp") * small_rows, 1.0, 0.0).astype(BF)
+        high = signal.astype(BF)
+        low = (signal - high.astype(jnp.float32)).astype(BF)
+        picked = [dot_nn(part, pick).astype(BF) for part in (high, low)]
+        kind = lax.rem(lax.broadcasted_iota(jnp.int32, (total, 1), 0), 16) // 4
+
+        def rows_of(which):
+            mask = jnp.where(kind == which, 1.0, 0.0).astype(BF)
+            return [part * mask for part in picked]
+
+        late_ref[...] = sum(dot_tn(part, fact) for part in rows_of(1))
+        early_ref[...] = sum(dot_tn(part, fact) for part in rows_of(2))
+        label = fact[:, 0:1].astype(jnp.float32) + 32.0 * fact[:, 128:129].astype(jnp.float32)
+        wide = lax.broadcasted_iota(jnp.int32, (total, 3 * D), 1).astype(jnp.float32)
+        hot = jnp.where(wide == label, 1.0, 0.0).astype(BF)
+        class_ref[...] = sum(dot_tn(part, hot) for part in rows_of(3))
 
     for layer in range(layers):
         mod = mod_of(layer)
@@ -1717,6 +1987,8 @@
                 flat(stage_in, wide_rows)[...] = acc_one[...].astype(BF)
                 flat(stage_out, wide_rows)[...] = acc_two[...].astype(BF)
                 run(*both(pair, 0))
+                if layer == layers - 1:
+                    send_small()
 
         @pl.when(is_turn & (h == 1))
         def _(layer=layer, mod=mod, attn_w=attn_w):
@@ -1759,27 +2031,24 @@
                         copy.wait_send()
                 flat(stage_attn, wide_rows)[...] = acc_one[...].astype(BF)
                 if layer > 0:
-                    cond_act = silu(cond_ref[...]).astype(BF)
-                    cond_two = jnp.concatenate([cond_act, cond_act], axis=0)
+                    run(*both(1, 0))
                     spread(layer)
-                    wide = places.count * part_rows
                     for p in range(SPLIT):
                         if p * part_rows >= layer * ada_rows:
-                            d_mod = split_low(d_raw_s[:, p * wide : (p + 1) * wide])
                             takes[slots + p].wait()
-                            sum_s[...] += dot_nn(d_mod, ada_refs[p][...])
-                            ada_refs[p][...] = dot_tn(d_mod, cond_two).astype(BF)
-                    run(*both(1, 0))
+                            sum_s[...] += dot_nn(raw_part(p), ada_refs[p][...])
+                    send_mods(layer)
                 else:
                     finish_all()
 
 
-def fused_backward(places, slots, nb, count_all, given, feat, hot, mods, fmod, pre, cond, square, streams):
+def fused_backward(places, slots, nb, count_all, given, mods, fmod, pre, cond, square, streams):
     clean_t, noise_t, noisy, start, result, *kept = streams
     layers = mods.shape[0]
     lat_count, _, tokens = noisy.shape
     total, rows, steps = lat_count * tokens, nb * tokens, lat_count // nb
-    chunks = len(given)
+    chunks = len(given) - 1
+    jobs = chunks - slots - SPLIT + 2
     dims = places.dims
     depth, widest = len(dims), max(dims)
     block = given[0].shape[-2:]
@@ -1811,8 +2080,8 @@
     def attn_spec(cols):
         return pl.BlockSpec((1, rows, cols), lambda t, h, n: (layers - 1 - t, jnp.where(h == 1, n, 0), 0))
 
-    consts = (feat, hot, mods, fmod, pre, cond, square)
-    in_specs = [pl.BlockSpec(memory_space=pl.ANY)] * chunks + [const_shape(a.shape) for a in consts]
+    consts = (mods, fmod, pre, cond, square)
+    in_specs = [pl.BlockSpec(memory_space=pl.ANY)] * (chunks + 1) + [const_shape(a.shape) for a in consts]
     in_specs += [spec((nb, PATCH_IN, tokens), only(0, 0, 0, last))] * 2
     in_specs += [
         spec((nb, PATCH_IN, tokens), only(1, 1, 0, last)),
@@ -1820,15 +2089,30 @@
         pl.BlockSpec((1, rows, D), result_index),
     ]
     in_specs += [attn_spec(a.shape[2]) for a in kept[:4]] + [mlp_spec(a.shape[2]) for a in kept[4:]]
-    shared = (lax.axis_size("tp"), slots, *block)
-    out_shape = [jax.ShapeDtypeStruct(block, jnp.float32)] * chunks
-    out_shape += [jax.ShapeDtypeStruct(s, jnp.float32) for s in (shared, (8, 128))]
+    patch_block = (PATCH_IN, 128)
+    shared = (lax.axis_size("tp"), *block)
+    out_shape = [jax.ShapeDtypeStruct(block, jnp.float32)] * (jobs - 2)
+    out_shape += [
+        jax.ShapeDtypeStruct(s, jnp.float32)
+        for s in (patch_block, shared, block, block, (block[0], 3 * D), (layers * mods.shape[2] // places.count, D), (8, 128))
+    ]
     full = (*dims, *block)
-    lands = []
-    for at in range(chunks):
-        lands += [pltpu.VMEM(shape, BF) for shape in land_shapes(places, at % 2 == 1, block)]
+    blocks = [block] * (jobs - 1) + [patch_block]
+    accs, lands = [], []
+    for at in range(jobs):
+        accs.append(pltpu.VMEM(dims[:-1] + blocks[at], BF))
+        lands += [pltpu.VMEM(shape, BF) for shape in land_shapes(places, at % 2 == 1, blocks[at])]
     f32 = jnp.float32
-    scratch = [pltpu.VMEM(full, BF)] * chunks + [pltpu.VMEM(dims[:-1] + block, BF)] * chunks + lands
+    scratch = [pltpu.VMEM(full, BF)] * chunks + [pltpu.VMEM((*dims, 16, D), BF)] + accs + lands
+    scratch += [pltpu.VMEM((*dims, 8, 128), f32)] * (layers * (depth + 1))
+    scratch += [
+        pltpu.VMEM((places.count, 16, 128), f32),
+        pltpu.VMEM(full, BF),
+        pltpu.VMEM((*dims, *patch_block), BF),
+        pltpu.VMEM(block, f32),
+        pltpu.VMEM((16, D), f32),
+        pltpu.VMEM((*dims, 16, D), f32),
+    ]
     scratch += [pltpu.VMEM(full, BF)] * 3
     scratch += [
         pltpu.VMEM(shape, kind)
@@ -1837,7 +2121,7 @@
             ((4 * D, D), f32),
             ((total, D), f32),
             ((rows, 3 * D), BF),
-            (mods.shape, f32),
+            ((*mods.shape[:2], mods.shape[2] + 128), f32),
             ((8, SPLIT * places.count * block[0]), f32),
             ((8, 2 * D), f32),
             ((PATCH_IN, D), f32),
@@ -1850,8 +2134,8 @@
         )
     ]
     dma = pltpu.SemaphoreType.DMA
-    count = chunks * copies_per_part(places)
-    scratch += [dma((count,)), dma((count,)), dma((chunks,)), dma((chunks,))]
+    count = (jobs + 1 + layers) * copies_per_part(places)
+    scratch += [dma((count,)), dma((count,)), dma((jobs + 1,)), dma((chunks + 1,))]
     scratch += [dma((depth, widest - 1))] * 4
     sizes = (block[0], 6 * D // places.count, block[0], block[0])
     return pl.pallas_call(
@@ -1941,8 +2225,6 @@
     count_rms = float(lat_count * devices * tokens * D)
     nb = 1
     clean_t, noise_t = swap(clean_latents), swap(noise_field)
-    cos_part, sin_part = noise_scales(timesteps)
-    noisy = (cos_part[:, None, None] * clean_t + sin_part[:, None, None] * noise_t).astype(BF)
     n_dp, n_tp = lax.axis_size("dp"), lax.axis_size("tp")
     places = Places(n_dp, n_tp)
     slots = -(-SMALL // n_tp)
@@ -1978,23 +2260,27 @@
         block = block.reshape(n_tp, n_dp, dp_rows, D).swapaxes(0, 1)
         return pad_rows(block.reshape(places.count, dp_rows, D))
 
-    time_feat = time_table(timesteps, FREQ).astype(BF)
-    feat = jnp.pad(time_feat, ((0, 8 - lat_count), (PATCH_IN, D - PATCH_IN - FREQ)))
-    classes_used = jnp.where(drop_flags == 1, CLASSES, labels)
-    classes_used = jnp.pad(classes_used, (0, 8 - lat_count), constant_values=3 * D)
-    class_hot = (classes_used[:, None] == jnp.arange(3 * D, dtype=jnp.int32)[None, :]).astype(BF)
-    pos = position_table(GRID, D)
     fused = dp_rows == wide_rows == part_rows and dp_rows % 16 == 0 and len(places.dims) >= 4 and layers == 2
+    fused = fused and n_tp >= 3 and lat_count == 4
     if fused:
-        outs = fused_forward(places, slots, nb, weights_in, feat, class_hot, noisy, pos)
+        outs = fused_forward(
+            places, slots, nb, weights_in, (timesteps, labels, drop_flags), clean_t, noise_t
+        )
         chunks = slots + SPLIT + 3 * layers
-        mods, fmod, pre, cond, start, result, *kept, square = outs[chunks:]
+        mods, fmod, pre, cond, noisy, start, result, *kept, square = outs[chunks + 1 :]
         streams = (clean_t, noise_t, noisy, start, result, *kept)
-        *summed, both, stats = fused_backward(
-            places, slots, nb, count_all, outs[:chunks], feat, class_hot, mods, fmod, pre, cond, square, streams
+        *summed, patch, both, early, late, classes, ada_grad, stats = fused_backward(
+            places, slots, nb, count_all, outs[: chunks + 1], mods, fmod, pre, cond, square, streams
         )
-        wide = summed[slots + SPLIT :]
     else:
+        cos_part, sin_part = noise_scales(timesteps)
+        noisy = (cos_part[:, None, None] * clean_t + sin_part[:, None, None] * noise_t).astype(BF)
+        time_feat = time_table(timesteps, FREQ).astype(BF)
+        feat = jnp.pad(time_feat, ((0, 8 - lat_count), (PATCH_IN, D - PATCH_IN - FREQ)))
+        classes_used = jnp.where(drop_flags == 1, CLASSES, labels)
+        classes_used = jnp.pad(classes_used, (0, 8 - lat_count), constant_values=3 * D)
+        class_hot = (classes_used[:, None] == jnp.arange(3 * D, dtype=jnp.int32)[None, :]).astype(BF)
+        pos = position_table(GRID, D)
         gathered = gather_all(places, slots, *weights_in)
         slot_full = [to_slot(g) for g in gathered[:slots]]
         ada_full = [whole_rows(g, part_rows) for g in gathered[slots : slots + SPLIT]]
@@ -2063,7 +2349,10 @@
         (lambda a: a, (final_weight, final_first, final_second)),
     ):
         states.extend(shape_it(a) for a in triple)
-    out = adam_all(slots, layers, count_rms, stats, both, [*summed[slots : slots + SPLIT], *wide], states)
+    if fused:
+        out = fused_adam(layers, count_rms, (stats, both, early, late, classes, ada_grad, patch), summed, states)
+    else:
+        out = adam_all(slots, layers, count_rms, stats, both, [*summed[slots : slots + SPLIT], *wide], states)
     news = []
     for at in range(21):
         value = out[at]

time: 244 us -> 224 us (0.918)
  Pallas kernels: 235 us -> 223 us
  other arithmetic: 8.37 us -> 0 us
    pallas_call x1, Pallas kernels: 123 us -> 109 us  [fused_backward(): pl.pallas_call(functools.partial(fused_backward_kernel, places, slots, la...]
    convert_element_type x4 -> x0, other arithmetic: 2.9 us -> none  [the longest x1 1.57 us: body(): (cos_part[:, None, None] * clean_t + sin_part[:, None, None] * noise_t).a...]
where the time goes in v3:
time: 224 us
  Pallas kernels  223 us (100%)
    pallas_call x1, Pallas kernels, fused_forward(): pl.pallas_call(functools.partial(fused_forward_kernel, places, slots, lay...  110 us
    pallas_call x1, Pallas kernels, fused_backward(): pl.pallas_call(functools.partial(fused_backward_kernel, places, slots, la...  109 us
    pallas_call x1, Pallas kernels, fused_adam(): pl.pallas_call(functools.partial(fused_adam_kernel, layers, count_rms), o...  4.75 us

profile of v3, /device:TPU:0, one launch (start us, length us, event | category | flops | bytes accessed | tf_op | source)
XLA Modules:
  0.0 224.2 jit_solution(14088387959601178020)
XLA Ops:
  0.7 109.9 %gather_and_forward.1 = (bf16[4,2,2,2,48,384]{5,4,3,2,1,0:T(8,128)(2,1)}, bf16[4,2,2,2,48,384]{5,4,3,2,1,0:T(8,128)(2,1)}, bf16[4,2,2,2,48,384]{5,4,3,2,1,0:T(8,...) custom-call(f32[48,656]{1,0:T(8,128)} %bitcast.51, ...), custom_call_target="tpu_custom_call" | custom-call | tf_op jit(solution)/shard_map/gather_and_forward/pallas_call | solution.py:1460
  110.5 108.7 %backward_and_reduce.1 = (f32[48,384]{1,0:T(8,128)}, f32[48,384]{1,0:T(8,128)}, f32[48,384]{1,0:T(8,128)}, f32[48,384]{1,0:T(8,128)}, f32[48,384]{1,0:T(8,128)},...) custom-call(bf16[4,2,2,2,48,384]{5,4,3,2,1,0:T(8,128)(2,1)} %get-tup, ...), custom_call_target="tpu_custom_call" | custom-call | tf_op jit(solution)/shard_map/backward_and_reduce/pallas_call | solution.py:2141
  219.2 4.8 %adam_update.1 = (f32[48,656]{1,0:T(8,128)}, f32[48,656]{1,0:T(8,128)}, f32[48,656]{1,0:T(8,128)}, f32[48,1001]{1,0:T(8,128)}, f32[48,1001]{1,0:T(8,128)}, /*ind...) custom-call(f32[8,128]{1,0:T(8,128)} %get-tuple-element.117.refs_0_,, ...), custom_call_target="tpu_custom_call" | custom-call | tf_op jit(solution)/shard_map/adam_update/pallas_call | solution.py:1051

commit v4 on v3

--- a/solution.py
+++ b/solution.py
@@ -20,6 +20,7 @@
 NOISE_STEPS = 1000
 STEP = 10
 BF = jnp.bfloat16
+NB_FORWARD = 1
 
 
 highest = lax.Precision.HIGHEST
@@ -416,6 +417,7 @@
                 self.digits.append((axis, stride, size))
         self.dims = tuple(size for _, _, size in self.digits)
         self.count = n_dp * n_tp
+        self.n_tp = n_tp
 
     def order(self, odd):
         names = list(range(len(self.digits)))
@@ -430,6 +432,20 @@
         axis, stride, size = self.digits[digit]
         value = lax.rem(mine[digit] + shift, size)
         return {axis: lax.axis_index(axis) + (value - mine[digit]) * stride}, value
+
+    def index(self):
+        return lax.axis_index("dp") * self.n_tp + lax.axis_index("tp")
+
+    def device(self, index):
+        return (index // self.n_tp, lax.rem(index, self.n_tp))
+
+    def barrier_all(self):
+        barrier = pltpu.get_barrier_semaphore()
+        me = self.index()
+        for shift in range(1, self.count):
+            target = self.device(lax.rem(me + shift, self.count))
+            pl.semaphore_signal(barrier, inc=1, device_id=target, device_id_type=MESH)
+        pl.semaphore_wait(barrier, self.count - 1)
 
     def barrier(self, mine):
         barrier = pltpu.get_barrier_semaphore()
@@ -443,7 +459,7 @@
 
 
 SMALL = 8
-SPLIT = 3
+SPLIT = 2
 
 
 def small_blocks(entry_t, table_t, final):
@@ -660,7 +676,7 @@
             packed[SPLIT + 3 * l + k, : source.shape[1], :] = source[l].astype(BF)
     first = lax.axis_index("tp") * slots
     ins = [small.at[first + s] for s in range(slots)]
-    ins += [packed.at[m] for m in range(SPLIT + 3 * layers)]
+    ins += [packed.at[m, : outs[slots + m].shape[-2]] for m in range(SPLIT + 3 * layers)]
     places.barrier(mine)
     traffic = Traffic(places, mine, send_sems, recv_sems, own_sems)
     jobs = [gather_job(traffic, m % 2 == 1, ins[m], outs[m]) for m in range(chunks)]
@@ -681,7 +697,6 @@
     chunks = len(sizes)
     vmem = pl.BlockSpec(memory_space=pltpu.VMEM)
     packed_rows = max(ada_rows, wide_rows)
-    assert packed_rows == min(ada_rows, wide_rows)
     outs = pl.pallas_call(
         functools.partial(gather_kernel, places, slots, layers),
         out_shape=[jax.ShapeDtypeStruct((*places.dims, rows, D), BF) for rows in sizes],
@@ -1059,7 +1074,7 @@
     )(*args)
 
 
-def modulation_pieces(layers, ada_rows, part_rows, count):
+def modulation_pieces(layers, ada_rows, part_rows, part_pad, count):
     pieces = []
     for j in range(count):
         for l in range(layers):
@@ -1067,7 +1082,7 @@
             while low < (l + 1) * ada_rows:
                 p, r = divmod(low, part_rows)
                 length = min((l + 1) * ada_rows - low, part_rows - r)
-                pieces.append((l, j * ada_rows + low - l * ada_rows, p, j * part_rows + r, length))
+                pieces.append((l, j * ada_rows + low - l * ada_rows, p, j * part_pad + r, length))
                 low += length
     return pieces
 
@@ -1092,7 +1107,7 @@
         high = (label - low) // 32
         fact_s[12 + b : 13 + b, :128] = jnp.full((1, 128), low, jnp.int32).astype(jnp.float32)
         fact_s[12 + b : 13 + b, 128:256] = jnp.full((1, 128), high, jnp.int32).astype(jnp.float32)
-    fact_s[8 : 8 + lat_count, :] = feat_s[:lat_count, :]
+    fact_s[4 : 4 + lat_count, :] = feat_s[:lat_count, :]
 
 
 def embed_condition(lat_count, feat_s, hot_s, fact_s, slot_refs, pre_ref, cond_ref, fmod_ref):
@@ -1104,8 +1119,8 @@
         cond = cond + dot_nt(hot_s[:, k * D : (k + 1) * D].astype(BF), block_of(slot_refs, 2 + k))
     cond_ref[...] = cond
     act = silu(cond).astype(BF)
-    fact_s[:lat_count, :] = act.astype(jnp.float32)[:lat_count]
-    fact_s[4 : 4 + lat_count, :] = time_act.astype(jnp.float32)[:lat_count]
+    fact_s[8 : 8 + lat_count, :] = act.astype(jnp.float32)[:lat_count]
+    fact_s[:lat_count, :] = time_act.astype(jnp.float32)[:lat_count]
     for k in range(2):
         fmod_ref[:, k * D : (k + 1) * D] = dot_nn(act, block_of(slot_refs, 5 + k))
 
@@ -1173,44 +1188,12 @@
     return jnp.asarray(freq[None], jnp.float32), jnp.asarray(table, jnp.float32)
 
 
-PROLOGUE = [
-    (0, 1),
-    (2, 0),
-    (1, 1),
-    (0, 2),
-    (3, 0),
-    (2, 1),
-    (1, 2),
-    (0, 3),
-    (4, 0),
-    (3, 1),
-    (2, 2),
-    (1, 3),
-    (0, 4),
-    "cond",
-    (5, 0),
-    (4, 1),
-    (3, 2),
-    (2, 3),
-    (1, 4),
-    "mods",
-    (5, 1),
-    (4, 2),
-    (3, 3),
-    (2, 4),
-]
-LATER = {
-    1: [(6, 0)],
-    3: [(6, 1)],
-    4: [(5, 2), (4, 3), (3, 4)],
-    6: [(6, 2)],
-    8: [(5, 3), (4, 4), "mods", (6, 3)],
-    12: [(5, 4), (6, 4), "hand"],
-}
+PROLOGUE = [(0, 1), (0, 2), (1, 1), (0, 3), (2, 0), (1, 2), (0, 4), 'cond', (2, 1), (1, 3), (3, 0), (1, 4), 'mods', (2, 2)]
+LATER = {1: [(3, 1), (4, 0)], 3: [(2, 3)], 4: [(2, 4), (3, 2)], 6: [(4, 1), (5, 0)], 7: [(3, 3)], 8: [(3, 4), 'mods', (5, 1)], 9: [(4, 2)], 10: [(5, 2)], 11: [(4, 3)], 12: [(4, 4), (5, 3)], 14: [(5, 4), 'hand']}
 
 
 def fused_forward_kernel(places, slots, layers, nb, tokens, lat_count, sizes, *refs):
-    small_rows, ada_rows, part_rows, wide_rows = sizes
+    small_rows, ada_rows, part_rows, part_pad, wide_rows = sizes
     chunks = slots + SPLIT + 3 * layers
     entry_ref, table_ref, final_ref, ada_ref, attn_ref, in_ref, out_ref = refs[:7]
     times_ref, labels_ref, drops_ref, freq_ref, clean_ref, noise_ref, pos_ref = refs[7:14]
@@ -1238,6 +1221,7 @@
     fulls = refs[: chunks + 1]
     (
         small,
+        packed_ada,
         packed,
         stream_s,
         middle_s,
@@ -1253,9 +1237,12 @@
     l, h, n = (pl.program_id(axis) for axis in range(3))
     mine = places.mine()
     first = lax.axis_index("tp") * slots
-    order = [*range(slots), slots, slots + 1, slots + SPLIT, slots + SPLIT + 1, slots + SPLIT + 2, slots + 2]
-    order += range(slots + SPLIT + 3, chunks)
-    sources = [small.at[first + s] for s in range(slots)] + [packed.at[m] for m in range(SPLIT + 3 * layers)]
+    order = [*range(slots)]
+    for ll in range(layers):
+        at = slots + SPLIT + 3 * ll
+        order += [at, slots + ll, at + 1, at + 2]
+    sources = [small.at[first + s] for s in range(slots)] + [packed_ada.at[p] for p in range(SPLIT)]
+    sources += [packed.at[m] for m in range(3 * layers)]
     traffic = Traffic(places, mine, send_sems, recv_sems, own_sems)
     jobs = [gather_job(traffic, at % 2 == 1, sources[m], fulls[m]) for at, m in enumerate(order)]
     pairs = [jobs[at : at + 2] for at in range(0, chunks, 2)]
@@ -1277,8 +1264,8 @@
         act = silu(cond_ref[...]).astype(BF)
         low, high = layer * ada_rows, (layer + 1) * ada_rows
         parts = range(low // part_rows, -(-high // part_rows))
-        raw = {p: dot_nt(act, flat(slots + p, part_rows)[...]) for p in parts}
-        for ll, col, p, at, length in modulation_pieces(layers, ada_rows, part_rows, places.count):
+        raw = {p: dot_nt(act, flat(slots + p, part_pad)[...]) for p in parts}
+        for ll, col, p, at, length in modulation_pieces(layers, ada_rows, part_rows, part_pad, places.count):
             if ll == layer:
                 mods_ref[layer, :, col : col + length] = raw[p][:, at : at + length]
 
@@ -1287,7 +1274,8 @@
     def pack_blocks():
         for ll in range(layers):
             for k, source in enumerate((attn_ref, in_ref, out_ref)):
-                packed[SPLIT + 3 * ll + k] = source[ll].astype(BF)
+                if ll or k:
+                    packed[3 * ll + k] = source[ll].astype(BF)
 
     @at_step(0, 0, 0)
     def _():
@@ -1296,8 +1284,10 @@
             small[k, : source.shape[0], at : at + high - low] = source[:, low:high].astype(BF)
         places.barrier(mine)
         run((0, 0))
+        packed_ada[...] = jnp.zeros_like(packed_ada)
         for p in range(SPLIT):
-            packed[p] = ada_ref[p * part_rows : (p + 1) * part_rows, :].astype(BF)
+            packed_ada[p, :part_rows, :] = ada_ref[p * part_rows : (p + 1) * part_rows, :].astype(BF)
+        packed[0] = attn_ref[0].astype(BF)
         run((1, 0))
         pack_blocks()
         embed_inputs(lat_count, times_ref, labels_ref, drops_ref, freq_ref, feat_s, hot_s, fact_s)
@@ -1402,7 +1392,8 @@
     layers, wide_rows = attn_t.shape[:2]
     lat_count, _, tokens = clean_t.shape
     small_rows, part_rows, ada_rows = final.shape[0], ada_t.shape[0] // SPLIT, ada_t.shape[0] // layers
-    sizes = [small_rows] * slots + [part_rows] * SPLIT + [wide_rows] * (3 * layers)
+    part_pad = pad16(part_rows)
+    sizes = [small_rows] * slots + [part_pad] * SPLIT + [wide_rows] * (3 * layers)
     chunks = len(sizes)
     steps = lat_count // nb
     rows, total = nb * tokens, lat_count * tokens
@@ -1466,7 +1457,7 @@
             nb,
             tokens,
             lat_count,
-            (small_rows, ada_rows, part_rows, wide_rows),
+            (small_rows, ada_rows, part_rows, part_pad, wide_rows),
         ),
         grid=(layers, 2, steps),
         out_shape=out_shape,
@@ -1475,7 +1466,8 @@
         scratch_shapes=[pltpu.VMEM(s, BF) for s in full_shapes]
         + [
             pltpu.VMEM((slots * lax.axis_size("tp"), small_rows, D), BF),
-            pltpu.VMEM((SPLIT + 3 * layers, wide_rows, D), BF),
+            pltpu.VMEM((SPLIT, part_pad, D), BF),
+            pltpu.VMEM((3 * layers, wide_rows, D), BF),
             pltpu.VMEM((total, D), jnp.float32),
             pltpu.VMEM((total, D), jnp.float32),
             pltpu.VMEM((8, D), jnp.float32),
@@ -1496,38 +1488,10 @@
 
 LIMIT_B = 62 * 1024 * 1024
 
-LATER_BACK = {
-    5: [(0, 1)],
-    7: [(0, 2)],
-    9: [(0, 3), (1, 1), (7, 1)],
-    11: [(1, 2), (0, 4), (7, 2)],
-    13: [(1, 3), (2, 1), (7, 3)],
-    14: [(1, 4), (7, 4)],
-    15: [(2, 2)],
-}
-SHARES = {14: 0, 15: 1}
-TAIL_ONE = [(3, 1), (6, 1), (4, 1)]
-TAIL_TWO = [
-    (5, 0),
-    (2, 3),
-    (3, 2),
-    (6, 2),
-    (5, 1),
-    (4, 2),
-    (3, 3),
-    (6, 3),
-    (5, 2),
-    (4, 3),
-    (2, 4),
-    (5, 3),
-    (6, 4),
-    "ada",
-    (5, 4),
-    "small",
-    "share",
-    (4, 4),
-    (3, 4),
-]
+LATER_BACK = {5: [(0, 1)], 8: [(0, 2)], 9: [(1, 1)], 10: [(0, 3), (7, 1)], 11: [(1, 2)], 12: [(7, 2)], 13: [(1, 3), (2, 1), (0, 4)], 14: [(7, 3)], 15: [(2, 2)]}
+SHARES = {}
+TAIL_ONE = [(3, 1), (2, 3), (6, 1), (4, 1)]
+TAIL_TWO = [(5, 1), (7, 4), (1, 4), 0, (3, 2), (6, 2), (4, 2), 1, (3, 3), (6, 3), (5, 2), (4, 3), (2, 4), 2, (5, 3), (6, 4), 'ada', (5, 4), 'small', (4, 4), (3, 4)]
 
 
 def exchange_job(traffic, bufs):
@@ -1593,7 +1557,7 @@
 
 
 def fused_backward_kernel(places, slots, layers, nb, tokens, lat_count, count_all, sizes, *refs):
-    small_rows, ada_rows, part_rows, wide_rows = sizes
+    small_rows, ada_rows, part_rows, part_pad, wide_rows = sizes
     chunks = slots + SPLIT + 3 * layers
     steps = lat_count // nb
     depth = len(places.dims)
@@ -1633,6 +1597,8 @@
         small_out,
         mine_s,
         all_s,
+        signal_s,
+        code_s,
         stage_attn,
         stage_in,
         stage_out,
@@ -1668,7 +1634,7 @@
 
     takes = [pltpu.make_async_copy(given[m], fulls[m], take_sems.at[m]) for m in range(chunks + 1)]
     slot_refs = [f.reshape(-1, lax.axis_size("tp"), small_rows, D) for f in fulls[:slots]]
-    ada_refs = [flat(f, part_rows) for f in fulls[slots:lead]]
+    ada_refs = [flat(f, part_pad) for f in fulls[slots:lead]]
     staged = {0: stage_attn, 1: stage_in, 2: stage_out}
     order = [lead + 4, lead + 5, lead + 3, lead + 1, lead + 2, lead]
     sources = [staged[(m - lead) % 3] for m in order] + [patch_s]
@@ -1753,6 +1719,7 @@
         for m in [*range(slots), *range(chunks - 1, slots - 1, -1), chunks]:
             takes[m].start()
         d_mods_s[...] = jnp.zeros_like(d_mods_s)
+        d_raw_s[...] = jnp.zeros_like(d_raw_s)
         d_fmod_s[...] = jnp.zeros_like(d_fmod_s)
         d_patch_s[...] = jnp.zeros_like(d_patch_s)
         d_head_s[...] = jnp.zeros_like(d_head_s)
@@ -1760,9 +1727,10 @@
         sum_s[...] = jnp.zeros_like(sum_s)
         mine_s[...] = jnp.zeros_like(mine_s)
         wide_s[...] = jnp.zeros_like(wide_s)
+        signal_s[...] = jnp.zeros_like(signal_s)
         small_s[...] = jnp.zeros_like(small_s)
         patch_s[...] = jnp.zeros_like(patch_s)
-        places.barrier(mine)
+        places.barrier_all()
         for m in (*range(slots), lead + 5, lead + 4):
             takes[m].wait()
 
@@ -1784,7 +1752,7 @@
                 share(shares[number])
 
     def raw_part(p):
-        wide = places.count * part_rows
+        wide = places.count * part_pad
         return split_low(d_raw_s[:, p * wide : (p + 1) * wide])
 
     def send_mods(layer):
@@ -1795,7 +1763,7 @@
 
     def ada_grads(layer):
         arrived = swaps[layer * (depth + 1) + depth].reshape(places.count, 8, 128)
-        wide_s[:, :8, :] = arrived[...]
+        wide_s[:, 8:, :] = arrived[...]
         signal = wide_s.reshape(places.count * 16, 128)[...]
         high = signal.astype(BF)
         low = (signal - high.astype(jnp.float32)).astype(BF)
@@ -1804,8 +1772,8 @@
         ada_grad_ref[layer * ada_rows : (layer + 1) * ada_rows, :] = grad[:ada_rows]
 
     def spread(layer):
-        wide = places.count * part_rows
-        for l, col, p, at, length in modulation_pieces(layers, ada_rows, part_rows, places.count):
+        wide = places.count * part_pad
+        for l, col, p, at, length in modulation_pieces(layers, ada_rows, part_rows, part_pad, places.count):
             if l == layer:
                 d_raw_s[:, p * wide + at : p * wide + at + length] = d_mods_s[layer, :, col : col + length]
 
@@ -1828,16 +1796,6 @@
 
     def finish_all():
         run((6, 0))
-        send_mods(0)
-        patch = jnp.pad(d_patch_s[...], ((0, 0), (0, 128)))
-        view = patch_s.reshape(-1, lax.axis_size("tp"), PATCH_IN, 128)
-        for i in range(view.shape[0]):
-            here_cols = patch[:, i * small_rows : i * small_rows + 128].astype(BF)
-            for t in range(view.shape[1]):
-                view[i, t] = here_cols
-        run((7, 0))
-        for entry in TAIL_ONE:
-            run(*expand(entry))
         cond = cond_ref[...]
         pre = pre_ref[...]
         spread(0)
@@ -1851,17 +1809,27 @@
         d_pre = (d_cond[:8] + d_cond[8:]) * silu_slope(cond)
         d_time = dot_nn(split_low(d_pre), block_of(slot_refs, 1))
         d_time = (d_time[:8] + d_time[8:]) * silu_slope(pre)
-        mine_s[4 : 4 + lat_count, :] = d_pre[:lat_count]
-        mine_s[8 : 8 + lat_count, :] = d_time[:lat_count]
-        mine_s[12 : 12 + lat_count, :] = d_pre[:lat_count]
+        mine_s[:lat_count, :] = d_pre[:lat_count]
+        mine_s[4 : 4 + lat_count, :] = d_time[:lat_count]
+        run((factors, 0))
+        send_mods(0)
+        patch = jnp.pad(d_patch_s[...], ((0, 0), (0, 128)))
+        view = patch_s.reshape(-1, lax.axis_size("tp"), PATCH_IN, 128)
+        for i in range(view.shape[0]):
+            here_cols = patch[:, i * small_rows : i * small_rows + 128].astype(BF)
+            for t in range(view.shape[1]):
+                view[i, t] = here_cols
+        run((7, 0))
+        for entry in TAIL_ONE:
+            run(*expand(entry))
         for entry in TAIL_TWO:
             if entry == "small":
                 small_grads()
             elif entry == "ada":
                 for layer in range(layers):
                     ada_grads(layer)
-            elif entry == "share":
-                share(len(exchange))
+            elif isinstance(entry, int):
+                share(entry)
             else:
                 run(*expand(entry))
         copies_of_tp = 1.0 / lax.axis_size("tp")
@@ -1874,29 +1842,24 @@
         stats_s[...] = jnp.concatenate(
             [grad, lane_sums(loss_s[...]), *squares, jnp.zeros((6 - layers, 128), jnp.float32)], axis=0
         )
-        for stage, digit in enumerate(reversed(range(depth))):
-            size = places.dims[digit]
-            stats_land[stage, mine[digit]] = stats_s[...]
-            copies = []
-            for shift in range(1, size):
-                target, _ = places.other(mine, digit, shift)
-                copies.append(
-                    pltpu.make_async_remote_copy(
-                        src_ref=stats_s,
-                        dst_ref=stats_land.at[stage, mine[digit]],
-                        send_sem=stats_send.at[stage, shift - 1],
-                        recv_sem=stats_recv.at[stage, shift - 1],
-                        device_id=target,
-                        device_id_type=MESH,
-                    )
+        me = places.index()
+        stats_land[me] = stats_s[...]
+        copies = []
+        for shift in range(1, places.count):
+            copies.append(
+                pltpu.make_async_remote_copy(
+                    src_ref=stats_s,
+                    dst_ref=stats_land.at[me],
+                    send_sem=stats_send.at[shift - 1],
+                    recv_sem=stats_recv.at[shift - 1],
+                    device_id=places.device(lax.rem(me + shift, places.count)),
+                    device_id_type=MESH,
                 )
-                copies[-1].start()
-            for copy in copies:
-                copy.wait()
-            total = stats_land[stage, 0]
-            for value in range(1, size):
-                total = total + stats_land[stage, value]
-            stats_s[...] = total
+            )
+            copies[-1].start()
+        for copy in copies:
+            copy.wait()
+        stats_s[...] = jnp.sum(stats_land[...], axis=0)
         stats_ref[...] = stats_s[...]
         both_ref[...] = both_s[...]
         waited = {id(copy) for group in first_copies[:3] for copy in group}
@@ -1907,7 +1870,8 @@
     def small_grads():
         total = places.count * 16
         fact = fulls[chunks].reshape(total, D)[...]
-        signal = all_s.reshape(total, D)[...]
+        signal_s[:, :8, :] = all_s.reshape(places.count, 8, D)[...]
+        signal = signal_s.reshape(total, D)[...]
         row = lax.broadcasted_iota(jnp.int32, (D, small_rows), 0)
         column = lax.broadcasted_iota(jnp.int32, (D, small_rows), 1)
         pick = jnp.where(row == column + lax.axis_index("dp") * small_rows, 1.0, 0.0).astype(BF)
@@ -1920,12 +1884,16 @@
             mask = jnp.where(kind == which, 1.0, 0.0).astype(BF)
             return [part * mask for part in picked]
 
-        late_ref[...] = sum(dot_tn(part, fact) for part in rows_of(1))
-        early_ref[...] = sum(dot_tn(part, fact) for part in rows_of(2))
-        label = fact[:, 0:1].astype(jnp.float32) + 32.0 * fact[:, 128:129].astype(jnp.float32)
+        late_ref[...] = sum(dot_tn(part, fact) for part in rows_of(0))
+        early_ref[...] = sum(dot_tn(part, fact) for part in rows_of(1))
+        code_s[...] = (fact[:, :128].astype(jnp.float32) + 32.0 * fact[:, 128:256].astype(jnp.float32)).reshape(
+            places.count, 16, 128
+        )
+        code_s[:, :4, :] = code_s[:, 12:, :]
+        label = code_s.reshape(total, 128)[:, 0:1]
         wide = lax.broadcasted_iota(jnp.int32, (total, 3 * D), 1).astype(jnp.float32)
         hot = jnp.where(wide == label, 1.0, 0.0).astype(BF)
-        class_ref[...] = sum(dot_tn(part, hot) for part in rows_of(3))
+        class_ref[...] = sum(dot_tn(part, hot) for part in rows_of(0))
 
     for layer in range(layers):
         mod = mod_of(layer)
@@ -2103,15 +2071,17 @@
         accs.append(pltpu.VMEM(dims[:-1] + blocks[at], BF))
         lands += [pltpu.VMEM(shape, BF) for shape in land_shapes(places, at % 2 == 1, blocks[at])]
     f32 = jnp.float32
-    scratch = [pltpu.VMEM(full, BF)] * chunks + [pltpu.VMEM((*dims, 16, D), BF)] + accs + lands
+    scratch = [pltpu.VMEM(g.shape, BF) for g in given[:-1]] + [pltpu.VMEM((*dims, 16, D), BF)] + accs + lands
     scratch += [pltpu.VMEM((*dims, 8, 128), f32)] * (layers * (depth + 1))
     scratch += [
         pltpu.VMEM((places.count, 16, 128), f32),
         pltpu.VMEM(full, BF),
         pltpu.VMEM((*dims, *patch_block), BF),
         pltpu.VMEM(block, f32),
-        pltpu.VMEM((16, D), f32),
-        pltpu.VMEM((*dims, 16, D), f32),
+        pltpu.VMEM((8, D), f32),
+        pltpu.VMEM((*dims, 8, D), f32),
+        pltpu.VMEM((places.count, 16, D), f32),
+        pltpu.VMEM((places.count, 16, 128), f32),
     ]
     scratch += [pltpu.VMEM(full, BF)] * 3
     scratch += [
@@ -2122,7 +2092,7 @@
             ((total, D), f32),
             ((rows, 3 * D), BF),
             ((*mods.shape[:2], mods.shape[2] + 128), f32),
-            ((8, SPLIT * places.count * block[0]), f32),
+            ((8, SPLIT * places.count * given[slots].shape[-2]), f32),
             ((8, 2 * D), f32),
             ((PATCH_IN, D), f32),
             ((OUT, D), f32),
@@ -2130,14 +2100,15 @@
             ((16, D), f32),
             ((8, 128), f32),
             (shared, f32),
-            ((depth, widest, 8, 128), f32),
+            ((places.count, 8, 128), f32),
         )
     ]
     dma = pltpu.SemaphoreType.DMA
     count = (jobs + 1 + layers) * copies_per_part(places)
     scratch += [dma((count,)), dma((count,)), dma((jobs + 1,)), dma((chunks + 1,))]
-    scratch += [dma((depth, widest - 1))] * 4
-    sizes = (block[0], 6 * D // places.count, block[0], block[0])
+    scratch += [dma((places.count - 1,))] * 2 + [dma((depth, widest - 1))] * 2
+    ada_rows = mods.shape[2] // places.count
+    sizes = (block[0], ada_rows, layers * ada_rows // SPLIT, given[slots].shape[-2], block[0])
     return pl.pallas_call(
         functools.partial(
             fused_backward_kernel, places, slots, layers, nb, tokens, lat_count, count_all, sizes
@@ -2260,11 +2231,11 @@
         block = block.reshape(n_tp, n_dp, dp_rows, D).swapaxes(0, 1)
         return pad_rows(block.reshape(places.count, dp_rows, D))
 
-    fused = dp_rows == wide_rows == part_rows and dp_rows % 16 == 0 and len(places.dims) >= 4 and layers == 2
+    fused = dp_rows == wide_rows and dp_rows % 16 == 0 and part_rows == ada_rows and len(places.dims) >= 4 and layers == 2
     fused = fused and n_tp >= 3 and lat_count == 4
     if fused:
         outs = fused_forward(
-            places, slots, nb, weights_in, (timesteps, labels, drop_flags), clean_t, noise_t
+            places, slots, NB_FORWARD, weights_in, (timesteps, labels, drop_flags), clean_t, noise_t
         )
         chunks = slots + SPLIT + 3 * layers
         mods, fmod, pre, cond, noisy, start, result, *kept, square = outs[chunks + 1 :]

time: 224 us -> 200 us (0.89)
  Pallas kernels: 223 us -> 199 us
    pallas_call x1, Pallas kernels: 110 us -> 95.6 us  [fused_forward(): pl.pallas_call(functools.partial(fused_forward_kernel, places, slots, lay...]
    pallas_call x1, Pallas kernels: 109 us -> 98.8 us  [fused_backward(): pl.pallas_call(functools.partial(fused_backward_kernel, places, slots, la...]
where the time goes in v4:
time: 200 us
  Pallas kernels  199 us (100%)
    pallas_call x1, Pallas kernels, fused_backward(): pl.pallas_call(functools.partial(fused_backward_kernel, places, slots, la...  98.8 us
    pallas_call x1, Pallas kernels, fused_forward(): pl.pallas_call(functools.partial(fused_forward_kernel, places, slots, lay...  95.6 us
    pallas_call x1, Pallas kernels, fused_adam(): pl.pallas_call(functools.partial(fused_adam_kernel, layers, count_rms), o...  4.75 us

profile of v4, /device:TPU:0, one launch (start us, length us, event | category | flops | bytes accessed | tf_op | source)
XLA Modules:
  0.0 200.0 jit_solution(17194025425692027951)
XLA Ops:
  0.7 95.6 %gather_and_forward.1 = (bf16[4,2,2,2,48,384]{5,4,3,2,1,0:T(8,128)(2,1)}, bf16[4,2,2,2,48,384]{5,4,3,2,1,0:T(8,128)(2,1)}, bf16[4,2,2,2,80,384]{5,4,3,2,1,0:T(8,...) custom-call(f32[48,656]{1,0:T(8,128)} %bitcast.51, ...), custom_call_target="tpu_custom_call" | custom-call | tf_op jit(solution)/shard_map/gather_and_forward/pallas_call | solution.py:1451
  96.3 98.8 %backward_and_reduce.1 = (f32[48,384]{1,0:T(8,128)}, f32[48,384]{1,0:T(8,128)}, f32[48,384]{1,0:T(8,128)}, f32[48,384]{1,0:T(8,128)}, f32[48,384]{1,0:T(8,128)},...) custom-call(bf16[4,2,2,2,48,384]{5,4,3,2,1,0:T(8,128)(2,1)} %get-tup, ...), custom_call_target="tpu_custom_call" | custom-call | tf_op jit(solution)/shard_map/backward_and_reduce/pallas_call | solution.py:2112
  195.1 4.8 %adam_update.1 = (f32[48,656]{1,0:T(8,128)}, f32[48,656]{1,0:T(8,128)}, f32[48,656]{1,0:T(8,128)}, f32[48,1001]{1,0:T(8,128)}, f32[48,1001]{1,0:T(8,128)}, /*ind...) custom-call(f32[8,128]{1,0:T(8,128)} %get-tuple-element.115.refs_0_,, ...), custom_call_target="tpu_custom_call" | custom-call | tf_op jit(solution)/shard_map/adam_update/pallas_call | solution.py:1066

commit v5 on v4

--- a/solution.py
+++ b/solution.py
@@ -1188,8 +1188,8 @@
     return jnp.asarray(freq[None], jnp.float32), jnp.asarray(table, jnp.float32)
 
 
-PROLOGUE = [(0, 1), (0, 2), (1, 1), (0, 3), (2, 0), (1, 2), (0, 4), 'cond', (2, 1), (1, 3), (3, 0), (1, 4), 'mods', (2, 2)]
-LATER = {1: [(3, 1), (4, 0)], 3: [(2, 3)], 4: [(2, 4), (3, 2)], 6: [(4, 1), (5, 0)], 7: [(3, 3)], 8: [(3, 4), 'mods', (5, 1)], 9: [(4, 2)], 10: [(5, 2)], 11: [(4, 3)], 12: [(4, 4), (5, 3)], 14: [(5, 4), 'hand']}
+PROLOGUE = [(0, 1), (0, 2), (1, 1), (0, 3), (2, 0), (1, 2), (0, 4), 'cond', (3, 0), (2, 1), (1, 3), (1, 4), 'mods', (2, 2), (3, 1)]
+LATER = {1: [(4, 0)], 3: [(2, 3)], 4: [(2, 4), (3, 2)], 6: [(4, 1), (5, 0)], 7: [(3, 3)], 8: [(3, 4), 'mods', (5, 1)], 9: [(4, 2)], 10: [(5, 2)], 11: [(4, 3)], 12: [(4, 4), (5, 3)], 14: [(5, 4), 'hand']}
 
 
 def fused_forward_kernel(places, slots, layers, nb, tokens, lat_count, sizes, *refs):
@@ -1490,7 +1490,7 @@
 
 LATER_BACK = {5: [(0, 1)], 8: [(0, 2)], 9: [(1, 1)], 10: [(0, 3), (7, 1)], 11: [(1, 2)], 12: [(7, 2)], 13: [(1, 3), (2, 1), (0, 4)], 14: [(7, 3)], 15: [(2, 2)]}
 SHARES = {}
-TAIL_ONE = [(3, 1), (2, 3), (6, 1), (4, 1)]
+TAIL_ONE = [(2, 3), (3, 1), (6, 1), (4, 1)]
 TAIL_TWO = [(5, 1), (7, 4), (1, 4), 0, (3, 2), (6, 2), (4, 2), 1, (3, 3), (6, 3), (5, 2), (4, 3), (2, 4), 2, (5, 3), (6, 4), 'ada', (5, 4), 'small', (4, 4), (3, 4)]
 
 

time: 200 us -> 200 us (level)
  no operation moved by 1% of the time
where the time goes in v5:
time: 200 us
  Pallas kernels  199 us (100%)
    pallas_call x1, Pallas kernels, fused_backward(): pl.pallas_call(functools.partial(fused_backward_kernel, places, slots, la...  98.8 us
    pallas_call x1, Pallas kernels, fused_forward(): pl.pallas_call(functools.partial(fused_forward_kernel, places, slots, lay...  95.1 us
    pallas_call x1, Pallas kernels, fused_adam(): pl.pallas_call(functools.partial(fused_adam_kernel, layers, count_rms), o...  4.75 us

profile of v5, /device:TPU:0, one launch (start us, length us, event | category | flops | bytes accessed | tf_op | source)
XLA Modules:
  0.0 199.5 jit_solution(13313934988110746555)
XLA Ops:
  0.7 95.1 %gather_and_forward.1 = (bf16[4,2,2,2,48,384]{5,4,3,2,1,0:T(8,128)(2,1)}, bf16[4,2,2,2,48,384]{5,4,3,2,1,0:T(8,128)(2,1)}, bf16[4,2,2,2,80,384]{5,4,3,2,1,0:T(8,...) custom-call(f32[48,656]{1,0:T(8,128)} %bitcast.51, ...), custom_call_target="tpu_custom_call" | custom-call | tf_op jit(solution)/shard_map/gather_and_forward/pallas_call | solution.py:1451
  95.8 98.8 %backward_and_reduce.1 = (f32[48,384]{1,0:T(8,128)}, f32[48,384]{1,0:T(8,128)}, f32[48,384]{1,0:T(8,128)}, f32[48,384]{1,0:T(8,128)}, f32[48,384]{1,0:T(8,128)},...) custom-call(bf16[4,2,2,2,48,384]{5,4,3,2,1,0:T(8,128)(2,1)} %get-tup, ...), custom_call_target="tpu_custom_call" | custom-call | tf_op jit(solution)/shard_map/backward_and_reduce/pallas_call | solution.py:2112
  194.6 4.8 %adam_update.1 = (f32[48,656]{1,0:T(8,128)}, f32[48,656]{1,0:T(8,128)}, f32[48,656]{1,0:T(8,128)}, f32[48,1001]{1,0:T(8,128)}, f32[48,1001]{1,0:T(8,128)}, /*ind...) custom-call(f32[8,128]{1,0:T(8,128)} %get-tuple-element.115.refs_0_,, ...), custom_call_target="tpu_custom_call" | custom-call | tf_op jit(solution)/shard_map/adam_update/pallas_call | solution.py:1066
